TPU v7x, 512 devices: a whole 4x8x8 slice. The times are simulated.
512 devices in a mesh: dp: 16 (over z_lo, x), ctx: 32 (over y, z_hi, core).
Axes of the slice: x: 4, y: 8, z: 8 (z_hi: 2, z_lo: 4; z = z_hi * 4 + z_lo), core: 2. Of those that a mesh axis runs over, the one named last changes fastest.
Arguments:
- queries: bfloat16 [8192, 8192], P('ctx', 'dp'), may hold values from -150 to 150
- key_rows: bfloat16 [8192, 8192], P('ctx', 'dp'), may hold values from -10 to 10
- value_rows: bfloat16 [8192, 8192], P('ctx', 'dp'), may hold values from -6 to 6
- lengths: int32 [64], replicated, may hold values from 1 to 2048, 8192 in all
- w_first: bfloat16 [8192, 2048], P('dp'), may hold values from -0.25 to 0.25
- w_noise: bfloat16 [128, 2048], replicated, may hold values from -0.5 to 0.5
- w_out: bfloat16 [2048, 128], replicated, may hold values from -0.125 to 0.125
- noise_draws: bfloat16 [8192, 8, 128], P('ctx'), may hold values from -6 to 6
- target: bfloat16 [8192, 128], P('ctx'), may hold values from -6 to 6
- loss_weights: float32 [8192], P('ctx'), may hold values from 0.25 to 4
Outputs:
- attended: bfloat16 [8192, 8192], P('ctx', 'dp')
- losses: float32 [32, 256], P('ctx', 'dp')
- first_grad: bfloat16 [2048, 8192], P('ctx', 'dp')
Inputs may be any that keep to these rules, and one draw needn't show every extreme that they name: `lengths`: lengths fill the 8192 positions in order; the longest document is exactly 2048 positions.
All inputs are finite; a program needn't handle non-finite values.
Results may differ from a plain program's by a relative error of at most 0.02.
Values may be sent and summed in bfloat16 or wider, within the bound.
No kernel may reach another device: no remote copies, remote signals or barrier semaphores. Data moves between devices by JAX's collectives and lax.ppermute only.
A program may use at most 64 MiB of HBM per device.

v0:
```python
import math

import jax
import jax.numpy as jnp
from jax import lax
from jax.sharding import PartitionSpec as P

HD = 128


EPS = 1e-05


def from_behind(array, axis, by):
    length = lax.axis_size(axis)
    pairs = [(i, i + by) for i in range(length) if 0 <= i + by < length]
    return lax.ppermute(array, axis, pairs)


def doc_index(lengths, positions):
    ends = jnp.cumsum(lengths)
    return jnp.sum((ends[None, :] <= positions[:, None]).astype(jnp.int32), axis=1)


def attend(queries, key_rows, value_rows, query_pos, key_pos, lengths, heads):
    count = queries.shape[0]
    width = queries.shape[1] // heads
    q_heads = queries.reshape(count, heads, width)
    k_heads = key_rows.reshape(-1, heads, width)
    v_heads = value_rows.reshape(-1, heads, width)
    scores = jnp.einsum("qhd,khd->hqk", q_heads, k_heads, preferred_element_type=jnp.float32) * (
        1.0 / math.sqrt(width)
    )
    allowed = doc_index(lengths, query_pos)[:, None] == doc_index(lengths, key_pos)[None, :]
    allowed = allowed & (key_pos[None, :] <= query_pos[:, None]) & (key_pos[None, :] >= 0)
    scores = jnp.where(allowed[None], scores, -1e30)
    top = jnp.max(scores, axis=2, keepdims=True)
    raised = jnp.exp(scores - top)
    probs = (raised / jnp.sum(raised, axis=2, keepdims=True)).astype(jnp.bfloat16)
    output = jnp.einsum("hqk,khd->qhd", probs, v_heads, preferred_element_type=jnp.float32)
    return output.reshape(count, heads * width).astype(jnp.bfloat16)


def head_rows(hidden_sum, noise_draws, w_noise, w_out, target, loss_weights):
    count, samples, depth = noise_draws.shape
    lift = jnp.dot(
        noise_draws.reshape(count * samples, depth), w_noise, preferred_element_type=jnp.float32
    )
    pre = hidden_sum[:, None, :] + lift.reshape(count, samples, -1)
    act = jax.nn.silu(pre).astype(jnp.bfloat16)
    latent = jnp.dot(act.reshape(count * samples, -1), w_out, preferred_element_type=jnp.float32)
    latent = latent.reshape(count, samples, -1)
    width = latent.shape[2]
    apart = latent[:, :, None, :] - latent[:, None, :, :]
    pair = jnp.sqrt(jnp.mean(apart * apart, axis=3) + EPS)
    others = 1.0 - jnp.eye(samples, dtype=jnp.float32)
    miss = latent - target.astype(jnp.float32)[:, None, :]
    far = jnp.sqrt(jnp.mean(miss * miss, axis=2) + EPS)
    spread = samples * (samples - 1.0)
    losses = 2.0 / samples * jnp.sum(far, axis=1) - jnp.sum(pair * others, axis=(1, 2)) / spread
    toward = 2.0 / samples * miss / (width * far[:, :, None])
    repel = 2.0 / spread * jnp.sum((others[None] / (width * pair))[:, :, :, None] * apart, axis=2)
    latent_grad = (loss_weights[:, None, None] * (toward - repel)).astype(jnp.bfloat16)
    act_grad = jnp.dot(
        latent_grad.reshape(count * samples, width), w_out.T, preferred_element_type=jnp.float32
    )
    act_grad = act_grad.reshape(count, samples, -1)
    sigma = jax.nn.sigmoid(pre)
    pre_grad = act_grad * sigma * (1.0 + pre * (1.0 - sigma))
    return (losses, jnp.sum(pre_grad, axis=1).astype(jnp.bfloat16))


def shards(
    queries,
    key_rows,
    value_rows,
    lengths,
    w_first,
    w_noise,
    w_out,
    noise_draws,
    target,
    loss_weights,
):
    rows = queries.shape[0]
    feat = queries.shape[1]
    heads = feat // HD
    block_index = lax.axis_index("ctx")
    reach = min(8, lax.axis_size("ctx") // 2)
    stacked = jnp.stack((key_rows, value_rows))
    arrived = []
    moving = stacked
    for step in range(reach):
        moving = from_behind(moving, "ctx", 1)
        arrived.append(moving)
    pieces = arrived[::-1]
    pieces.append(stacked)
    window = jnp.concatenate(pieces, axis=1)
    query_pos = block_index * rows + jnp.arange(rows, dtype=jnp.int32)
    key_pos = (block_index - reach) * rows + jnp.arange((reach + 1) * rows, dtype=jnp.int32)
    attended = attend(queries, window[0], window[1], query_pos, key_pos, lengths, heads)
    groups = lax.axis_size("dp")
    share = rows // groups
    dp_index = lax.axis_index("dp")
    contract = (((0,), (0,)), ((), ()))
    hidden_sum = lax.psum_scatter(
        jnp.dot(attended, w_first, preferred_element_type=jnp.float32),
        "dp",
        scatter_dimension=0,
        tiled=True,
    )
    here = dp_index * share
    losses_here, grad_here = head_rows(
        hidden_sum,
        lax.dynamic_slice_in_dim(noise_draws, here, share, 0),
        w_noise,
        w_out,
        lax.dynamic_slice_in_dim(target, here, share, 0),
        lax.dynamic_slice_in_dim(loss_weights, here, share, 0),
    )
    carried = lax.dot_general(
        lax.all_gather(grad_here, "dp", axis=0, tiled=True),
        attended,
        contract,
        preferred_element_type=jnp.float32,
    )
    first_grad = lax.psum_scatter(
        carried.astype(jnp.bfloat16), "ctx", scatter_dimension=0, tiled=True
    )
    return (attended, losses_here[None, :], first_grad)


def solution(mesh):
    placed = (
        P("ctx", "dp"),
        P("ctx", "dp"),
        P("ctx", "dp"),
        P(),
        P("dp", None),
        P(),
        P(),
        P("ctx", None, None),
        P("ctx", None),
        P("ctx"),
    )
    return jax.shard_map(
        shards,
        mesh=mesh,
        in_specs=placed,
        out_specs=(P("ctx", "dp"), P("ctx", "dp"), P("ctx", "dp")),
        check_vma=False,
    )
```

profile of v0, /device:TPU:1, one launch (start us, length us, event | category | flops | bytes accessed | tf_op | source)
XLA Modules:
  0.0 518.3 jit_solution(3749293411955317386)
XLA Ops:
  9.6 12.0 %collective-permute-start = (bf16[2,256,512]{1,2,0:T(8,128)(2,1)S(1)}, bf16[2,256,512]{1,2,0:T(8,128)(2,1)S(1)}, u32[]{:S(2)}, u32[]{:S(2)}) collective-permute-start(bf16[2,256,512]{1,2,0:T(8,128)(2,1)S(1)} %pad_maximum_fusion), channel_id=1, source_target_pairs={{0,1},{1,2},{2,3},{3,4},{4,5},{5,6},{6,7},{7,8},{8,9},{9,10},{10,1... | collective-permute-start | bytes 1572872 | tf_op jit(solution)/shard_map/ppermute | solution.py:17
  21.6 6.1 %collective-permute-done = bf16[2,256,512]{1,2,0:T(8,128)(2,1)S(1)} collective-permute-done((bf16[2,256,512]{1,2,0:T(8,128)(2,1)S(1)}, bf16[2,256,512]{1,2,0:T(8,128)(2,1)S(1)}, u32[]{:S(2)}, u32[]{:S(2)}) %collective-permute-start) | collective-permute-done | bytes 524320 | tf_op jit(solution)/shard_map/ppermute | solution.py:17
  28.5 8.4 %collective-permute-start.1 = (bf16[2,256,512]{1,2,0:T(8,128)(2,1)S(1)}, bf16[2,256,512]{1,2,0:T(8,128)(2,1)S(1)}, u32[]{:S(2)}, u32[]{:S(2)}) collective-permute-start(bf16[2,256,512]{1,2,0:T(8,128)(2,1)S(1)} %collective-permute-done), channel_id=1, source_target_pairs={{0,1},{1,2},{2,3},{3,4},{4,5},{5,6},{6,7},{7,8},{8,9},{9,10},{10,1... | collective-permute-start | bytes 1572872 | tf_op jit(solution)/shard_map/ppermute | solution.py:17
  36.9 6.1 %collective-permute-done.1 = bf16[2,256,512]{1,2,0:T(8,128)(2,1)S(1)} collective-permute-done((bf16[2,256,512]{1,2,0:T(8,128)(2,1)S(1)}, bf16[2,256,512]{1,2,0:T(8,128)(2,1)S(1)}, u32[]{:S(2)}, u32[]{:S(2)}) %collective-permute-start.1) | collective-permute-done | bytes 524320 | tf_op jit(solution)/shard_map/ppermute | solution.py:17
  43.8 8.3 %collective-permute-start.2 = (bf16[2,256,512]{1,2,0:T(8,128)(2,1)S(1)}, bf16[2,256,512]{1,2,0:T(8,128)(2,1)S(1)}, u32[]{:S(2)}, u32[]{:S(2)}) collective-permute-start(bf16[2,256,512]{1,2,0:T(8,128)(2,1)S(1)} %collective-permute-done.1), channel_id=1, source_target_pairs={{0,1},{1,2},{2,3},{3,4},{4,5},{5,6},{6,7},{7,8},{8,9},{9,10},{10,1... | collective-permute-start | bytes 1572872 | tf_op jit(solution)/shard_map/ppermute | solution.py:17
  52.1 6.1 %collective-permute-done.2 = bf16[2,256,512]{1,2,0:T(8,128)(2,1)S(1)} collective-permute-done((bf16[2,256,512]{1,2,0:T(8,128)(2,1)S(1)}, bf16[2,256,512]{1,2,0:T(8,128)(2,1)S(1)}, u32[]{:S(2)}, u32[]{:S(2)}) %collective-permute-start.2) | collective-permute-done | bytes 524320 | tf_op jit(solution)/shard_map/ppermute | solution.py:17
  59.1 8.3 %collective-permute-start.3 = (bf16[2,256,512]{1,2,0:T(8,128)(2,1)S(1)}, bf16[2,256,512]{1,2,0:T(8,128)(2,1)S(1)}, u32[]{:S(2)}, u32[]{:S(2)}) collective-permute-start(bf16[2,256,512]{1,2,0:T(8,128)(2,1)S(1)} %collective-permute-done.2), channel_id=1, source_target_pairs={{0,1},{1,2},{2,3},{3,4},{4,5},{5,6},{6,7},{7,8},{8,9},{9,10},{10,1... | collective-permute-start | bytes 1572872 | tf_op jit(solution)/shard_map/ppermute | solution.py:17
  67.3 6.1 %collective-permute-done.3 = bf16[2,256,512]{1,2,0:T(8,128)(2,1)S(1)} collective-permute-done((bf16[2,256,512]{1,2,0:T(8,128)(2,1)S(1)}, bf16[2,256,512]{1,2,0:T(8,128)(2,1)S(1)}, u32[]{:S(2)}, u32[]{:S(2)}) %collective-permute-start.3) | collective-permute-done | bytes 524320 | tf_op jit(solution)/shard_map/ppermute | solution.py:17
  74.3 8.3 %collective-permute-start.4 = (bf16[2,256,512]{1,2,0:T(8,128)(2,1)S(1)}, bf16[2,256,512]{1,2,0:T(8,128)(2,1)S(1)}, u32[]{:S(2)}, u32[]{:S(2)}) collective-permute-start(bf16[2,256,512]{1,2,0:T(8,128)(2,1)S(1)} %collective-permute-done.3), channel_id=1, source_target_pairs={{0,1},{1,2},{2,3},{3,4},{4,5},{5,6},{6,7},{7,8},{8,9},{9,10},{10,1... | collective-permute-start | bytes 1572872 | tf_op jit(solution)/shard_map/ppermute | solution.py:17
  82.6 6.1 %collective-permute-done.4 = bf16[2,256,512]{1,2,0:T(8,128)(2,1)S(1)} collective-permute-done((bf16[2,256,512]{1,2,0:T(8,128)(2,1)S(1)}, bf16[2,256,512]{1,2,0:T(8,128)(2,1)S(1)}, u32[]{:S(2)}, u32[]{:S(2)}) %collective-permute-start.4) | collective-permute-done | bytes 524320 | tf_op jit(solution)/shard_map/ppermute | solution.py:17
  88.7 8.3 %collective-permute-start.5 = (bf16[2,256,512]{1,2,0:T(8,128)(2,1)S(1)}, bf16[2,256,512]{1,2,0:T(8,128)(2,1)}, u32[]{:S(2)}, u32[]{:S(2)}) collective-permute-start(bf16[2,256,512]{1,2,0:T(8,128)(2,1)S(1)} %collective-permute-done.4), channel_id=1, source_target_pairs={{0,1},{1,2},{2,3},{3,4},{4,5},{5,6},{6,7},{7,8},{8,9},{9,10},{10,1... | collective-permute-start | bytes 1572872 | tf_op jit(solution)/shard_map/ppermute | solution.py:17
  98.0 5.1 collective-permute-done.5
  103.1 8.4 %collective-permute-start.6 = (bf16[2,256,512]{1,2,0:T(8,128)(2,1)}, bf16[2,256,512]{1,2,0:T(8,128)(2,1)S(1)}, u32[]{:S(2)}, u32[]{:S(2)}) collective-permute-start(bf16[2,256,512]{1,2,0:T(8,128)(2,1)} %collective-permute-done.5), channel_id=1, source_target_pairs={{0,1},{1,2},{2,3},{3,4},{4,5},{5,6},{6,7},{7,8},{8,9},{9,10},{10,1... | collective-permute-start | bytes 1572872 | tf_op jit(solution)/shard_map/ppermute | solution.py:17
  111.7 6.1 %collective-permute-done.6 = bf16[2,256,512]{1,2,0:T(8,128)(2,1)S(1)} collective-permute-done((bf16[2,256,512]{1,2,0:T(8,128)(2,1)}, bf16[2,256,512]{1,2,0:T(8,128)(2,1)S(1)}, u32[]{:S(2)}, u32[]{:S(2)}) %collective-permute-start.6) | collective-permute-done | bytes 524320 | tf_op jit(solution)/shard_map/ppermute | solution.py:17
  117.9 8.5 %collective-permute-start.7 = (bf16[2,256,512]{1,2,0:T(8,128)(2,1)S(1)}, bf16[2,256,512]{1,2,0:T(8,128)(2,1)S(1)}, u32[]{:S(2)}, u32[]{:S(2)}) collective-permute-start(bf16[2,256,512]{1,2,0:T(8,128)(2,1)S(1)} %collective-permute-done.6), channel_id=1, source_target_pairs={{0,1},{1,2},{2,3},{3,4},{4,5},{5,6},{6,7},{7,8},{8,9},{9,10},{10,1... | collective-permute-start | bytes 1572872 | tf_op jit(solution)/shard_map/ppermute | solution.py:17
  126.4 2.2 and_and_fusion
  128.6 3.9 collective-permute-done.7
  135.0 2.4 fusion.52
  137.5 5.2 fusion.53
  142.6 7.3 %fusion.10 = bf16[4,128,256]{2,1,0:T(8,128)(2,1)S(1)} fusion(bf16[2304,4,128]{0,2,1:T(8,128)(2,1)} %bitcast.88, f32[4,256]{1,0:T(4,128)S(1)} %fusion.53, pred[256,2304]{0,1:T(8,128)(4,1)S(1)} %and_and_fusion, bf16[2304,4,128]{0,2,1:T(8,128)(2,1)} %bitcast.87, bf16[256,512]{1,0:T(8,128)(2,1)S(1)} %copy-done.12), kind=kOutput, calls=%fused_computation.16 | convolution fusion | flops 1219890432 | bytes 5836800 | tf_op jit(solution)/shard_map/hqk,khd->qhd/dot_general | solution.py:40
  153.2 129.6 %reduce-scatter.3.cloned.1.call-done = f32[16,2048]{1,0:T(8,128)} async-done(((f32[256,2048]{1,0:T(8,128)}), f32[16,2048]{1,0:T(8,128)}) %reduce-scatter.3.cloned.1.call-update) | async-done | bytes 131088 | tf_op jit(solution)/shard_map/reduce_scatter | solution.py:106
  286.7 80.3 %all-gather.2.cloned.1.call-done = bf16[256,2048]{1,0:T(8,128)(2,1)} async-done(((bf16[16,2048]{1,0:T(8,128)(2,1)}), bf16[256,2048]{1,0:T(8,128)(2,1)}) %all-gather.2.cloned.1.call-update) | async-done | bytes 1048592 | tf_op jit(solution)/shard_map/all_gather | solution.py:122
  367.0 3.3 convolution_convert_fusion
  371.9 139.8 %reduce-scatter.5.cloned.1.call-done = bf16[64,512]{1,0:T(8,128)(2,1)} async-done(((bf16[2048,512]{1,0:T(8,128)(2,1)}), bf16[64,512]{1,0:T(8,128)(2,1)}) %reduce-scatter.5.cloned.1.call-update) | async-done | bytes 65552 | tf_op jit(solution)/shard_map/reduce_scatter | solution.py:127
  (71 shorter events, 18.0 us)
Async XLA Ops:
  7.2 142.8 %copy-start = (bf16[512,2048]{1,0:T(8,128)(2,1)S(1)}, bf16[512,2048]{1,0:T(8,128)(2,1)}, u32[]{:S(2)}) copy-start(bf16[512,2048]{1,0:T(8,128)(2,1)} %param.14) | copy-start | bytes 6291460
  7.2 275.7 %reduce-scatter.3.cloned.1.call-start = ((), (), s32[]{:S(2)}) async-start(), calls=%async_computation.2 | async-start | bytes 2228224 | tf_op jit(solution)/shard_map/reduce_scatter | solution.py:106
  9.6 18.1 %collective-permute-start = (bf16[2,256,512]{1,2,0:T(8,128)(2,1)S(1)}, bf16[2,256,512]{1,2,0:T(8,128)(2,1)S(1)}, u32[]{:S(2)}, u32[]{:S(2)}) collective-permute-start(bf16[2,256,512]{1,2,0:T(8,128)(2,1)S(1)} %pad_maximum_fusion), channel_id=1, source_target_pairs={{0,1},{1,2},{2,3},{3,4},{4,5},{5,6},{6,7},{7,8},{8,9},{9,10},{10,1... | collective-permute-start | bytes 1572872 | tf_op jit(solution)/shard_map/ppermute | solution.py:17
  28.5 14.5 %collective-permute-start.1 = (bf16[2,256,512]{1,2,0:T(8,128)(2,1)S(1)}, bf16[2,256,512]{1,2,0:T(8,128)(2,1)S(1)}, u32[]{:S(2)}, u32[]{:S(2)}) collective-permute-start(bf16[2,256,512]{1,2,0:T(8,128)(2,1)S(1)} %collective-permute-done), channel_id=1, source_target_pairs={{0,1},{1,2},{2,3},{3,4},{4,5},{5,6},{6,7},{7,8},{8,9},{9,10},{10,1... | collective-permute-start | bytes 1572872 | tf_op jit(solution)/shard_map/ppermute | solution.py:17
  43.0 0.8 copy-start.4
  43.8 14.4 %collective-permute-start.2 = (bf16[2,256,512]{1,2,0:T(8,128)(2,1)S(1)}, bf16[2,256,512]{1,2,0:T(8,128)(2,1)S(1)}, u32[]{:S(2)}, u32[]{:S(2)}) collective-permute-start(bf16[2,256,512]{1,2,0:T(8,128)(2,1)S(1)} %collective-permute-done.1), channel_id=1, source_target_pairs={{0,1},{1,2},{2,3},{3,4},{4,5},{5,6},{6,7},{7,8},{8,9},{9,10},{10,1... | collective-permute-start | bytes 1572872 | tf_op jit(solution)/shard_map/ppermute | solution.py:17
  58.2 0.8 copy-start.6
  59.1 14.4 %collective-permute-start.3 = (bf16[2,256,512]{1,2,0:T(8,128)(2,1)S(1)}, bf16[2,256,512]{1,2,0:T(8,128)(2,1)S(1)}, u32[]{:S(2)}, u32[]{:S(2)}) collective-permute-start(bf16[2,256,512]{1,2,0:T(8,128)(2,1)S(1)} %collective-permute-done.2), channel_id=1, source_target_pairs={{0,1},{1,2},{2,3},{3,4},{4,5},{5,6},{6,7},{7,8},{8,9},{9,10},{10,1... | collective-permute-start | bytes 1572872 | tf_op jit(solution)/shard_map/ppermute | solution.py:17
  73.5 0.8 copy-start.8
  74.3 14.4 %collective-permute-start.4 = (bf16[2,256,512]{1,2,0:T(8,128)(2,1)S(1)}, bf16[2,256,512]{1,2,0:T(8,128)(2,1)S(1)}, u32[]{:S(2)}, u32[]{:S(2)}) collective-permute-start(bf16[2,256,512]{1,2,0:T(8,128)(2,1)S(1)} %collective-permute-done.3), channel_id=1, source_target_pairs={{0,1},{1,2},{2,3},{3,4},{4,5},{5,6},{6,7},{7,8},{8,9},{9,10},{10,1... | collective-permute-start | bytes 1572872 | tf_op jit(solution)/shard_map/ppermute | solution.py:17
  88.7 29.2 %copy-start.10 = (bf16[2,256,512]{1,2,0:T(8,128)(2,1)}, bf16[2,256,512]{1,2,0:T(8,128)(2,1)S(1)}, u32[]{:S(2)}) copy-start(bf16[2,256,512]{1,2,0:T(8,128)(2,1)S(1)} %collective-permute-done.4) | copy-start | bytes 1572868
  88.7 14.4 %collective-permute-start.5 = (bf16[2,256,512]{1,2,0:T(8,128)(2,1)S(1)}, bf16[2,256,512]{1,2,0:T(8,128)(2,1)}, u32[]{:S(2)}, u32[]{:S(2)}) collective-permute-start(bf16[2,256,512]{1,2,0:T(8,128)(2,1)S(1)} %collective-permute-done.4), channel_id=1, source_target_pairs={{0,1},{1,2},{2,3},{3,4},{4,5},{5,6},{6,7},{7,8},{8,9},{9,10},{10,1... | collective-permute-start | bytes 1572872 | tf_op jit(solution)/shard_map/ppermute | solution.py:17
  97.9 36.8 %copy-start.9 = (bf16[2,256,512]{1,2,0:T(8,128)(2,1)S(1)}, bf16[2,256,512]{1,2,0:T(8,128)(2,1)}, u32[]{:S(2)}) copy-start(bf16[2,256,512]{1,2,0:T(8,128)(2,1)} %copy-done.8) | copy-start | bytes 1572868
  97.9 36.9 %copy-start.7 = (bf16[2,256,512]{1,2,0:T(8,128)(2,1)S(1)}, bf16[2,256,512]{1,2,0:T(8,128)(2,1)}, u32[]{:S(2)}) copy-start(bf16[2,256,512]{1,2,0:T(8,128)(2,1)} %copy-done.6) | copy-start | bytes 1572868
  97.9 36.9 %copy-start.5 = (bf16[2,256,512]{1,2,0:T(8,128)(2,1)S(1)}, bf16[2,256,512]{1,2,0:T(8,128)(2,1)}, u32[]{:S(2)}) copy-start(bf16[2,256,512]{1,2,0:T(8,128)(2,1)} %copy-done.4) | copy-start | bytes 1572868
  97.9 37.0 %copy-start.3 = (bf16[2,256,512]{1,2,0:T(8,128)(2,1)S(1)}, bf16[2,256,512]{1,2,0:T(8,128)(2,1)}, u32[]{:S(2)}) copy-start(bf16[2,256,512]{1,2,0:T(8,128)(2,1)} %copy-done.2) | copy-start | bytes 1572868
  103.1 14.8 %collective-permute-start.6 = (bf16[2,256,512]{1,2,0:T(8,128)(2,1)}, bf16[2,256,512]{1,2,0:T(8,128)(2,1)S(1)}, u32[]{:S(2)}, u32[]{:S(2)}) collective-permute-start(bf16[2,256,512]{1,2,0:T(8,128)(2,1)} %collective-permute-done.5), channel_id=1, source_target_pairs={{0,1},{1,2},{2,3},{3,4},{4,5},{5,6},{6,7},{7,8},{8,9},{9,10},{10,1... | collective-permute-start | bytes 1572872 | tf_op jit(solution)/shard_map/ppermute | solution.py:17
  117.9 14.6 %collective-permute-start.7 = (bf16[2,256,512]{1,2,0:T(8,128)(2,1)S(1)}, bf16[2,256,512]{1,2,0:T(8,128)(2,1)S(1)}, u32[]{:S(2)}, u32[]{:S(2)}) collective-permute-start(bf16[2,256,512]{1,2,0:T(8,128)(2,1)S(1)} %collective-permute-done.6), channel_id=1, source_target_pairs={{0,1},{1,2},{2,3},{3,4},{4,5},{5,6},{6,7},{7,8},{8,9},{9,10},{10,1... | collective-permute-start | bytes 1572872 | tf_op jit(solution)/shard_map/ppermute | solution.py:17
  135.0 2.4 copy-start.12
  149.9 2.4 copy-start.13
  149.9 133.0 %copy-start.1 = (bf16[128,2048]{1,0:T(8,128)(2,1)S(1)}, bf16[128,2048]{1,0:T(8,128)(2,1)}, u32[]{:S(2)}) copy-start(bf16[128,2048]{1,0:T(8,128)(2,1)} %param.15) | copy-start | bytes 1572868
  149.9 134.2 %copy-start.11 = (bf16[2048,128]{1,0:T(8,128)(2,1)S(1)}, bf16[2048,128]{1,0:T(8,128)(2,1)}, u32[]{:S(2)}) copy-start(bf16[2048,128]{1,0:T(8,128)(2,1)} %param.16) | copy-start | bytes 1572868
  152.0 215.0 %all-gather.2.cloned.1.call-start = ((), (), s32[]{:S(2)}) async-start(), calls=%async_computation.3 | async-start | bytes 1114112 | tf_op jit(solution)/shard_map/all_gather | solution.py:122
  286.7 225.1 %reduce-scatter.5.cloned.1.call-start = ((), (), s32[]{:S(2)}) async-start(), calls=%async_computation.4 | async-start | bytes 2162688 | tf_op jit(solution)/shard_map/reduce_scatter | solution.py:127
  (1 other events, 0.8 us)
Sparse Core Ops, SparseCore 0:
  152.2 130.6 reduce-scatter.2
  286.8 80.1 all-gather.1
  372.3 139.4 reduce-scatter.4
where the time goes:
time: 523 us; the launch traced here: 518 us
  waiting for transfers between devices  395 us (76%)
  starting transfers between devices  70.8 us (14%)
  matrix products  21 us (4%)
  between operations  14.1 us (3%)
  local copies, waits for them, and re-layouts  12.3 us (2%)
    reduce_scatter x1, waiting for transfers between devices, shards(): lax.psum_scatter(carried.astype(jnp.bfloat16), 'ctx', scatter_dimension=0...  140 us
    reduce_scatter x1, waiting for transfers between devices, shards(): lax.psum_scatter(jnp.dot(attended, w_first, preferred_element_type=jnp.fl...  130 us
    all_gather x1, waiting for transfers between devices, shards(): lax.all_gather(grad_here, 'dp', axis=0, tiled=True)  80.3 us
    ppermute x8, starting transfers between devices, from_behind(): return lax.ppermute(array, axis, pairs)  70.5 us
    ppermute x8, waiting for transfers between devices, from_behind(): return lax.ppermute(array, axis, pairs)  45.7 us
  transfers between devices with their start and end apart: 11, of which 11 were waited for; matrix products, arithmetic and copies ran while one was open for 1% of the time, Pallas kernels for 0%

commit v1 on v0

--- a/solution.py
+++ b/solution.py
@@ -3,6 +3,7 @@
 import jax
 import jax.numpy as jnp
 from jax import lax
+from jax.sharding import Mesh
 from jax.sharding import PartitionSpec as P
 
 HD = 128
@@ -70,6 +71,14 @@
     return (losses, jnp.sum(pre_grad, axis=1).astype(jnp.bfloat16))
 
 
+def swap(array, axis):
+    return lax.ppermute(array, axis, [(0, 1), (1, 0)])
+
+
+def exchange(array, axis):
+    return lax.all_to_all(array, axis, 0, 0, tiled=True)
+
+
 def shards(
     queries,
     key_rows,
@@ -82,16 +91,17 @@
     target,
     loss_weights,
 ):
-    rows = queries.shape[0]
-    feat = queries.shape[1]
+    rows, feat = queries.shape
     heads = feat // HD
-    block_index = lax.axis_index("ctx")
-    reach = min(8, lax.axis_size("ctx") // 2)
+    ctx = ("y", "z_hi", "core")
+    block_index = lax.axis_index(ctx)
+    z_hi, core = lax.axis_index("z_hi"), lax.axis_index("core")
+    reach = min(8, lax.axis_size(ctx) // 2)
     stacked = jnp.stack((key_rows, value_rows))
     arrived = []
     moving = stacked
     for step in range(reach):
-        moving = from_behind(moving, "ctx", 1)
+        moving = from_behind(moving, ctx, 1)
         arrived.append(moving)
     pieces = arrived[::-1]
     pieces.append(stacked)
@@ -99,17 +109,29 @@
     query_pos = block_index * rows + jnp.arange(rows, dtype=jnp.int32)
     key_pos = (block_index - reach) * rows + jnp.arange((reach + 1) * rows, dtype=jnp.int32)
     attended = attend(queries, window[0], window[1], query_pos, key_pos, lengths, heads)
-    groups = lax.axis_size("dp")
-    share = rows // groups
-    dp_index = lax.axis_index("dp")
-    contract = (((0,), (0,)), ((), ()))
-    hidden_sum = lax.psum_scatter(
-        jnp.dot(attended, w_first, preferred_element_type=jnp.float32),
-        "dp",
-        scatter_dimension=0,
-        tiled=True,
-    )
-    here = dp_index * share
+
+    n_zl, n_x, n_y = (lax.axis_size(name) for name in ("z_lo", "x", "y"))
+    n_zh, n_c = lax.axis_size("z_hi"), lax.axis_size("core")
+    share = rows // (n_zl * n_x)
+    width = w_first.shape[1]
+
+    by_x = attended.reshape(n_zl, n_x, share, feat).transpose(1, 0, 2, 3).reshape(rows, feat)
+    partial = jnp.dot(by_x, w_first, preferred_element_type=jnp.float32).astype(jnp.bfloat16)
+    partial = exchange(partial, "x").reshape(n_x, n_zl * share, width)
+    partial = jnp.sum(partial.astype(jnp.float32), axis=0).astype(jnp.bfloat16)
+    partial = exchange(partial, "z_lo").reshape(n_zl, share, width)
+    hidden_sum = jnp.sum(partial.astype(jnp.float32), axis=0)
+
+    beside = swap(attended, "core")
+    across = swap(attended, "z_hi")
+    corner = swap(across, "core")
+    near = jnp.where(core == 0, jnp.stack((attended, beside)), jnp.stack((beside, attended)))
+    far = jnp.where(core == 0, jnp.stack((across, corner)), jnp.stack((corner, across)))
+    group = jnp.where(z_hi == 0, jnp.stack((near, far)), jnp.stack((far, near)))
+    group = group.reshape(n_zh, n_c, n_zl, n_x, share, feat).transpose(3, 0, 2, 1, 4, 5)
+    group = group.reshape(n_zh * n_c * rows, feat)
+
+    here = lax.axis_index(("z_lo", "x")) * share
     losses_here, grad_here = head_rows(
         hidden_sum,
         lax.dynamic_slice_in_dim(noise_draws, here, share, 0),
@@ -118,35 +140,40 @@
         lax.dynamic_slice_in_dim(target, here, share, 0),
         lax.dynamic_slice_in_dim(loss_weights, here, share, 0),
     )
+    part = width // (n_y * n_zh * n_c)
+    units = grad_here.reshape(share, n_y, n_zh, n_c, part).transpose(2, 3, 0, 1, 4)
+    units = jnp.broadcast_to(units[:, None], (n_zh, n_zl, n_c, share, n_y, part))
+    units = exchange(units.reshape(n_zh * n_zl * n_c * share, n_y * part), ("z_hi", "z_lo", "core"))
+    units = jnp.broadcast_to(units[None], (n_x,) + units.shape).reshape(-1, n_y * part)
+    units = exchange(units, "x")
     carried = lax.dot_general(
-        lax.all_gather(grad_here, "dp", axis=0, tiled=True),
-        attended,
-        contract,
-        preferred_element_type=jnp.float32,
+        units, group, (((0,), (0,)), ((), ())), preferred_element_type=jnp.float32
     )
-    first_grad = lax.psum_scatter(
-        carried.astype(jnp.bfloat16), "ctx", scatter_dimension=0, tiled=True
-    )
+    carried = exchange(carried.astype(jnp.bfloat16), "y").reshape(n_y, part, feat)
+    first_grad = jnp.sum(carried.astype(jnp.float32), axis=0).astype(jnp.bfloat16)
     return (attended, losses_here[None, :], first_grad)
 
 
 def solution(mesh):
+    sizes = (4, 4, 8, 2, 2)
+    fine = Mesh(mesh.devices.reshape(sizes), ("z_lo", "x", "y", "z_hi", "core"))
+    ctx, dp = ("y", "z_hi", "core"), ("z_lo", "x")
     placed = (
-        P("ctx", "dp"),
-        P("ctx", "dp"),
-        P("ctx", "dp"),
+        P(ctx, dp),
+        P(ctx, dp),
+        P(ctx, dp),
         P(),
-        P("dp", None),
+        P(dp, None),
         P(),
         P(),
-        P("ctx", None, None),
-        P("ctx", None),
-        P("ctx"),
+        P(ctx, None, None),
+        P(ctx, None),
+        P(ctx),
     )
     return jax.shard_map(
         shards,
-        mesh=mesh,
+        mesh=fine,
         in_specs=placed,
-        out_specs=(P("ctx", "dp"), P("ctx", "dp"), P("ctx", "dp")),
+        out_specs=(P(ctx, dp), P(ctx, dp), P(ctx, dp)),
         check_vma=False,
     )

time: 523 us -> 294 us (0.56)
  waiting for transfers between devices: 395 us -> 77.4 us
  starting transfers between devices: 70.8 us -> 155 us
  blocking collectives: 0 us -> 13.6 us
  between operations: 14.1 us -> 1.16 us
    reduce_scatter x2 -> x0, waiting for transfers between devices: 269 us -> none  [the longest x1 140 us: shards(): lax.psum_scatter(carried.astype(jnp.bfloat16), 'ctx', scatter_dimension=0...]
    all_gather x1 -> x0, waiting for transfers between devices: 80.3 us -> none  [shards(): lax.all_gather(grad_here, 'dp', axis=0, tiled=True)]
    all_to_all x0 -> x4, starting transfers between devices: none -> 73 us  [exchange(): return lax.all_to_all(array, axis, 0, 0, tiled=True)]
    all_to_all x0 -> x4, waiting for transfers between devices: none -> 26.8 us  [exchange(): return lax.all_to_all(array, axis, 0, 0, tiled=True)]
    all_to_all x0 -> x1, blocking collectives: none -> 13.6 us  [exchange(): return lax.all_to_all(array, axis, 0, 0, tiled=True)]
    ppermute x0 -> x3, starting transfers between devices: none -> 11.7 us  [swap(): return lax.ppermute(array, axis, [(0, 1), (1, 0)])]
  transfers between devices with their start and end apart: 11 -> 15, of which waited for: 11 -> 13; matrix products, arithmetic and copies ran while one was open for 1% -> 4% of each run, Pallas kernels for 0% -> 0%
where the time goes in v1:
time: 294 us; the launch traced here: 293 us
  starting transfers between devices  155 us (53%)
  waiting for transfers between devices  77.4 us (26%)
  matrix products  19.6 us (7%)
  local copies, waits for them, and re-layouts  16.9 us (6%)
  blocking collectives  13.6 us (5%)
  other arithmetic  9.13 us (3%)
    all_to_all x4, starting transfers between devices, exchange(): return lax.all_to_all(array, axis, 0, 0, tiled=True)  73 us
    ppermute x8, starting transfers between devices, from_behind(): return lax.ppermute(array, axis, pairs)  70.5 us
    ppermute x8, waiting for transfers between devices, from_behind(): return lax.ppermute(array, axis, pairs)  45.7 us
    all_to_all x4, waiting for transfers between devices, exchange(): return lax.all_to_all(array, axis, 0, 0, tiled=True)  26.8 us
    all_to_all x1, blocking collectives, exchange(): return lax.all_to_all(array, axis, 0, 0, tiled=True)  13.6 us
    ppermute x3, starting transfers between devices, swap(): return lax.ppermute(array, axis, [(0, 1), (1, 0)])  11.7 us
    unnamed x41, local copies, waits for them, and re-layouts  8.81 us
    dot_general x1, matrix products, attend(): jnp.einsum('hqk,khd->qhd', probs, v_heads, preferred_element_type=jnp.flo...  7.26 us
  transfers between devices with their start and end apart: 15, of which 13 were waited for; matrix products, arithmetic and copies ran while one was open for 4% of the time, Pallas kernels for 0%

profile of v1, /device:TPU:1, one launch (start us, length us, event | category | flops | bytes accessed | tf_op | source)
XLA Modules:
  0.0 292.9 jit_solution(2070784497166849651)
XLA Ops:
  3.0 12.0 %collective-permute-start = (bf16[2,256,512]{1,2,0:T(8,128)(2,1)S(1)}, bf16[2,256,512]{1,2,0:T(8,128)(2,1)S(1)}, u32[]{:S(2)}, u32[]{:S(2)}) collective-permute-start(bf16[2,256,512]{1,2,0:T(8,128)(2,1)S(1)} %pad_maximum_fusion), channel_id=1, source_target_pairs={{0,1},{1,2},{2,3},{3,4},{4,5},{5,6},{6,7},{7,8},{8,9},{9,10},{10,1... | collective-permute-start | bytes 1572872 | tf_op jit(solution)/shard_map/ppermute | solution.py:18
  15.1 6.1 %collective-permute-done = bf16[2,256,512]{1,2,0:T(8,128)(2,1)S(1)} collective-permute-done((bf16[2,256,512]{1,2,0:T(8,128)(2,1)S(1)}, bf16[2,256,512]{1,2,0:T(8,128)(2,1)S(1)}, u32[]{:S(2)}, u32[]{:S(2)}) %collective-permute-start) | collective-permute-done | bytes 524320 | tf_op jit(solution)/shard_map/ppermute | solution.py:18
  22.0 8.4 %collective-permute-start.1 = (bf16[2,256,512]{1,2,0:T(8,128)(2,1)S(1)}, bf16[2,256,512]{1,2,0:T(8,128)(2,1)S(1)}, u32[]{:S(2)}, u32[]{:S(2)}) collective-permute-start(bf16[2,256,512]{1,2,0:T(8,128)(2,1)S(1)} %collective-permute-done), channel_id=1, source_target_pairs={{0,1},{1,2},{2,3},{3,4},{4,5},{5,6},{6,7},{7,8},{8,9},{9,10},{10,1... | collective-permute-start | bytes 1572872 | tf_op jit(solution)/shard_map/ppermute | solution.py:18
  30.4 6.1 %collective-permute-done.1 = bf16[2,256,512]{1,2,0:T(8,128)(2,1)S(1)} collective-permute-done((bf16[2,256,512]{1,2,0:T(8,128)(2,1)S(1)}, bf16[2,256,512]{1,2,0:T(8,128)(2,1)S(1)}, u32[]{:S(2)}, u32[]{:S(2)}) %collective-permute-start.1) | collective-permute-done | bytes 524320 | tf_op jit(solution)/shard_map/ppermute | solution.py:18
  37.3 8.3 %collective-permute-start.2 = (bf16[2,256,512]{1,2,0:T(8,128)(2,1)S(1)}, bf16[2,256,512]{1,2,0:T(8,128)(2,1)S(1)}, u32[]{:S(2)}, u32[]{:S(2)}) collective-permute-start(bf16[2,256,512]{1,2,0:T(8,128)(2,1)S(1)} %collective-permute-done.1), channel_id=1, source_target_pairs={{0,1},{1,2},{2,3},{3,4},{4,5},{5,6},{6,7},{7,8},{8,9},{9,10},{10,1... | collective-permute-start | bytes 1572872 | tf_op jit(solution)/shard_map/ppermute | solution.py:18
  45.6 6.1 %collective-permute-done.2 = bf16[2,256,512]{1,2,0:T(8,128)(2,1)S(1)} collective-permute-done((bf16[2,256,512]{1,2,0:T(8,128)(2,1)S(1)}, bf16[2,256,512]{1,2,0:T(8,128)(2,1)S(1)}, u32[]{:S(2)}, u32[]{:S(2)}) %collective-permute-start.2) | collective-permute-done | bytes 524320 | tf_op jit(solution)/shard_map/ppermute | solution.py:18
  52.5 8.3 %collective-permute-start.3 = (bf16[2,256,512]{1,2,0:T(8,128)(2,1)S(1)}, bf16[2,256,512]{1,2,0:T(8,128)(2,1)S(1)}, u32[]{:S(2)}, u32[]{:S(2)}) collective-permute-start(bf16[2,256,512]{1,2,0:T(8,128)(2,1)S(1)} %collective-permute-done.2), channel_id=1, source_target_pairs={{0,1},{1,2},{2,3},{3,4},{4,5},{5,6},{6,7},{7,8},{8,9},{9,10},{10,1... | collective-permute-start | bytes 1572872 | tf_op jit(solution)/shard_map/ppermute | solution.py:18
  60.8 6.1 %collective-permute-done.3 = bf16[2,256,512]{1,2,0:T(8,128)(2,1)S(1)} collective-permute-done((bf16[2,256,512]{1,2,0:T(8,128)(2,1)S(1)}, bf16[2,256,512]{1,2,0:T(8,128)(2,1)S(1)}, u32[]{:S(2)}, u32[]{:S(2)}) %collective-permute-start.3) | collective-permute-done | bytes 524320 | tf_op jit(solution)/shard_map/ppermute | solution.py:18
  67.7 8.3 %collective-permute-start.4 = (bf16[2,256,512]{1,2,0:T(8,128)(2,1)S(1)}, bf16[2,256,512]{1,2,0:T(8,128)(2,1)S(1)}, u32[]{:S(2)}, u32[]{:S(2)}) collective-permute-start(bf16[2,256,512]{1,2,0:T(8,128)(2,1)S(1)} %collective-permute-done.3), channel_id=1, source_target_pairs={{0,1},{1,2},{2,3},{3,4},{4,5},{5,6},{6,7},{7,8},{8,9},{9,10},{10,1... | collective-permute-start | bytes 1572872 | tf_op jit(solution)/shard_map/ppermute | solution.py:18
  76.0 6.1 %collective-permute-done.4 = bf16[2,256,512]{1,2,0:T(8,128)(2,1)S(1)} collective-permute-done((bf16[2,256,512]{1,2,0:T(8,128)(2,1)S(1)}, bf16[2,256,512]{1,2,0:T(8,128)(2,1)S(1)}, u32[]{:S(2)}, u32[]{:S(2)}) %collective-permute-start.4) | collective-permute-done | bytes 524320 | tf_op jit(solution)/shard_map/ppermute | solution.py:18
  82.1 8.3 %collective-permute-start.5 = (bf16[2,256,512]{1,2,0:T(8,128)(2,1)S(1)}, bf16[2,256,512]{1,2,0:T(8,128)(2,1)}, u32[]{:S(2)}, u32[]{:S(2)}) collective-permute-start(bf16[2,256,512]{1,2,0:T(8,128)(2,1)S(1)} %collective-permute-done.4), channel_id=1, source_target_pairs={{0,1},{1,2},{2,3},{3,4},{4,5},{5,6},{6,7},{7,8},{8,9},{9,10},{10,1... | collective-permute-start | bytes 1572872 | tf_op jit(solution)/shard_map/ppermute | solution.py:18
  91.4 5.1 %collective-permute-done.5 = bf16[2,256,512]{1,2,0:T(8,128)(2,1)} collective-permute-done((bf16[2,256,512]{1,2,0:T(8,128)(2,1)S(1)}, bf16[2,256,512]{1,2,0:T(8,128)(2,1)}, u32[]{:S(2)}, u32[]{:S(2)}) %collective-permute-start.5) | collective-permute-done | bytes 524320 | tf_op jit(solution)/shard_map/ppermute | solution.py:18
  96.5 8.4 %collective-permute-start.6 = (bf16[2,256,512]{1,2,0:T(8,128)(2,1)}, bf16[2,256,512]{1,2,0:T(8,128)(2,1)S(1)}, u32[]{:S(2)}, u32[]{:S(2)}) collective-permute-start(bf16[2,256,512]{1,2,0:T(8,128)(2,1)} %collective-permute-done.5), channel_id=1, source_target_pairs={{0,1},{1,2},{2,3},{3,4},{4,5},{5,6},{6,7},{7,8},{8,9},{9,10},{10,1... | collective-permute-start | bytes 1572872 | tf_op jit(solution)/shard_map/ppermute | solution.py:18
  105.2 6.1 %collective-permute-done.6 = bf16[2,256,512]{1,2,0:T(8,128)(2,1)S(1)} collective-permute-done((bf16[2,256,512]{1,2,0:T(8,128)(2,1)}, bf16[2,256,512]{1,2,0:T(8,128)(2,1)S(1)}, u32[]{:S(2)}, u32[]{:S(2)}) %collective-permute-start.6) | collective-permute-done | bytes 524320 | tf_op jit(solution)/shard_map/ppermute | solution.py:18
  111.3 8.5 %collective-permute-start.7 = (bf16[2,256,512]{1,2,0:T(8,128)(2,1)S(1)}, bf16[2,256,512]{1,2,0:T(8,128)(2,1)S(1)}, u32[]{:S(2)}, u32[]{:S(2)}) collective-permute-start(bf16[2,256,512]{1,2,0:T(8,128)(2,1)S(1)} %collective-permute-done.6), channel_id=1, source_target_pairs={{0,1},{1,2},{2,3},{3,4},{4,5},{5,6},{6,7},{7,8},{8,9},{9,10},{10,1... | collective-permute-start | bytes 1572872 | tf_op jit(solution)/shard_map/ppermute | solution.py:18
  130.9 5.2 %fusion.54 = f32[4,256]{1,0:T(4,128)S(1)} fusion(pred[256,2304]{0,1:T(8,128)(4,1)S(1)} %and_and_fusion, bf16[2304,4,128]{0,2,1:T(8,128)(2,1)} %bitcast.103, bf16[256,512]{1,0:T(8,128)(2,1)S(1)} %copy-done.13), kind=kOutput, calls=%fused_computation.85 | convolution fusion | flops 613419264 | bytes 3215360 | tf_op jit(solution)/shard_map/sub | solution.py:39
  136.1 7.3 %fusion.10 = bf16[4,128,256]{2,1,0:T(8,128)(2,1)S(1)} fusion(bf16[2304,4,128]{0,2,1:T(8,128)(2,1)} %bitcast.105, f32[4,256]{1,0:T(4,128)S(1)} %fusion.54, pred[256,2304]{0,1:T(8,128)(4,1)S(1)} %and_and_fusion, bf16[2304,4,128]{0,2,1:T(8,128)(2,1)} %bitcast.104, bf16[256,512]{1,0:T(8,128)(2,1)S(1)} %copy-done.13), kind=kOutput, calls=%fused_computation.17 | convolution fusion | flops 1219890432 | bytes 5836800 | tf_op jit(solution)/shard_map/hqk,khd->qhd/dot_general | solution.py:41
  144.4 13.6 %all_to_all.45 = bf16[4,64,2048]{2,1,0:T(8,128)(2,1)S(1)} all-to-all(bf16[4,64,2048]{2,1,0:T(8,128)(2,1)S(1)} %bitcast.102), channel_id=1, replica_groups=mesh['z_lo'=4,'x'=4,'y'=8,'z_hi'=2,'core'=2] {'x'}, dimensions={0} | all-to-all | bytes 2097152 | tf_op jit(solution)/shard_map/all_to_all | solution.py:79
  158.9 9.7 %all-to-all-start.1 = ((bf16[4,16,2048]{2,1,0:T(8,128)(2,1)}), bf16[4,16,2048]{2,1,0:T(8,128)(2,1)S(1)}, u32[]{:S(2)}, u32[]{:S(2)}) async-start(bf16[4,16,2048]{2,1,0:T(8,128)(2,1)} %bitcast.110), calls=%async_computation.1 | async-start | bytes 524288 | tf_op jit(solution)/shard_map/all_to_all | solution.py:79
  180.0 23.6 %all-to-all-start.2 = ((bf16[16,16,512]{2,1,0:T(8,128)(2,1)}), bf16[16,16,512]{2,1,0:T(8,128)(2,1)S(1)}, u32[]{:S(2)}, u32[]{:S(2)}) async-start(bf16[16,16,512]{2,1,0:T(8,128)(2,1)} %all_to_all.34), calls=%async_computation.2 | async-start | bytes 524288 | tf_op jit(solution)/shard_map/all_to_all | solution.py:79
  204.4 7.2 %collective-permute-start.9 = (bf16[256,512]{1,0:T(8,128)(2,1)}, bf16[256,512]{1,0:T(8,128)(2,1)}, u32[]{:S(2)}, u32[]{:S(2)}) collective-permute-start(bf16[256,512]{1,0:T(8,128)(2,1)} %copy.47), channel_id=1, source_target_pairs={{0,2},{2,0},{1,3},{3,1},{4,6},{6,4},{5,7},{7,5},{8,10},{10,8},{9,1... | collective-permute-start | bytes 786440 | tf_op jit(solution)/shard_map/ppermute | solution.py:75
  222.1 4.9 %collective-permute-done.9 = bf16[256,512]{1,0:T(8,128)(2,1)} collective-permute-done((bf16[256,512]{1,0:T(8,128)(2,1)}, bf16[256,512]{1,0:T(8,128)(2,1)}, u32[]{:S(2)}, u32[]{:S(2)}) %collective-permute-start.9) | collective-permute-done | bytes 262176 | tf_op jit(solution)/shard_map/ppermute | solution.py:75
  238.1 36.2 %all-to-all-start.4 = ((bf16[8,64,512]{2,1,0:T(8,128)(2,1)}), bf16[8,64,512]{2,1,0:T(8,128)(2,1)S(1)}, u32[]{:S(2)}, u32[]{:S(2)}) async-start(bf16[8,64,512]{2,1,0:T(8,128)(2,1)} %bitcast.120), calls=%async_computation.4 | async-start | bytes 1048576 | tf_op jit(solution)/shard_map/all_to_all | solution.py:79
  275.0 17.2 %all-to-all-done.4 = bf16[8,64,512]{2,1,0:T(8,128)(2,1)S(1)} async-done(((bf16[8,64,512]{2,1,0:T(8,128)(2,1)}), bf16[8,64,512]{2,1,0:T(8,128)(2,1)S(1)}, u32[]{:S(2)}, u32[]{:S(2)}) %all-to-all-start.4) | async-done | bytes 524320 | tf_op jit(solution)/shard_map/all_to_all | solution.py:79
  (95 shorter events, 54.7 us)
Async XLA Ops:
  0.6 143.0 %copy-start = (bf16[512,2048]{1,0:T(8,128)(2,1)S(1)}, bf16[512,2048]{1,0:T(8,128)(2,1)}, u32[]{:S(2)}) copy-start(bf16[512,2048]{1,0:T(8,128)(2,1)} %param.14) | copy-start | bytes 6291460
  3.0 18.1 %collective-permute-start = (bf16[2,256,512]{1,2,0:T(8,128)(2,1)S(1)}, bf16[2,256,512]{1,2,0:T(8,128)(2,1)S(1)}, u32[]{:S(2)}, u32[]{:S(2)}) collective-permute-start(bf16[2,256,512]{1,2,0:T(8,128)(2,1)S(1)} %pad_maximum_fusion), channel_id=1, source_target_pairs={{0,1},{1,2},{2,3},{3,4},{4,5},{5,6},{6,7},{7,8},{8,9},{9,10},{10,1... | collective-permute-start | bytes 1572872 | tf_op jit(solution)/shard_map/ppermute | solution.py:18
  22.0 14.5 %collective-permute-start.1 = (bf16[2,256,512]{1,2,0:T(8,128)(2,1)S(1)}, bf16[2,256,512]{1,2,0:T(8,128)(2,1)S(1)}, u32[]{:S(2)}, u32[]{:S(2)}) collective-permute-start(bf16[2,256,512]{1,2,0:T(8,128)(2,1)S(1)} %collective-permute-done), channel_id=1, source_target_pairs={{0,1},{1,2},{2,3},{3,4},{4,5},{5,6},{6,7},{7,8},{8,9},{9,10},{10,1... | collective-permute-start | bytes 1572872 | tf_op jit(solution)/shard_map/ppermute | solution.py:18
  37.3 14.4 %collective-permute-start.2 = (bf16[2,256,512]{1,2,0:T(8,128)(2,1)S(1)}, bf16[2,256,512]{1,2,0:T(8,128)(2,1)S(1)}, u32[]{:S(2)}, u32[]{:S(2)}) collective-permute-start(bf16[2,256,512]{1,2,0:T(8,128)(2,1)S(1)} %collective-permute-done.1), channel_id=1, source_target_pairs={{0,1},{1,2},{2,3},{3,4},{4,5},{5,6},{6,7},{7,8},{8,9},{9,10},{10,1... | collective-permute-start | bytes 1572872 | tf_op jit(solution)/shard_map/ppermute | solution.py:18
  52.5 14.4 %collective-permute-start.3 = (bf16[2,256,512]{1,2,0:T(8,128)(2,1)S(1)}, bf16[2,256,512]{1,2,0:T(8,128)(2,1)S(1)}, u32[]{:S(2)}, u32[]{:S(2)}) collective-permute-start(bf16[2,256,512]{1,2,0:T(8,128)(2,1)S(1)} %collective-permute-done.2), channel_id=1, source_target_pairs={{0,1},{1,2},{2,3},{3,4},{4,5},{5,6},{6,7},{7,8},{8,9},{9,10},{10,1... | collective-permute-start | bytes 1572872 | tf_op jit(solution)/shard_map/ppermute | solution.py:18
  67.7 14.4 %collective-permute-start.4 = (bf16[2,256,512]{1,2,0:T(8,128)(2,1)S(1)}, bf16[2,256,512]{1,2,0:T(8,128)(2,1)S(1)}, u32[]{:S(2)}, u32[]{:S(2)}) collective-permute-start(bf16[2,256,512]{1,2,0:T(8,128)(2,1)S(1)} %collective-permute-done.3), channel_id=1, source_target_pairs={{0,1},{1,2},{2,3},{3,4},{4,5},{5,6},{6,7},{7,8},{8,9},{9,10},{10,1... | collective-permute-start | bytes 1572872 | tf_op jit(solution)/shard_map/ppermute | solution.py:18
  82.1 29.2 %copy-start.11 = (bf16[2,256,512]{1,2,0:T(8,128)(2,1)}, bf16[2,256,512]{1,2,0:T(8,128)(2,1)S(1)}, u32[]{:S(2)}) copy-start(bf16[2,256,512]{1,2,0:T(8,128)(2,1)S(1)} %collective-permute-done.4) | copy-start | bytes 1572868
  82.1 14.4 %collective-permute-start.5 = (bf16[2,256,512]{1,2,0:T(8,128)(2,1)S(1)}, bf16[2,256,512]{1,2,0:T(8,128)(2,1)}, u32[]{:S(2)}, u32[]{:S(2)}) collective-permute-start(bf16[2,256,512]{1,2,0:T(8,128)(2,1)S(1)} %collective-permute-done.4), channel_id=1, source_target_pairs={{0,1},{1,2},{2,3},{3,4},{4,5},{5,6},{6,7},{7,8},{8,9},{9,10},{10,1... | collective-permute-start | bytes 1572872 | tf_op jit(solution)/shard_map/ppermute | solution.py:18
  91.4 36.8 %copy-start.10 = (bf16[2,256,512]{1,2,0:T(8,128)(2,1)S(1)}, bf16[2,256,512]{1,2,0:T(8,128)(2,1)}, u32[]{:S(2)}) copy-start(bf16[2,256,512]{1,2,0:T(8,128)(2,1)} %copy-done.9) | copy-start | bytes 1572868
  91.4 36.9 %copy-start.8 = (bf16[2,256,512]{1,2,0:T(8,128)(2,1)S(1)}, bf16[2,256,512]{1,2,0:T(8,128)(2,1)}, u32[]{:S(2)}) copy-start(bf16[2,256,512]{1,2,0:T(8,128)(2,1)} %copy-done.7) | copy-start | bytes 1572868
  91.4 36.9 %copy-start.6 = (bf16[2,256,512]{1,2,0:T(8,128)(2,1)S(1)}, bf16[2,256,512]{1,2,0:T(8,128)(2,1)}, u32[]{:S(2)}) copy-start(bf16[2,256,512]{1,2,0:T(8,128)(2,1)} %copy-done.5) | copy-start | bytes 1572868
  91.4 37.0 %copy-start.4 = (bf16[2,256,512]{1,2,0:T(8,128)(2,1)S(1)}, bf16[2,256,512]{1,2,0:T(8,128)(2,1)}, u32[]{:S(2)}) copy-start(bf16[2,256,512]{1,2,0:T(8,128)(2,1)} %copy-done.3) | copy-start | bytes 1572868
  96.5 14.8 %collective-permute-start.6 = (bf16[2,256,512]{1,2,0:T(8,128)(2,1)}, bf16[2,256,512]{1,2,0:T(8,128)(2,1)S(1)}, u32[]{:S(2)}, u32[]{:S(2)}) collective-permute-start(bf16[2,256,512]{1,2,0:T(8,128)(2,1)} %collective-permute-done.5), channel_id=1, source_target_pairs={{0,1},{1,2},{2,3},{3,4},{4,5},{5,6},{6,7},{7,8},{8,9},{9,10},{10,1... | collective-permute-start | bytes 1572872 | tf_op jit(solution)/shard_map/ppermute | solution.py:18
  111.3 14.6 %collective-permute-start.7 = (bf16[2,256,512]{1,2,0:T(8,128)(2,1)S(1)}, bf16[2,256,512]{1,2,0:T(8,128)(2,1)S(1)}, u32[]{:S(2)}, u32[]{:S(2)}) collective-permute-start(bf16[2,256,512]{1,2,0:T(8,128)(2,1)S(1)} %collective-permute-done.6), channel_id=1, source_target_pairs={{0,1},{1,2},{2,3},{3,4},{4,5},{5,6},{6,7},{7,8},{8,9},{9,10},{10,1... | collective-permute-start | bytes 1572872 | tf_op jit(solution)/shard_map/ppermute | solution.py:18
  143.3 25.2 %copy-start.14 = (f32[256]{0:T(256)S(1)}, f32[256]{0:T(256)}, u32[]{:S(2)}) copy-start(f32[256]{0:T(256)} %param.19) | copy-start | bytes 3076
  158.9 15.3 %all-to-all-start.1 = ((bf16[4,16,2048]{2,1,0:T(8,128)(2,1)}), bf16[4,16,2048]{2,1,0:T(8,128)(2,1)S(1)}, u32[]{:S(2)}, u32[]{:S(2)}) async-start(bf16[4,16,2048]{2,1,0:T(8,128)(2,1)} %bitcast.110), calls=%async_computation.1 | async-start | bytes 524288 | tf_op jit(solution)/shard_map/all_to_all | solution.py:79
  174.2 3.7 %copy-start.12 = (bf16[2048,128]{1,0:T(8,128)(2,1)S(1)}, bf16[2048,128]{1,0:T(8,128)(2,1)}, u32[]{:S(2)}) copy-start(bf16[2048,128]{1,0:T(8,128)(2,1)} %param.16) | copy-start | bytes 1572868
  177.2 26.4 %copy-start.2 = (bf16[4,128,256]{2,1,0:T(8,128)(2,1)S(1)}, bf16[4,128,256]{2,1,0:T(8,128)(2,1)}, u32[]{:S(2)}) copy-start(bf16[4,128,256]{2,1,0:T(8,128)(2,1)} %copy-done.1) | copy-start | bytes 786436
  180.0 35.6 %all-to-all-start.2 = ((bf16[16,16,512]{2,1,0:T(8,128)(2,1)}), bf16[16,16,512]{2,1,0:T(8,128)(2,1)S(1)}, u32[]{:S(2)}, u32[]{:S(2)}) async-start(bf16[16,16,512]{2,1,0:T(8,128)(2,1)} %all_to_all.34), calls=%async_computation.2 | async-start | bytes 524288 | tf_op jit(solution)/shard_map/all_to_all | solution.py:79
  204.4 22.6 %collective-permute-start.9 = (bf16[256,512]{1,0:T(8,128)(2,1)}, bf16[256,512]{1,0:T(8,128)(2,1)}, u32[]{:S(2)}, u32[]{:S(2)}) collective-permute-start(bf16[256,512]{1,0:T(8,128)(2,1)} %copy.47), channel_id=1, source_target_pairs={{0,2},{2,0},{1,3},{3,1},{4,6},{6,4},{5,7},{7,5},{8,10},{10,8},{9,1... | collective-permute-start | bytes 786440 | tf_op jit(solution)/shard_map/ppermute | solution.py:75
  216.6 18.7 %all-to-all-start.3 = ((bf16[4,256,512]{2,1,0:T(8,128)(2,1)}), bf16[4,256,512]{2,1,0:T(8,128)(2,1)S(1)}, u32[]{:S(2)}, u32[]{:S(2)}) async-start(bf16[4,256,512]{2,1,0:T(8,128)(2,1)} %broadcast_in_dim.22), calls=%async_computation.3 | async-start | bytes 2097152 | tf_op jit(solution)/shard_map/all_to_all | solution.py:79
  220.2 10.3 %collective-permute-start.8 = (bf16[256,512]{1,0:T(8,128)(2,1)}, bf16[256,512]{1,0:T(8,128)(2,1)}, u32[]{:S(2)}, u32[]{:S(2)}) collective-permute-start(bf16[256,512]{1,0:T(8,128)(2,1)} %copy.47), channel_id=1, source_target_pairs={{0,1},{1,0},{2,3},{3,2},{4,5},{5,4},{6,7},{7,6},{8,9},{9,8},{10,11... | collective-permute-start | bytes 786440 | tf_op jit(solution)/shard_map/ppermute | solution.py:75
  227.0 4.7 %collective-permute-start.10 = (bf16[256,512]{1,0:T(8,128)(2,1)}, bf16[256,512]{1,0:T(8,128)(2,1)}, u32[]{:S(2)}, u32[]{:S(2)}) collective-permute-start(bf16[256,512]{1,0:T(8,128)(2,1)} %collective-permute-done.9), channel_id=1, source_target_pairs={{0,1},{1,0},{2,3},{3,2},{4,5},{5,4},{6,7},{7,6},{8,9},{9,8},{10,11... | collective-permute-start | bytes 786440 | tf_op jit(solution)/shard_map/ppermute | solution.py:75
  238.1 54.1 %all-to-all-start.4 = ((bf16[8,64,512]{2,1,0:T(8,128)(2,1)}), bf16[8,64,512]{2,1,0:T(8,128)(2,1)S(1)}, u32[]{:S(2)}, u32[]{:S(2)}) async-start(bf16[8,64,512]{2,1,0:T(8,128)(2,1)} %bitcast.120), calls=%async_computation.4 | async-start | bytes 1048576 | tf_op jit(solution)/shard_map/all_to_all | solution.py:79
  (6 other events, 6.8 us)

commit v2 on v1

--- a/solution.py
+++ b/solution.py
@@ -1,45 +1,174 @@
+import functools
 import math
 
 import jax
 import jax.numpy as jnp
 from jax import lax
+from jax.experimental import pallas as pl
+from jax.experimental.pallas import tpu as pltpu
 from jax.sharding import Mesh
 from jax.sharding import PartitionSpec as P
 
 HD = 128
+FLOOR = -1e20
+MASKED = -1e30
 
 
 EPS = 1e-05
 
 
-def from_behind(array, axis, by):
-    length = lax.axis_size(axis)
-    pairs = [(i, i + by) for i in range(length) if 0 <= i + by < length]
-    return lax.ppermute(array, axis, pairs)
-
-
-def doc_index(lengths, positions):
-    ends = jnp.cumsum(lengths)
-    return jnp.sum((ends[None, :] <= positions[:, None]).astype(jnp.int32), axis=1)
-
-
-def attend(queries, key_rows, value_rows, query_pos, key_pos, lengths, heads):
-    count = queries.shape[0]
-    width = queries.shape[1] // heads
-    q_heads = queries.reshape(count, heads, width)
-    k_heads = key_rows.reshape(-1, heads, width)
-    v_heads = value_rows.reshape(-1, heads, width)
-    scores = jnp.einsum("qhd,khd->hqk", q_heads, k_heads, preferred_element_type=jnp.float32) * (
-        1.0 / math.sqrt(width)
-    )
-    allowed = doc_index(lengths, query_pos)[:, None] == doc_index(lengths, key_pos)[None, :]
-    allowed = allowed & (key_pos[None, :] <= query_pos[:, None]) & (key_pos[None, :] >= 0)
-    scores = jnp.where(allowed[None], scores, -1e30)
-    top = jnp.max(scores, axis=2, keepdims=True)
-    raised = jnp.exp(scores - top)
-    probs = (raised / jnp.sum(raised, axis=2, keepdims=True)).astype(jnp.bfloat16)
-    output = jnp.einsum("hqk,khd->qhd", probs, v_heads, preferred_element_type=jnp.float32)
-    return output.reshape(count, heads * width).astype(jnp.bfloat16)
+def attend_kernel(lengths, where, q_ref, here_ref, one_ref, two_ref, *rest, final):
+    out_refs, (start_ref, top_ref, total_ref, acc_ref) = rest[:-4], rest[-4:]
+    blocks, rows, feat = q_ref.shape
+    heads = feat // HD
+    scale = 1.4426950408889634 / math.sqrt(HD)
+    query = where[0] * rows + lax.broadcasted_iota(jnp.int32, (1, blocks * rows), 1)
+
+    def pass_end(i, carry):
+        end, start, first, second = carry
+        end = end + lengths[i]
+        return (
+            end,
+            jnp.where(query >= end, end, start),
+            jnp.where(where[0] * rows >= end, end, first),
+            jnp.where((where[0] + 1) * rows >= end, end, second),
+        )
+
+    zero = jnp.int32(0)
+    _, start, first, second = lax.fori_loop(
+        0, lengths.shape[0], pass_end, (zero, jnp.zeros_like(query), zero, zero)
+    )
+    for block in range(blocks):
+        start_ref[block] = jnp.broadcast_to(start[:, block * rows : (block + 1) * rows], (8, rows))
+    top_ref[...] = jnp.full_like(top_ref, FLOOR)
+    total_ref[...] = jnp.zeros_like(total_ref)
+    acc_ref[...] = jnp.zeros_like(acc_ref)
+
+    for behind, kv_ref in enumerate((here_ref, one_ref, two_ref)):
+
+        def tile(i, carry, behind=behind, kv_ref=kv_ref):
+            block, core = i // 2, i % 2
+            key_block = where[1] - 4 * behind + core
+            query_block = where[0] + block
+            lowest = jnp.where(block == 0, first, second)
+            live = (key_block <= query_block) & (key_block * rows + rows > lowest)
+
+            @pl.when(live)
+            def _():
+                key = key_block * rows + lax.broadcasted_iota(jnp.int32, (rows, rows), 0)
+                at = query_block * rows + lax.broadcasted_iota(jnp.int32, (rows, rows), 1)
+                kept = (key >= start_ref[block, 0:1, :]) & (key <= at)
+                for head in range(heads):
+                    cols = slice(head * HD, (head + 1) * HD)
+                    scores = lax.dot_general(
+                        kv_ref[core, 0, :, cols],
+                        q_ref[block, :, cols],
+                        (((1,), (1,)), ((), ())),
+                        preferred_element_type=jnp.float32,
+                    )
+                    scores = jnp.where(kept, scores * scale, MASKED)
+                    old = top_ref[block, head, 0:1, :]
+                    top = jnp.maximum(old, jnp.max(scores, axis=0, keepdims=True))
+                    raised = jnp.exp2(scores - top)
+                    decay = jnp.exp2(old - top)
+                    total = total_ref[block, head, 0:1, :] * decay
+                    total = total + jnp.sum(raised, axis=0, keepdims=True)
+                    product = lax.dot_general(
+                        kv_ref[core, 1, :, cols],
+                        raised.astype(jnp.bfloat16),
+                        (((0,), (0,)), ((), ())),
+                        preferred_element_type=jnp.float32,
+                    )
+                    acc_ref[block, head] = acc_ref[block, head] * decay + product
+                    top_ref[block, head] = jnp.broadcast_to(top, (8, rows))
+                    total_ref[block, head] = jnp.broadcast_to(total, (8, rows))
+
+            return carry
+
+        lax.fori_loop(0, 2 * blocks, tile, 0)
+
+    for block in range(blocks):
+        span = slice(block * rows, (block + 1) * rows)
+        for head in range(heads):
+            total = total_ref[block, head, 0:1, :]
+            some = total > 0.0
+            total = jnp.where(some, total, 1.0)
+            level = jnp.where(some, top_ref[block, head, 0:1, :] + jnp.log2(total), MASKED)
+            values = acc_ref[block, head] * (1.0 / total)
+            out_ref = out_refs[0]
+            out_ref[head * HD : (head + 1) * HD, span] = values.astype(out_ref.dtype)
+            top_ref[block, head, 0:1, :] = level
+        if final:
+            levels = jnp.concatenate([top_ref[block, head, 0:1, :] for head in range(heads)] * 4, axis=0)
+            out_refs[1][:, span] = levels
+        else:
+            parts = []
+            for head in range(heads):
+                left = top_ref[block, head, 0:1, :]
+                for _ in range(3):
+                    part = left.astype(jnp.bfloat16).astype(jnp.float32)
+                    parts.append(part)
+                    left = left - part
+            parts.append(jnp.zeros((16 - 3 * heads, rows), jnp.float32))
+            out_refs[0][heads * HD :, span] = jnp.concatenate(parts, axis=0).astype(jnp.bfloat16)
+
+
+def attend(lengths, where, queries, here, one, two, final):
+    blocks, rows, feat = queries.shape
+    heads = feat // HD
+    if final:
+        out = (
+            jax.ShapeDtypeStruct((feat, blocks * rows), jnp.float32),
+            jax.ShapeDtypeStruct((4 * heads, blocks * rows), jnp.float32),
+        )
+    else:
+        out = (jax.ShapeDtypeStruct((feat + 16, blocks * rows), jnp.bfloat16),)
+    smem = pl.BlockSpec(memory_space=pltpu.SMEM)
+    vmem = pl.BlockSpec(memory_space=pltpu.VMEM)
+    return pl.pallas_call(
+        functools.partial(attend_kernel, final=final),
+        out_shape=out,
+        in_specs=[smem, smem] + [vmem] * 4,
+        out_specs=tuple(vmem for _ in out),
+        scratch_shapes=[
+            pltpu.VMEM((blocks, 8, rows), jnp.int32),
+            pltpu.VMEM((blocks, heads, 8, rows), jnp.float32),
+            pltpu.VMEM((blocks, heads, 8, rows), jnp.float32),
+            pltpu.VMEM((blocks, heads, HD, rows), jnp.float32),
+        ],
+        compiler_params=pltpu.CompilerParams(vmem_limit_bytes=32 * 1024 * 1024),
+        cost_estimate=pl.CostEstimate(
+            flops=4 * 9 * rows * rows * feat, bytes_accessed=3 << 20, transcendentals=10 * rows * rows * heads
+        ),
+        name="attend_own" if final else "attend_across",
+    )(lengths, where, queries, here, one, two)
+
+
+def join_kernel(values_ref, levels_ref, other_ref, out_ref):
+    feat, count = values_ref.shape
+    for head in range(feat // HD):
+        span = slice(head * HD, (head + 1) * HD)
+        mine = levels_ref[head : head + 1, :]
+        other = other_ref[feat : feat + 16, :].astype(jnp.float32)
+        other = other[3 * head : 3 * head + 1] + other[3 * head + 1 : 3 * head + 2] + other[3 * head + 2 : 3 * head + 3]
+        top = jnp.maximum(mine, other)
+        mine, other = jnp.exp2(mine - top), jnp.exp2(other - top)
+        part = 1.0 / (mine + other)
+        joined = values_ref[span, :] * (mine * part) + other_ref[span, :].astype(jnp.float32) * (other * part)
+        out_ref[:, span] = joined.T.astype(jnp.bfloat16)
+
+
+def join(values, levels, other):
+    feat, count = values.shape
+    vmem = pl.BlockSpec(memory_space=pltpu.VMEM)
+    return pl.pallas_call(
+        join_kernel,
+        out_shape=jax.ShapeDtypeStruct((count, feat), jnp.bfloat16),
+        in_specs=[vmem] * 3,
+        out_specs=vmem,
+        compiler_params=pltpu.CompilerParams(vmem_limit_bytes=32 * 1024 * 1024),
+        name="join",
+    )(values, levels, other)
 
 
 def head_rows(hidden_sum, noise_draws, w_noise, w_out, target, loss_weights):
@@ -75,6 +204,17 @@
     return lax.ppermute(array, axis, [(0, 1), (1, 0)])
 
 
+def shift(array, axis):
+    length = lax.axis_size(axis)
+    return lax.ppermute(array, axis, [(i, (i + 1) % length) for i in range(length)])
+
+
+def sides(mine, other, core):
+    return jnp.where(
+        core == 0, jnp.concatenate((mine, other), axis=2), jnp.concatenate((other, mine), axis=2)
+    )
+
+
 def exchange(array, axis):
     return lax.all_to_all(array, axis, 0, 0, tiled=True)
 
@@ -92,23 +232,27 @@
     loss_weights,
 ):
     rows, feat = queries.shape
-    heads = feat // HD
-    ctx = ("y", "z_hi", "core")
-    block_index = lax.axis_index(ctx)
-    z_hi, core = lax.axis_index("z_hi"), lax.axis_index("core")
-    reach = min(8, lax.axis_size(ctx) // 2)
-    stacked = jnp.stack((key_rows, value_rows))
-    arrived = []
-    moving = stacked
-    for step in range(reach):
-        moving = from_behind(moving, ctx, 1)
-        arrived.append(moving)
-    pieces = arrived[::-1]
-    pieces.append(stacked)
-    window = jnp.concatenate(pieces, axis=1)
-    query_pos = block_index * rows + jnp.arange(rows, dtype=jnp.int32)
-    key_pos = (block_index - reach) * rows + jnp.arange((reach + 1) * rows, dtype=jnp.int32)
-    attended = attend(queries, window[0], window[1], query_pos, key_pos, lengths, heads)
+    z_hi, core, y = lax.axis_index("z_hi"), lax.axis_index("core"), lax.axis_index("y")
+    half = feat // 2
+
+    kv = jnp.stack((key_rows, value_rows)).reshape(2, rows, 2, half).transpose(2, 0, 1, 3)
+    kv = exchange(kv.reshape(4, rows, half), "core").reshape(2, 2, rows, half)
+    asked = queries.reshape(rows, 2, half).transpose(1, 0, 2)
+    asked = exchange(asked, "core")
+    one = shift(kv, "y")
+    asked_across = swap(asked, "z_hi")
+    two = shift(one, "y")
+    base = 4 * y.astype(jnp.int32)
+    own, across = base + 2 * z_hi.astype(jnp.int32), base + 2 * (1 - z_hi.astype(jnp.int32))
+    sent = attend(lengths, jnp.stack((across, own)), asked_across, kv, one, two, False)[0]
+    back = swap(sent, "z_hi")
+    values, levels = attend(lengths, jnp.stack((own, own)), asked, kv, one, two, True)
+    pair = join(values, levels, back).reshape(2, rows, half)
+
+    pair_across = swap(pair, "z_hi")
+    pair_beside = swap(pair, "core")
+    near = sides(pair, pair_beside, core)
+    attended = lax.dynamic_index_in_dim(near, core, 0, keepdims=False)
 
     n_zl, n_x, n_y = (lax.axis_size(name) for name in ("z_lo", "x", "y"))
     n_zh, n_c = lax.axis_size("z_hi"), lax.axis_size("core")
@@ -122,11 +266,7 @@
     partial = exchange(partial, "z_lo").reshape(n_zl, share, width)
     hidden_sum = jnp.sum(partial.astype(jnp.float32), axis=0)
 
-    beside = swap(attended, "core")
-    across = swap(attended, "z_hi")
-    corner = swap(across, "core")
-    near = jnp.where(core == 0, jnp.stack((attended, beside)), jnp.stack((beside, attended)))
-    far = jnp.where(core == 0, jnp.stack((across, corner)), jnp.stack((corner, across)))
+    far = sides(pair_across, swap(pair_across, "core"), core)
     group = jnp.where(z_hi == 0, jnp.stack((near, far)), jnp.stack((far, near)))
     group = group.reshape(n_zh, n_c, n_zl, n_x, share, feat).transpose(3, 0, 2, 1, 4, 5)
     group = group.reshape(n_zh * n_c * rows, feat)

time: 294 us -> 192 us (0.65)
  starting transfers between devices: 155 us -> 59.5 us
  blocking collectives: 13.6 us -> 40.2 us
  waiting for transfers between devices: 77.4 us -> 61.4 us
  matrix products: 19.6 us -> 6.08 us
  local copies, waits for them, and re-layouts: 16.9 us -> 8.69 us
  Pallas kernels: 0 us -> 6.89 us
    ppermute x8 -> x2, starting transfers between devices: 70.5 us -> 3.82 us  [shift(): lax.ppermute(array, axis, [(i, (i + 1) % length) for i in range(length)])]
    all_to_all x4, starting transfers between devices: 73 us -> 28.9 us  [exchange(): return lax.all_to_all(array, axis, 0, 0, tiled=True)]
    ppermute x8 -> x2, waiting for transfers between devices: 45.7 us -> 14.3 us  [shift(): lax.ppermute(array, axis, [(i, (i + 1) % length) for i in range(length)])]
    all_to_all x1 -> x3, blocking collectives: 13.6 us -> 40.2 us  [exchange(): return lax.all_to_all(array, axis, 0, 0, tiled=True)]
    ppermute x3 -> x5, starting transfers between devices: 11.7 us -> 26.7 us  [swap(): return lax.ppermute(array, axis, [(0, 1), (1, 0)])]
    ppermute x3 -> x5, waiting for transfers between devices: 4.94 us -> 18.7 us  [swap(): return lax.ppermute(array, axis, [(0, 1), (1, 0)])]
    dot_general x1 -> x0, matrix products: 7.26 us -> none  [attend(): jnp.einsum('hqk,khd->qhd', probs, v_heads, preferred_element_type=jnp.flo...]
    unnamed x41 -> x13, local copies, waits for them, and re-layouts: 8.81 us -> 1.78 us
  transfers between devices with their start and end apart: 15 -> 11, of which waited for: 13 -> 10; matrix products, arithmetic and copies ran while one was open for 4% -> 5% of each run, Pallas kernels for 0% -> 2%
where the time goes in v2:
time: 192 us; the launch traced here: 191 us
  waiting for transfers between devices  61.4 us (32%)
  starting transfers between devices  59.5 us (31%)
  blocking collectives  40.2 us (21%)
  local copies, waits for them, and re-layouts  8.69 us (5%)
  other arithmetic  7.36 us (4%)
  Pallas kernels  6.89 us (4%)
  matrix products  6.08 us (3%)
    all_to_all x3, blocking collectives, exchange(): return lax.all_to_all(array, axis, 0, 0, tiled=True)  40.2 us
    all_to_all x4, starting transfers between devices, exchange(): return lax.all_to_all(array, axis, 0, 0, tiled=True)  28.9 us
    all_to_all x4, waiting for transfers between devices, exchange(): return lax.all_to_all(array, axis, 0, 0, tiled=True)  28.3 us
    ppermute x5, starting transfers between devices, swap(): return lax.ppermute(array, axis, [(0, 1), (1, 0)])  26.7 us
    ppermute x5, waiting for transfers between devices, swap(): return lax.ppermute(array, axis, [(0, 1), (1, 0)])  18.7 us
    ppermute x2, waiting for transfers between devices, shift(): lax.ppermute(array, axis, [(i, (i + 1) % length) for i in range(length)])  14.3 us
    pallas_call x2, Pallas kernels, attend(): pl.pallas_call(functools.partial(attend_kernel, final=final), out_shape=o...  6.7 us
  transfers between devices with their start and end apart: 11, of which 10 were waited for; matrix products, arithmetic and copies ran while one was open for 5% of the time, Pallas kernels for 2%

profile of v2, /device:TPU:1, one launch (start us, length us, event | category | flops | bytes accessed | tf_op | source)
XLA Modules:
  0.0 191.0 jit_solution(2010644969450413078)
XLA Ops:
  3.7 10.7 %all_to_all.55 = bf16[4,256,256]{2,1,0:T(8,128)(2,1)S(1)} all-to-all(bf16[4,256,256]{2,1,0:T(8,128)(2,1)S(1)} %bitcast.77), channel_id=1, replica_groups=mesh['z_lo'=4,'x'=4,'y'=8,'z_hi'=2,'core'=2] {'core'}, dimensions={0} | all-to-all | bytes 1048576 | tf_op jit(solution)/shard_map/all_to_all | solution.py:219
  14.3 1.9 collective-permute-start
  16.2 14.3 %collective-permute-done.one_ref = bf16[2,2,256,256]{3,2,1,0:T(8,128)(2,1)S(1)} collective-permute-done((bf16[2,2,256,256]{3,2,1,0:T(8,128)(2,1)S(1)}, bf16[2,2,256,256]{3,2,1,0:T(8,128)(2,1)S(1)}, u32[]{:S(2)}, u32[]{:S(2)}) %collective-permute-start) | collective-permute-done | bytes 524320 | tf_op jit(solution)/shard_map/ppermute | solution.py:209
  30.6 1.9 collective-permute-start.1
  34.4 5.8 %all_to_all.56.q_ref = bf16[2,256,256]{2,1,0:T(8,128)(2,1)S(1)} all-to-all(bf16[2,256,256]{2,1,0:T(8,128)(2,1)} %bitcast.84), channel_id=1, replica_groups=mesh['z_lo'=4,'x'=4,'y'=8,'z_hi'=2,'core'=2] {'core'}, dimensions={0} | all-to-all | bytes 524288 | tf_op jit(solution)/shard_map/all_to_all | solution.py:219
  40.2 5.8 %collective-permute-start.2 = (bf16[2,256,256]{2,1,0:T(8,128)(2,1)S(1)}, bf16[2,256,256]{2,1,0:T(8,128)(2,1)}, u32[]{:S(2)}, u32[]{:S(2)}) collective-permute-start(bf16[2,256,256]{2,1,0:T(8,128)(2,1)S(1)} %all_to_all.56.q_ref), channel_id=1, source_target_pairs={{0,2},{2,0},{1,3},{3,1},{4,6},{6,4},{5,7},{7,5},{8,10},{10,8},{9,1... | collective-permute-start | bytes 786440 | tf_op jit(solution)/shard_map/ppermute | solution.py:204
  46.1 8.9 %collective-permute-done.2.q_ref = bf16[2,256,256]{2,1,0:T(8,128)(2,1)} collective-permute-done((bf16[2,256,256]{2,1,0:T(8,128)(2,1)S(1)}, bf16[2,256,256]{2,1,0:T(8,128)(2,1)}, u32[]{:S(2)}, u32[]{:S(2)}) %collective-permute-start.2) | collective-permute-done | bytes 262176 | tf_op jit(solution)/shard_map/ppermute | solution.py:204
  55.1 2.7 %attend_across.1 = bf16[272,512]{1,0:T(8,128)(2,1)S(1)} custom-call(s32[64]{0:T(128)S(1)} %copy-done.1, s32[2]{0:T(128)S(1)} %pad_add_fusion.1.where, bf16[2,256,256]{2,1,0:T(8,128)(2,1)} %collective-permute-done.2.q_ref, bf16[2,2,256,256]{3,2,1,0:T(8,128)(2,1)S(1)} %bitcast.74, bf16[2,2,256,256]{3,2,1,0:T(8,128)(2,1)S(1)} %collective-permute-done.one_ref, ...), custom_call_target="tpu_custom_call" | custom-call | flops 603979776 | bytes 3145728 | tf_op jit(solution)/shard_map/attend_across/pallas_call | solution.py:128
  57.8 7.0 %collective-permute-start.3 = (bf16[272,512]{1,0:T(8,128)(2,1)S(1)}, bf16[272,512]{1,0:T(8,128)(2,1)S(1)}, u32[]{:S(2)}, u32[]{:S(2)}) collective-permute-start(bf16[272,512]{1,0:T(8,128)(2,1)S(1)} %attend_across.1), channel_id=1, source_target_pairs={{0,2},{2,0},{1,3},{3,1},{4,6},{6,4},{5,7},{7,5},{8,10},{10,8},{9,1... | collective-permute-start | bytes 835592 | tf_op jit(solution)/shard_map/ppermute | solution.py:204
  64.9 4.0 %attend_own.1 = (f32[256,512]{1,0:T(8,128)S(1)}, f32[8,512]{1,0:T(8,128)S(1)}) custom-call(s32[64]{0:T(128)S(1)} %copy-done.1, s32[2]{0:T(128)S(1)} %pad_add_fusion.where, bf16[2,256,256]{2,1,0:T(8,128)(2,1)S(1)} %all_to_all.56.q_ref, bf16[2,2,256,256]{3,2,1,0:T(8,128)(2,1)S(1)} %bitcast.75, bf16[2,2,256,256]{3,2,1,0:T(8,128)(2,1)S(1)} %collective-permute-done.one_ref, ...), custom_call_target="tpu_custom_call" | custom-call | flops 603979776 | bytes 3145728 | tf_op jit(solution)/shard_map/attend_own/pallas_call | solution.py:128
  68.9 1.6 collective-permute-done.3.other_ref
  70.7 4.2 %collective-permute-start.4 = (bf16[2,256,256]{2,1,0:T(8,128)(2,1)S(1)}, bf16[2,256,256]{2,1,0:T(8,128)(2,1)S(1)}, u32[]{:S(2)}, u32[]{:S(2)}) collective-permute-start(bf16[2,256,256]{2,1,0:T(8,128)(2,1)S(1)} %bitcast.69), channel_id=1, source_target_pairs={{0,1},{1,0},{2,3},{3,2},{4,5},{5,4},{6,7},{7,6},{8,9},{9,8},{10,11... | collective-permute-start | bytes 786440 | tf_op jit(solution)/shard_map/ppermute | solution.py:204
  77.6 23.7 %all_to_all.57 = bf16[4,64,2048]{2,1,0:T(8,128)(2,1)S(1)} all-to-all(bf16[4,64,2048]{2,1,0:T(8,128)(2,1)S(1)} %bitcast.76), channel_id=1, replica_groups=mesh['z_lo'=4,'x'=4,'y'=8,'z_hi'=2,'core'=2] {'x'}, dimensions={0} | all-to-all | bytes 2097152 | tf_op jit(solution)/shard_map/all_to_all | solution.py:219
  102.2 4.3 %all-to-all-start.3 = ((bf16[4,16,2048]{2,1,0:T(8,128)(2,1)}), bf16[4,16,2048]{2,1,0:T(8,128)(2,1)S(1)}, u32[]{:S(2)}, u32[]{:S(2)}) async-start(bf16[4,16,2048]{2,1,0:T(8,128)(2,1)} %bitcast.78), calls=%async_computation.3 | async-start | bytes 524288 | tf_op jit(solution)/shard_map/all_to_all | solution.py:219
  107.5 4.7 %all-to-all-done.3 = bf16[4,16,2048]{2,1,0:T(8,128)(2,1)S(1)} async-done(((bf16[4,16,2048]{2,1,0:T(8,128)(2,1)}), bf16[4,16,2048]{2,1,0:T(8,128)(2,1)S(1)}, u32[]{:S(2)}, u32[]{:S(2)}) %all-to-all-start.3) | async-done | bytes 262176 | tf_op jit(solution)/shard_map/all_to_all | solution.py:219
  116.9 11.2 %all-to-all-start.4 = ((bf16[16,16,512]{2,1,0:T(8,128)(2,1)}), bf16[16,16,512]{2,1,0:T(8,128)(2,1)S(1)}, u32[]{:S(2)}, u32[]{:S(2)}) async-start(bf16[16,16,512]{2,1,0:T(8,128)(2,1)} %all_to_all.42), calls=%async_computation.4 | async-start | bytes 524288 | tf_op jit(solution)/shard_map/all_to_all | solution.py:219
  128.1 7.2 %collective-permute-start.5 = (bf16[2,256,256]{2,1,0:T(8,128)(2,1)S(1)}, bf16[2,256,256]{2,1,0:T(8,128)(2,1)}, u32[]{:S(2)}, u32[]{:S(2)}) collective-permute-start(bf16[2,256,256]{2,1,0:T(8,128)(2,1)S(1)} %bitcast.71), channel_id=1, source_target_pairs={{0,2},{2,0},{1,3},{3,1},{4,6},{6,4},{5,7},{7,5},{8,10},{10,8},{9,1... | collective-permute-start | bytes 786440 | tf_op jit(solution)/shard_map/ppermute | solution.py:204
  135.3 4.9 %all-to-all-done.4 = bf16[16,16,512]{2,1,0:T(8,128)(2,1)S(1)} async-done(((bf16[16,16,512]{2,1,0:T(8,128)(2,1)}), bf16[16,16,512]{2,1,0:T(8,128)(2,1)S(1)}, u32[]{:S(2)}, u32[]{:S(2)}) %all-to-all-start.4) | async-done | bytes 262176 | tf_op jit(solution)/shard_map/all_to_all | solution.py:219
  141.2 3.5 %all-to-all-start.5 = ((bf16[4,256,512]{2,1,0:T(8,128)(2,1)}), bf16[4,256,512]{2,1,0:T(8,128)(2,1)S(1)}, u32[]{:S(2)}, u32[]{:S(2)}) async-start(bf16[4,256,512]{2,1,0:T(8,128)(2,1)} %broadcast_in_dim.8), calls=%async_computation.5 | async-start | bytes 2097152 | tf_op jit(solution)/shard_map/all_to_all | solution.py:219
  144.7 6.8 %collective-permute-done.5 = bf16[2,256,256]{2,1,0:T(8,128)(2,1)} collective-permute-done((bf16[2,256,256]{2,1,0:T(8,128)(2,1)S(1)}, bf16[2,256,256]{2,1,0:T(8,128)(2,1)}, u32[]{:S(2)}, u32[]{:S(2)}) %collective-permute-start.5) | collective-permute-done | bytes 262176 | tf_op jit(solution)/shard_map/ppermute | solution.py:204
  151.5 2.6 %collective-permute-start.6 = (bf16[2,256,256]{2,1,0:T(8,128)(2,1)}, bf16[2,256,256]{2,1,0:T(8,128)(2,1)}, u32[]{:S(2)}, u32[]{:S(2)}) collective-permute-start(bf16[2,256,256]{2,1,0:T(8,128)(2,1)} %collective-permute-done.5), channel_id=1, source_target_pairs={{0,1},{1,0},{2,3},{3,2},{4,5},{5,4},{6,7},{7,6},{8,9},{9,8},{10,11... | collective-permute-start | bytes 786440 | tf_op jit(solution)/shard_map/ppermute | solution.py:204
  159.7 2.7 %convolution_convert_fusion.1 = bf16[512,512]{1,0:T(8,128)(2,1)} fusion(bf16[1024,512]{1,0:T(8,128)(2,1)S(1)} %bitcast.80, bf16[1024,512]{1,0:T(8,128)(2,1)} %bitcast.81), kind=kOutput, calls=%fused_computation.4 | convolution fusion | flops 537133056 | bytes 2621440 | tf_op jit(solution)/shard_map/dot_general | solution.py:289
  162.5 9.9 %all-to-all-start.6 = ((bf16[8,64,512]{2,1,0:T(8,128)(2,1)}), bf16[8,64,512]{2,1,0:T(8,128)(2,1)S(1)}, u32[]{:S(2)}, u32[]{:S(2)}) async-start(bf16[8,64,512]{2,1,0:T(8,128)(2,1)} %bitcast.90), calls=%async_computation.6 | async-start | bytes 1048576 | tf_op jit(solution)/shard_map/all_to_all | solution.py:219
  173.1 17.2 %all-to-all-done.6 = bf16[8,64,512]{2,1,0:T(8,128)(2,1)S(1)} async-done(((bf16[8,64,512]{2,1,0:T(8,128)(2,1)}), bf16[8,64,512]{2,1,0:T(8,128)(2,1)S(1)}, u32[]{:S(2)}, u32[]{:S(2)}) %all-to-all-start.6) | async-done | bytes 524320 | tf_op jit(solution)/shard_map/all_to_all | solution.py:219
  (55 shorter events, 22.5 us)
Async XLA Ops:
  0.6 76.2 %copy-start = (bf16[512,2048]{1,0:T(8,128)(2,1)S(1)}, bf16[512,2048]{1,0:T(8,128)(2,1)}, u32[]{:S(2)}) copy-start(bf16[512,2048]{1,0:T(8,128)(2,1)} %param.14) | copy-start | bytes 6291460
  3.6 51.5 %copy-start.1 = (s32[64]{0:T(128)S(1)}, s32[64]{0:T(128)}, u32[]{:S(2)}) copy-start(s32[64]{0:T(128)} %lengths.3) | copy-start | bytes 772
  14.3 16.2 %collective-permute-start = (bf16[2,2,256,256]{3,2,1,0:T(8,128)(2,1)S(1)}, bf16[2,2,256,256]{3,2,1,0:T(8,128)(2,1)S(1)}, u32[]{:S(2)}, u32[]{:S(2)}) collective-permute-start(bf16[2,2,256,256]{3,2,1,0:T(8,128)(2,1)S(1)} %bitcast.73), channel_id=1, source_target_pairs={{0,4},{4,8},{8,12},{12,16},{16,20},{20,24},{24,28},{28,0},{1,5},{5... | collective-permute-start | bytes 1572872 | tf_op jit(solution)/shard_map/ppermute | solution.py:209
  30.6 24.5 %collective-permute-start.1 = (bf16[2,2,256,256]{3,2,1,0:T(8,128)(2,1)S(1)}, bf16[2,2,256,256]{3,2,1,0:T(8,128)(2,1)}, u32[]{:S(2)}, u32[]{:S(2)}) collective-permute-start(bf16[2,2,256,256]{3,2,1,0:T(8,128)(2,1)S(1)} %collective-permute-done.one_ref), channel_id=1, source_target_pairs={{0,4},{4,8},{8,12},{12,16},{16,20},{20,24},{24,28},{28,0},{1,5},{5... | collective-permute-start | bytes 1572872 | tf_op jit(solution)/shard_map/ppermute | solution.py:209
  40.2 14.8 %collective-permute-start.2 = (bf16[2,256,256]{2,1,0:T(8,128)(2,1)S(1)}, bf16[2,256,256]{2,1,0:T(8,128)(2,1)}, u32[]{:S(2)}, u32[]{:S(2)}) collective-permute-start(bf16[2,256,256]{2,1,0:T(8,128)(2,1)S(1)} %all_to_all.56.q_ref), channel_id=1, source_target_pairs={{0,2},{2,0},{1,3},{3,1},{4,6},{6,4},{5,7},{7,5},{8,10},{10,8},{9,1... | collective-permute-start | bytes 786440 | tf_op jit(solution)/shard_map/ppermute | solution.py:204
  57.8 12.7 %collective-permute-start.3 = (bf16[272,512]{1,0:T(8,128)(2,1)S(1)}, bf16[272,512]{1,0:T(8,128)(2,1)S(1)}, u32[]{:S(2)}, u32[]{:S(2)}) collective-permute-start(bf16[272,512]{1,0:T(8,128)(2,1)S(1)} %attend_across.1), channel_id=1, source_target_pairs={{0,2},{2,0},{1,3},{3,1},{4,6},{6,4},{5,7},{7,5},{8,10},{10,8},{9,1... | collective-permute-start | bytes 835592 | tf_op jit(solution)/shard_map/ppermute | solution.py:204
  70.7 5.3 %collective-permute-start.4 = (bf16[2,256,256]{2,1,0:T(8,128)(2,1)S(1)}, bf16[2,256,256]{2,1,0:T(8,128)(2,1)S(1)}, u32[]{:S(2)}, u32[]{:S(2)}) collective-permute-start(bf16[2,256,256]{2,1,0:T(8,128)(2,1)S(1)} %bitcast.69), channel_id=1, source_target_pairs={{0,1},{1,0},{2,3},{3,2},{4,5},{5,4},{6,7},{7,6},{8,9},{9,8},{10,11... | collective-permute-start | bytes 786440 | tf_op jit(solution)/shard_map/ppermute | solution.py:204
  76.0 1.6 copy-start.3
  76.1 0.7 copy-start.2
  77.5 29.0 %copy-start.5 = (f32[256]{0:T(256)S(1)}, f32[256]{0:T(256)}, u32[]{:S(2)}) copy-start(f32[256]{0:T(256)} %param.19) | copy-start | bytes 3076
  102.2 11.4 %copy-start.4 = (bf16[2048,128]{1,0:T(8,128)(2,1)S(1)}, bf16[2048,128]{1,0:T(8,128)(2,1)}, u32[]{:S(2)}) copy-start(bf16[2048,128]{1,0:T(8,128)(2,1)} %param.16) | copy-start | bytes 1572868
  102.2 10.0 %all-to-all-start.3 = ((bf16[4,16,2048]{2,1,0:T(8,128)(2,1)}), bf16[4,16,2048]{2,1,0:T(8,128)(2,1)S(1)}, u32[]{:S(2)}, u32[]{:S(2)}) async-start(bf16[4,16,2048]{2,1,0:T(8,128)(2,1)} %bitcast.78), calls=%async_computation.3 | async-start | bytes 524288 | tf_op jit(solution)/shard_map/all_to_all | solution.py:219
  116.9 23.3 %all-to-all-start.4 = ((bf16[16,16,512]{2,1,0:T(8,128)(2,1)}), bf16[16,16,512]{2,1,0:T(8,128)(2,1)S(1)}, u32[]{:S(2)}, u32[]{:S(2)}) async-start(bf16[16,16,512]{2,1,0:T(8,128)(2,1)} %all_to_all.42), calls=%async_computation.4 | async-start | bytes 524288 | tf_op jit(solution)/shard_map/all_to_all | solution.py:219
  128.1 23.4 %collective-permute-start.5 = (bf16[2,256,256]{2,1,0:T(8,128)(2,1)S(1)}, bf16[2,256,256]{2,1,0:T(8,128)(2,1)}, u32[]{:S(2)}, u32[]{:S(2)}) collective-permute-start(bf16[2,256,256]{2,1,0:T(8,128)(2,1)S(1)} %bitcast.71), channel_id=1, source_target_pairs={{0,2},{2,0},{1,3},{3,1},{4,6},{6,4},{5,7},{7,5},{8,10},{10,8},{9,1... | collective-permute-start | bytes 786440 | tf_op jit(solution)/shard_map/ppermute | solution.py:204
  141.2 18.5 %all-to-all-start.5 = ((bf16[4,256,512]{2,1,0:T(8,128)(2,1)}), bf16[4,256,512]{2,1,0:T(8,128)(2,1)S(1)}, u32[]{:S(2)}, u32[]{:S(2)}) async-start(bf16[4,256,512]{2,1,0:T(8,128)(2,1)} %broadcast_in_dim.8), calls=%async_computation.5 | async-start | bytes 2097152 | tf_op jit(solution)/shard_map/all_to_all | solution.py:219
  151.5 4.0 %collective-permute-start.6 = (bf16[2,256,256]{2,1,0:T(8,128)(2,1)}, bf16[2,256,256]{2,1,0:T(8,128)(2,1)}, u32[]{:S(2)}, u32[]{:S(2)}) collective-permute-start(bf16[2,256,256]{2,1,0:T(8,128)(2,1)} %collective-permute-done.5), channel_id=1, source_target_pairs={{0,1},{1,0},{2,3},{3,2},{4,5},{5,4},{6,7},{7,6},{8,9},{9,8},{10,11... | collective-permute-start | bytes 786440 | tf_op jit(solution)/shard_map/ppermute | solution.py:204
  162.5 27.8 %all-to-all-start.6 = ((bf16[8,64,512]{2,1,0:T(8,128)(2,1)}), bf16[8,64,512]{2,1,0:T(8,128)(2,1)S(1)}, u32[]{:S(2)}, u32[]{:S(2)}) async-start(bf16[8,64,512]{2,1,0:T(8,128)(2,1)} %bitcast.90), calls=%async_computation.6 | async-start | bytes 1048576 | tf_op jit(solution)/shard_map/all_to_all | solution.py:219

commit v3 on v1

v3 whole, which is shorter than its diff:
```python
import functools
import math

import jax
import jax.numpy as jnp
from jax import lax
from jax.experimental import pallas as pl
from jax.experimental.pallas import tpu as pltpu
from jax.sharding import Mesh
from jax.sharding import PartitionSpec as P

HD = 128
FLOOR = -1e20
MASKED = -1e30


EPS = 1e-05


def attend_kernel(lengths, where, q_ref, *rest, final):
    kv_refs, out_refs = rest[:12], rest[12:-4]
    start_ref, top_ref, total_ref, acc_ref = rest[-4:]
    rows, feat = q_ref.shape
    heads = feat // HD
    scale = 1.4426950408889634 / math.sqrt(HD)
    query_at = where[0] * rows
    query = query_at + lax.broadcasted_iota(jnp.int32, (1, rows), 1)

    def pass_end(i, carry):
        end, start, lowest = carry
        end = end + lengths[i]
        return (end, jnp.where(query >= end, end, start), jnp.where(query_at >= end, end, lowest))

    zero = jnp.int32(0)
    _, start, lowest = lax.fori_loop(
        0, lengths.shape[0], pass_end, (zero, jnp.zeros_like(query), zero)
    )
    start_ref[...] = jnp.broadcast_to(start, start_ref.shape)
    top_ref[...] = jnp.full_like(top_ref, FLOOR)
    total_ref[...] = jnp.zeros_like(total_ref)
    acc_ref[...] = jnp.zeros_like(acc_ref)

    for i in range(6):
        k_ref, v_ref = kv_refs[2 * i], kv_refs[2 * i + 1]
        key_at = (where[1 + i % 2] - 4 * (i // 2)) * rows
        live = (key_at <= query_at) & (key_at + rows > lowest)

        @pl.when(live)
        def _(k_ref=k_ref, v_ref=v_ref, key_at=key_at):
            key = key_at + lax.broadcasted_iota(jnp.int32, (rows, rows), 0)
            at = query_at + lax.broadcasted_iota(jnp.int32, (rows, rows), 1)
            kept = (key >= start_ref[0:1, :]) & (key <= at)

            def two_heads(pair, carry):
                for head in (2 * pair, 2 * pair + 1):
                    cols = pl.ds(pl.multiple_of(head * HD, HD), HD)
                    scores = lax.dot_general(
                        k_ref[:, cols],
                        q_ref[:, cols],
                        (((1,), (1,)), ((), ())),
                        preferred_element_type=jnp.float32,
                    )
                    scores = jnp.where(kept, scores * scale, MASKED)
                    old = top_ref[head, 0:1, :]
                    top = jnp.maximum(old, jnp.max(scores, axis=0, keepdims=True))
                    raised = jnp.exp2(scores - top)
                    decay = jnp.exp2(old - top)
                    total = total_ref[head, 0:1, :] * decay
                    total = total + jnp.sum(raised, axis=0, keepdims=True)
                    product = lax.dot_general(
                        v_ref[:, cols],
                        raised.astype(jnp.bfloat16),
                        (((0,), (0,)), ((), ())),
                        preferred_element_type=jnp.float32,
                    )
                    acc_ref[head] = acc_ref[head] * decay + product
                    top_ref[head] = jnp.broadcast_to(top, (8, rows))
                    total_ref[head] = jnp.broadcast_to(total, (8, rows))
                return carry

            lax.fori_loop(0, heads // 2, two_heads, 0)

    parts = []
    for head in range(heads):
        total = total_ref[head, 0:1, :]
        some = total > 0.0
        total = jnp.where(some, total, 1.0)
        level = jnp.where(some, top_ref[head, 0:1, :] + jnp.log2(total), MASKED)
        values = acc_ref[head] * (1.0 / total)
        out_refs[0][head * HD : (head + 1) * HD, :] = values.astype(out_refs[0].dtype)
        if final:
            parts.append(level)
        else:
            for _ in range(3):
                part = level.astype(jnp.bfloat16).astype(jnp.float32)
                parts.append(part)
                level = level - part
    count = 8 if final else 16
    parts.append(jnp.zeros((count - len(parts), rows), jnp.float32))
    parts = jnp.concatenate(parts, axis=0)
    if final:
        out_refs[1][...] = parts
    else:
        out_refs[0][heads * HD :, :] = parts.astype(jnp.bfloat16)


def attend(lengths, where, queries, kv, final):
    rows, feat = queries.shape
    heads = feat // HD
    if final:
        out = (
            jax.ShapeDtypeStruct((feat, rows), jnp.float32),
            jax.ShapeDtypeStruct((8, rows), jnp.float32),
        )
    else:
        out = (jax.ShapeDtypeStruct((feat + 16, rows), jnp.bfloat16),)
    smem = pl.BlockSpec(memory_space=pltpu.SMEM)
    vmem = pl.BlockSpec(memory_space=pltpu.VMEM)
    return pl.pallas_call(
        functools.partial(attend_kernel, final=final),
        out_shape=out,
        in_specs=[smem, smem] + [vmem] * (1 + len(kv)),
        out_specs=tuple(vmem for _ in out),
        scratch_shapes=[
            pltpu.VMEM((8, rows), jnp.int32),
            pltpu.VMEM((heads, 8, rows), jnp.float32),
            pltpu.VMEM((heads, 8, rows), jnp.float32),
            pltpu.VMEM((heads, HD, rows), jnp.float32),
        ],
        compiler_params=pltpu.CompilerParams(vmem_limit_bytes=16 * 1024 * 1024),
        cost_estimate=pl.CostEstimate(
            flops=4 * 5 * rows * rows * feat, bytes_accessed=3 << 20, transcendentals=5 * rows * rows * heads
        ),
        name="attend_own" if final else "attend_across",
    )(lengths, where, queries, *kv)


def join_kernel(values_ref, levels_ref, other_ref, w_ref, out_ref, partial_ref, order_ref, n_zl):
    feat, count = values_ref.shape
    share = 16
    three = other_ref[feat : feat + 16, :].astype(jnp.float32)
    for head in range(feat // HD):
        span = slice(head * HD, (head + 1) * HD)
        mine = levels_ref[head : head + 1, :]
        other = three[3 * head : 3 * head + 1] + three[3 * head + 1 : 3 * head + 2] + three[3 * head + 2 : 3 * head + 3]
        top = jnp.maximum(mine, other)
        mine, other = jnp.exp2(mine - top), jnp.exp2(other - top)
        part = 1.0 / (mine + other)
        joined = values_ref[span, :] * (mine * part) + other_ref[span, :].astype(jnp.float32) * (other * part)
        out_ref[:, span] = joined.T.astype(jnp.bfloat16)
    n_x = count // share // n_zl
    for x in range(n_x):
        for z in range(n_zl):
            order_ref[pl.ds((x * n_zl + z) * share, share), :] = out_ref[pl.ds((z * n_x + x) * share, share), :]
    width = w_ref.shape[1]
    for at in range(0, width, 512):
        product = jnp.dot(order_ref[...], w_ref[:, at : at + 512], preferred_element_type=jnp.float32)
        partial_ref[:, at : at + 512] = product.astype(jnp.bfloat16)


def join(values, levels, other, w_first, n_zl):
    feat, count = values.shape
    vmem = pl.BlockSpec(memory_space=pltpu.VMEM)
    return pl.pallas_call(
        functools.partial(join_kernel, n_zl=n_zl),
        out_shape=(
            jax.ShapeDtypeStruct((count, feat), jnp.bfloat16),
            jax.ShapeDtypeStruct((count, w_first.shape[1]), jnp.bfloat16),
        ),
        in_specs=[vmem] * 4,
        out_specs=(vmem, vmem),
        scratch_shapes=[pltpu.VMEM((count, feat), jnp.bfloat16)],
        compiler_params=pltpu.CompilerParams(vmem_limit_bytes=16 * 1024 * 1024),
        name="join",
    )(values, levels, other, w_first)


def head_rows(hidden_sum, noise_draws, w_noise, w_out, target, loss_weights):
    count, samples, depth = noise_draws.shape
    lift = jnp.dot(
        noise_draws.reshape(count * samples, depth), w_noise, preferred_element_type=jnp.float32
    )
    pre = hidden_sum[:, None, :] + lift.reshape(count, samples, -1)
    act = jax.nn.silu(pre).astype(jnp.bfloat16)
    latent = jnp.dot(act.reshape(count * samples, -1), w_out, preferred_element_type=jnp.float32)
    latent = latent.reshape(count, samples, -1)
    width = latent.shape[2]
    apart = latent[:, :, None, :] - latent[:, None, :, :]
    pair = jnp.sqrt(jnp.mean(apart * apart, axis=3) + EPS)
    others = 1.0 - jnp.eye(samples, dtype=jnp.float32)
    miss = latent - target.astype(jnp.float32)[:, None, :]
    far = jnp.sqrt(jnp.mean(miss * miss, axis=2) + EPS)
    spread = samples * (samples - 1.0)
    losses = 2.0 / samples * jnp.sum(far, axis=1) - jnp.sum(pair * others, axis=(1, 2)) / spread
    toward = 2.0 / samples * miss / (width * far[:, :, None])
    repel = 2.0 / spread * jnp.sum((others[None] / (width * pair))[:, :, :, None] * apart, axis=2)
    latent_grad = (loss_weights[:, None, None] * (toward - repel)).astype(jnp.bfloat16)
    act_grad = jnp.dot(
        latent_grad.reshape(count * samples, width), w_out.T, preferred_element_type=jnp.float32
    )
    act_grad = act_grad.reshape(count, samples, -1)
    sigma = jax.nn.sigmoid(pre)
    pre_grad = act_grad * sigma * (1.0 + pre * (1.0 - sigma))
    return (losses, jnp.sum(pre_grad, axis=1).astype(jnp.bfloat16))


def swap(array, axis):
    return lax.ppermute(array, axis, [(0, 1), (1, 0)])


def shift(array, axis):
    length = lax.axis_size(axis)
    return lax.ppermute(array, axis, [(i, (i + 1) % length) for i in range(length)])


def exchange(array, axis):
    return lax.all_to_all(array, axis, 0, 0, tiled=True)


def contract_kernel(place, units_ref, mine_ref, other_ref, out_ref, rows_ref, total_ref, n_x, n_zl):
    share = 16
    blocks, count, feat = mine_ref.shape
    for block in range(2 * blocks):
        held_ref = mine_ref if block < blocks else other_ref
        z_hi = place[0] if block % 2 == 0 else 1 - place[0]
        core = place[1] if block < blocks else 1 - place[1]
        for x in range(n_x):
            for z in range(n_zl):
                at = (((x * 2 + z_hi) * n_zl + z) * 2 + core) * share
                rows_ref[pl.ds((z * n_x + x) * share, share), :] = units_ref[pl.ds(pl.multiple_of(at, share), share), :]
        product = lax.dot_general(
            rows_ref[...],
            held_ref[block % blocks],
            (((0,), (0,)), ((), ())),
            preferred_element_type=jnp.float32,
        )
        if block == 0:
            total_ref[...] = product
        else:
            total_ref[...] += product
    out_ref[...] = total_ref[...].astype(jnp.bfloat16)


def contract(place, units, mine, other, n_x, n_zl):
    count, feat = mine.shape[1:]
    width = units.shape[1]
    vmem = pl.BlockSpec(memory_space=pltpu.VMEM)
    return pl.pallas_call(
        functools.partial(contract_kernel, n_x=n_x, n_zl=n_zl),
        out_shape=jax.ShapeDtypeStruct((width, feat), jnp.bfloat16),
        in_specs=[pl.BlockSpec(memory_space=pltpu.SMEM)] + [vmem] * 3,
        out_specs=vmem,
        scratch_shapes=[
            pltpu.VMEM((count, width), jnp.bfloat16),
            pltpu.VMEM((width, feat), jnp.float32),
        ],
        compiler_params=pltpu.CompilerParams(vmem_limit_bytes=32 * 1024 * 1024),
        name="contract",
    )(place, units, mine, other)


def shards(
    queries,
    key_rows,
    value_rows,
    lengths,
    w_first,
    w_noise,
    w_out,
    noise_draws,
    target,
    loss_weights,
):
    rows, feat = queries.shape
    n_zl, n_x, n_y, n_zh, n_c = (
        lax.axis_size(name) for name in ("z_lo", "x", "y", "z_hi", "core")
    )
    y = "y"

    one_k, one_v = shift(key_rows, y), shift(value_rows, y)
    asked = swap(queries, "z_hi")
    two_k, two_v = shift(one_k, y), shift(one_v, y)
    kv = []
    for keys, values in ((key_rows, value_rows), (one_k, one_v), (two_k, two_v)):
        kv += [keys, values, swap(keys, "core"), swap(values, "core")]
    block = lax.axis_index(("y", "z_hi", "core")).astype(jnp.int32)
    beside = block + 1 - 2 * (block % 2)
    across = block + 2 - 4 * (block // 2 % 2)
    sent = attend(lengths, jnp.stack((across, block, beside)), asked, kv, False)[0]
    back = swap(sent, "z_hi")
    values, levels = attend(lengths, jnp.stack((block, block, beside)), queries, kv, True)
    attended, partial = join(values, levels, back, w_first, n_zl)

    share = rows // (n_zl * n_x)
    width = w_first.shape[1]

    over_z = swap(attended, "z_hi")
    partial = exchange(partial, "x").reshape(n_x, n_zl * share, width)
    partial = jnp.sum(partial.astype(jnp.float32), axis=0).astype(jnp.bfloat16)
    partial = exchange(partial, "z_lo").reshape(n_zl, share, width)
    hidden_sum = jnp.sum(partial.astype(jnp.float32), axis=0)

    here = lax.axis_index(("z_lo", "x")) * share
    losses_here, grad_here = head_rows(
        hidden_sum,
        lax.dynamic_slice_in_dim(noise_draws, here, share, 0),
        w_noise,
        w_out,
        lax.dynamic_slice_in_dim(target, here, share, 0),
        lax.dynamic_slice_in_dim(loss_weights, here, share, 0),
    )
    part = width // (n_y * n_zh * n_c)
    units = grad_here.reshape(share, n_y, n_zh, n_c, part).transpose(2, 3, 0, 1, 4)
    units = jnp.broadcast_to(units[:, None], (n_zh, n_zl, n_c, share, n_y, part))
    units = units.reshape(n_zh * n_zl * n_c * share, n_y * part)
    units = exchange(units, ("z_hi", "z_lo", "core"))
    units = jnp.broadcast_to(units[None], (n_x,) + units.shape).reshape(-1, n_y * part)
    mine = jnp.stack((attended, over_z))
    other = swap(mine, "core")
    units = exchange(units, "x")
    place = jnp.stack([lax.axis_index(name) for name in ("z_hi", "core")]).astype(jnp.int32)
    carried = contract(place, units, mine, other, n_x, n_zl)
    carried, losses_here = lax.optimization_barrier((carried, losses_here))
    carried = exchange(carried, "y")
    carried = carried.reshape(n_y, part, feat)
    first_grad = jnp.sum(carried.astype(jnp.float32), axis=0).astype(jnp.bfloat16)
    return (attended, losses_here[None, :], first_grad)


def solution(mesh):
    names = ("z_lo", "x", "y", "z_hi", "core")
    fine = Mesh(mesh.devices.reshape(4, 4, 8, 2, 2), names)
    ctx, dp = names[2:], names[:2]
    placed = (
        P(ctx, dp),
        P(ctx, dp),
        P(ctx, dp),
        P(),
        P(dp, None),
        P(),
        P(),
        P(ctx, None, None),
        P(ctx, None),
        P(ctx),
    )
    return jax.shard_map(
        shards,
        mesh=fine,
        in_specs=placed,
        out_specs=(P(ctx, dp), P(ctx, dp), P(ctx, dp)),
        check_vma=False,
    )
```

time: 294 us -> 171 us (0.58)
  starting transfers between devices: 155 us -> 78.7 us
  waiting for transfers between devices: 77.4 us -> 27.5 us
  blocking collectives: 13.6 us -> 44.1 us
  matrix products: 19.6 us -> 2.32 us
  local copies, waits for them, and re-layouts: 16.9 us -> 5.27 us
  Pallas kernels: 0 us -> 7.41 us
  other arithmetic: 9.13 us -> 3.95 us
    ppermute x8 -> x4, starting transfers between devices: 70.5 us -> 12.7 us  [shift(): lax.ppermute(array, axis, [(i, (i + 1) % length) for i in range(length)])]
    all_to_all x4 -> x3, starting transfers between devices: 73 us -> 26.2 us  [exchange(): return lax.all_to_all(array, axis, 0, 0, tiled=True)]
    ppermute x8 -> x4, waiting for transfers between devices: 45.7 us -> 0.01 us  [shift(): lax.ppermute(array, axis, [(i, (i + 1) % length) for i in range(length)])]
    all_to_all x1 -> x2, blocking collectives: 13.6 us -> 44.1 us  [exchange(): return lax.all_to_all(array, axis, 0, 0, tiled=True)]
    ppermute x3 -> x10, starting transfers between devices: 11.7 us -> 39.7 us  [swap(): return lax.ppermute(array, axis, [(0, 1), (1, 0)])]
    all_to_all x4 -> x3, waiting for transfers between devices: 26.8 us -> 14 us  [exchange(): return lax.all_to_all(array, axis, 0, 0, tiled=True)]
    dot_general x3 -> x0, matrix products: 10.7 us -> none  [the longest x1 7.26 us: attend(): jnp.einsum('hqk,khd->qhd', probs, v_heads, preferred_element_type=jnp.flo...]
    ppermute x3 -> x10, waiting for transfers between devices: 4.94 us -> 13.4 us  [swap(): return lax.ppermute(array, axis, [(0, 1), (1, 0)])]
  transfers between devices with their start and end apart: 15 -> 17, of which waited for: 13 -> 7; matrix products, arithmetic and copies ran while one was open for 4% -> 2% of each run, Pallas kernels for 0% -> 2%
where the time goes in v3:
time: 171 us; the launch traced here: 170 us
  starting transfers between devices  78.7 us (46%)
  blocking collectives  44.1 us (26%)
  waiting for transfers between devices  27.5 us (16%)
  Pallas kernels  7.41 us (4%)
  local copies, waits for them, and re-layouts  5.27 us (3%)
  other arithmetic  3.95 us (2%)
  matrix products  2.32 us (1%)
    all_to_all x2, blocking collectives, exchange(): return lax.all_to_all(array, axis, 0, 0, tiled=True)  44.1 us
    ppermute x10, starting transfers between devices, swap(): return lax.ppermute(array, axis, [(0, 1), (1, 0)])  39.7 us
    all_to_all x3, starting transfers between devices, exchange(): return lax.all_to_all(array, axis, 0, 0, tiled=True)  26.2 us
    all_to_all x3, waiting for transfers between devices, exchange(): return lax.all_to_all(array, axis, 0, 0, tiled=True)  14 us
    ppermute x10, waiting for transfers between devices, swap(): return lax.ppermute(array, axis, [(0, 1), (1, 0)])  13.4 us
    ppermute x4, starting transfers between devices, shift(): lax.ppermute(array, axis, [(i, (i + 1) % length) for i in range(length)])  12.7 us
    pallas_call x2, Pallas kernels, attend(): pl.pallas_call(functools.partial(attend_kernel, final=final), out_shape=o...  5.16 us
  transfers between devices with their start and end apart: 17, of which 7 were waited for; matrix products, arithmetic and copies ran while one was open for 2% of the time, Pallas kernels for 2%

profile of v3, /device:TPU:1, one launch (start us, length us, event | category | flops | bytes accessed | tf_op | source)
XLA Modules:
  0.0 170.2 jit_solution(5727602026779477938)
XLA Ops:
  0.6 4.2 %collective-permute-start.2 = (bf16[256,512]{1,0:T(8,128)(2,1)}, bf16[256,512]{1,0:T(8,128)(2,1)S(1)}, u32[]{:S(2)}, u32[]{:S(2)}) collective-permute-start(bf16[256,512]{1,0:T(8,128)(2,1)} %rest_0_.3), channel_id=1, source_target_pairs={{0,4},{4,8},{8,12},{12,16},{16,20},{20,24},{24,28},{28,0},{1,5},{5... | collective-permute-start | bytes 786440 | tf_op jit(solution)/shard_map/ppermute | solution.py:213
  4.8 3.2 %collective-permute-start.3 = (bf16[256,512]{1,0:T(8,128)(2,1)}, bf16[256,512]{1,0:T(8,128)(2,1)S(1)}, u32[]{:S(2)}, u32[]{:S(2)}) collective-permute-start(bf16[256,512]{1,0:T(8,128)(2,1)} %rest_1_.3), channel_id=1, source_target_pairs={{0,4},{4,8},{8,12},{12,16},{16,20},{20,24},{24,28},{28,0},{1,5},{5... | collective-permute-start | bytes 786440 | tf_op jit(solution)/shard_map/ppermute | solution.py:213
  8.0 5.4 %collective-permute-start = (bf16[256,512]{1,0:T(8,128)(2,1)}, bf16[256,512]{1,0:T(8,128)(2,1)S(1)}, u32[]{:S(2)}, u32[]{:S(2)}) collective-permute-start(bf16[256,512]{1,0:T(8,128)(2,1)} %rest_0_.3), channel_id=1, source_target_pairs={{0,1},{1,0},{2,3},{3,2},{4,5},{5,4},{6,7},{7,6},{8,9},{9,8},{10,11... | collective-permute-start | bytes 786440 | tf_op jit(solution)/shard_map/ppermute | solution.py:208
  13.4 1.9 %collective-permute-start.1 = (bf16[256,512]{1,0:T(8,128)(2,1)}, bf16[256,512]{1,0:T(8,128)(2,1)S(1)}, u32[]{:S(2)}, u32[]{:S(2)}) collective-permute-start(bf16[256,512]{1,0:T(8,128)(2,1)} %rest_1_.3), channel_id=1, source_target_pairs={{0,1},{1,0},{2,3},{3,2},{4,5},{5,4},{6,7},{7,6},{8,9},{9,8},{10,11... | collective-permute-start | bytes 786440 | tf_op jit(solution)/shard_map/ppermute | solution.py:208
  15.4 1.9 %collective-permute-start.6 = (bf16[256,512]{1,0:T(8,128)(2,1)S(1)}, bf16[256,512]{1,0:T(8,128)(2,1)S(1)}, u32[]{:S(2)}, u32[]{:S(2)}) collective-permute-start(bf16[256,512]{1,0:T(8,128)(2,1)S(1)} %collective-permute-done.2.rest_4_), channel_id=1, source_target_pairs={{0,4},{4,8},{8,12},{12,16},{16,20},{20,24},{24,28},{28,0},{1,5},{5... | collective-permute-start | bytes 786440 | tf_op jit(solution)/shard_map/ppermute | solution.py:213
  17.3 3.5 %collective-permute-start.7 = (bf16[256,512]{1,0:T(8,128)(2,1)S(1)}, bf16[256,512]{1,0:T(8,128)(2,1)S(1)}, u32[]{:S(2)}, u32[]{:S(2)}) collective-permute-start(bf16[256,512]{1,0:T(8,128)(2,1)S(1)} %collective-permute-done.3.rest_5_), channel_id=1, source_target_pairs={{0,4},{4,8},{8,12},{12,16},{16,20},{20,24},{24,28},{28,0},{1,5},{5... | collective-permute-start | bytes 786440 | tf_op jit(solution)/shard_map/ppermute | solution.py:213
  20.8 10.6 %collective-permute-start.10 = (bf16[256,512]{1,0:T(8,128)(2,1)}, bf16[256,512]{1,0:T(8,128)(2,1)S(1)}, u32[]{:S(2)}, u32[]{:S(2)}) collective-permute-start(bf16[256,512]{1,0:T(8,128)(2,1)} %q_ref.1), channel_id=1, source_target_pairs={{0,2},{2,0},{1,3},{3,1},{4,6},{6,4},{5,7},{7,5},{8,10},{10,8},{9,1... | collective-permute-start | bytes 786440 | tf_op jit(solution)/shard_map/ppermute | solution.py:208
  31.4 3.5 %collective-permute-start.4 = (bf16[256,512]{1,0:T(8,128)(2,1)S(1)}, bf16[256,512]{1,0:T(8,128)(2,1)S(1)}, u32[]{:S(2)}, u32[]{:S(2)}) collective-permute-start(bf16[256,512]{1,0:T(8,128)(2,1)S(1)} %collective-permute-done.2.rest_4_), channel_id=1, source_target_pairs={{0,1},{1,0},{2,3},{3,2},{4,5},{5,4},{6,7},{7,6},{8,9},{9,8},{10,11... | collective-permute-start | bytes 786440 | tf_op jit(solution)/shard_map/ppermute | solution.py:208
  34.9 1.9 %collective-permute-start.5 = (bf16[256,512]{1,0:T(8,128)(2,1)S(1)}, bf16[256,512]{1,0:T(8,128)(2,1)S(1)}, u32[]{:S(2)}, u32[]{:S(2)}) collective-permute-start(bf16[256,512]{1,0:T(8,128)(2,1)S(1)} %collective-permute-done.3.rest_5_), channel_id=1, source_target_pairs={{0,1},{1,0},{2,3},{3,2},{4,5},{5,4},{6,7},{7,6},{8,9},{9,8},{10,11... | collective-permute-start | bytes 786440 | tf_op jit(solution)/shard_map/ppermute | solution.py:208
  36.9 2.4 %collective-permute-start.8 = (bf16[256,512]{1,0:T(8,128)(2,1)S(1)}, bf16[256,512]{1,0:T(8,128)(2,1)S(1)}, u32[]{:S(2)}, u32[]{:S(2)}) collective-permute-start(bf16[256,512]{1,0:T(8,128)(2,1)S(1)} %collective-permute-done.6.rest_8_), channel_id=1, source_target_pairs={{0,1},{1,0},{2,3},{3,2},{4,5},{5,4},{6,7},{7,6},{8,9},{9,8},{10,11... | collective-permute-start | bytes 786440 | tf_op jit(solution)/shard_map/ppermute | solution.py:208
  46.5 2.1 %collective-permute-start.11 = (bf16[528,256]{1,0:T(8,128)(2,1)S(1)}, bf16[528,256]{1,0:T(8,128)(2,1)S(1)}, u32[]{:S(2)}, u32[]{:S(2)}) collective-permute-start(bf16[528,256]{1,0:T(8,128)(2,1)S(1)} %attend_across.1), channel_id=1, source_target_pairs={{0,2},{2,0},{1,3},{3,1},{4,6},{6,4},{5,7},{7,5},{8,10},{10,8},{9,1... | collective-permute-start | bytes 811016 | tf_op jit(solution)/shard_map/ppermute | solution.py:208
  48.6 4.0 %attend_own.1 = (f32[512,256]{1,0:T(8,128)S(1)}, f32[8,256]{1,0:T(8,128)S(1)}) custom-call(s32[64]{0:T(128)S(1)} %copy-done.7, s32[3]{0:T(128)S(1)} %add_add_fusion.where, bf16[256,512]{1,0:T(8,128)(2,1)S(1)} %copy-done.6, bf16[256,512]{1,0:T(8,128)(2,1)S(1)} %copy-done.3, bf16[256,512]{1,0:T(8,128)(2,1)S(1)} %copy-done.5, ...), custom_call_target="tpu_custom_call" | custom-call | flops 671088640 | bytes 3145728 | tf_op jit(solution)/shard_map/attend_own/pallas_call | solution.py:119
  52.7 5.1 %collective-permute-done.11.other_ref = bf16[528,256]{1,0:T(8,128)(2,1)S(1)} collective-permute-done((bf16[528,256]{1,0:T(8,128)(2,1)S(1)}, bf16[528,256]{1,0:T(8,128)(2,1)S(1)}, u32[]{:S(2)}, u32[]{:S(2)}) %collective-permute-start.11) | collective-permute-done | bytes 270368 | tf_op jit(solution)/shard_map/ppermute | solution.py:208
  58.8 15.1 %all_to_all.44 = bf16[4,64,2048]{2,1,0:T(8,128)(2,1)S(1)} all-to-all(bf16[4,64,2048]{2,1,0:T(8,128)(2,1)S(1)} %bitcast.52), channel_id=1, replica_groups=mesh['z_lo'=4,'x'=4,'y'=8,'z_hi'=2,'core'=2] {'x'}, dimensions={0} | all-to-all | bytes 2097152 | tf_op jit(solution)/shard_map/all_to_all | solution.py:217
  74.8 15.1 %all-to-all-start.1 = ((bf16[4,16,2048]{2,1,0:T(8,128)(2,1)}), bf16[4,16,2048]{2,1,0:T(8,128)(2,1)S(1)}, u32[]{:S(2)}, u32[]{:S(2)}) async-start(bf16[4,16,2048]{2,1,0:T(8,128)(2,1)} %bitcast.6), calls=%async_computation.1 | async-start | bytes 524288 | tf_op jit(solution)/shard_map/all_to_all | solution.py:217
  90.8 4.7 %all-to-all-done.1 = bf16[4,16,2048]{2,1,0:T(8,128)(2,1)S(1)} async-done(((bf16[4,16,2048]{2,1,0:T(8,128)(2,1)}), bf16[4,16,2048]{2,1,0:T(8,128)(2,1)S(1)}, u32[]{:S(2)}, u32[]{:S(2)}) %all-to-all-start.1) | async-done | bytes 262176 | tf_op jit(solution)/shard_map/all_to_all | solution.py:217
  100.0 7.7 %all-to-all-start.2 = ((bf16[16,16,512]{2,1,0:T(8,128)(2,1)}), bf16[16,16,512]{2,1,0:T(8,128)(2,1)S(1)}, u32[]{:S(2)}, u32[]{:S(2)}) async-start(bf16[16,16,512]{2,1,0:T(8,128)(2,1)} %all_to_all.33), calls=%async_computation.2 | async-start | bytes 524288 | tf_op jit(solution)/shard_map/all_to_all | solution.py:217
  107.6 7.2 %collective-permute-start.12 = (bf16[256,512]{1,0:T(8,128)(2,1)S(1)}, bf16[256,512]{1,0:T(8,128)(2,1)S(1)}, u32[]{:S(2)}, u32[]{:S(2)}) collective-permute-start(bf16[256,512]{1,0:T(8,128)(2,1)S(1)} %copy-done.8), channel_id=1, source_target_pairs={{0,2},{2,0},{1,3},{3,1},{4,6},{6,4},{5,7},{7,5},{8,10},{10,8},{9,1... | collective-permute-start | bytes 786440 | tf_op jit(solution)/shard_map/ppermute | solution.py:208
  114.9 5.2 %all-to-all-done.2 = bf16[16,16,512]{2,1,0:T(8,128)(2,1)S(1)} async-done(((bf16[16,16,512]{2,1,0:T(8,128)(2,1)}), bf16[16,16,512]{2,1,0:T(8,128)(2,1)S(1)}, u32[]{:S(2)}, u32[]{:S(2)}) %all-to-all-start.2) | async-done | bytes 262176 | tf_op jit(solution)/shard_map/all_to_all | solution.py:217
  121.2 3.5 %all-to-all-start.3 = ((bf16[4,256,512]{2,1,0:T(8,128)(2,1)}), bf16[4,256,512]{2,1,0:T(8,128)(2,1)S(1)}, u32[]{:S(2)}, u32[]{:S(2)}) async-start(bf16[4,256,512]{2,1,0:T(8,128)(2,1)} %broadcast_in_dim.10), calls=%async_computation.3 | async-start | bytes 2097152 | tf_op jit(solution)/shard_map/all_to_all | solution.py:217
  124.7 6.2 %collective-permute-done.12 = bf16[256,512]{1,0:T(8,128)(2,1)S(1)} collective-permute-done((bf16[256,512]{1,0:T(8,128)(2,1)S(1)}, bf16[256,512]{1,0:T(8,128)(2,1)S(1)}, u32[]{:S(2)}, u32[]{:S(2)}) %collective-permute-start.12) | collective-permute-done | bytes 262176 | tf_op jit(solution)/shard_map/ppermute | solution.py:208
  131.0 2.6 %collective-permute-start.13 = (bf16[2,256,512]{2,1,0:T(8,128)(2,1)S(1)}, bf16[2,256,512]{2,1,0:T(8,128)(2,1)S(1)}, u32[]{:S(2)}, u32[]{:S(2)}) collective-permute-start(bf16[2,256,512]{2,1,0:T(8,128)(2,1)S(1)} %pad_maximum_fusion.mine_ref), channel_id=1, source_target_pairs={{0,1},{1,0},{2,3},{3,2},{4,5},{5,4},{6,7},{7,6},{8,9},{9,8},{10,11... | collective-permute-start | bytes 1572872 | tf_op jit(solution)/shard_map/ppermute | solution.py:208
  135.1 4.1 %all-to-all-done.3 = bf16[4,256,512]{2,1,0:T(8,128)(2,1)S(1)} async-done(((bf16[4,256,512]{2,1,0:T(8,128)(2,1)}), bf16[4,256,512]{2,1,0:T(8,128)(2,1)S(1)}, u32[]{:S(2)}, u32[]{:S(2)}) %all-to-all-start.3) | async-done | bytes 1048608 | tf_op jit(solution)/shard_map/all_to_all | solution.py:217
  140.5 29.0 %all_to_all.45 = bf16[8,64,512]{2,1,0:T(8,128)(2,1)S(1)} all-to-all(bf16[8,64,512]{2,1,0:T(8,128)(2,1)S(1)} %bitcast.51), channel_id=1, replica_groups=mesh['z_lo'=4,'x'=4,'y'=8,'z_hi'=2,'core'=2] {'y'}, dimensions={0} | all-to-all | bytes 1048576 | tf_op jit(solution)/shard_map/all_to_all | solution.py:217
  (65 shorter events, 18.9 us)
Async XLA Ops:
  0.6 94.9 %copy-start = (bf16[128,2048]{1,0:T(8,128)(2,1)S(1)}, bf16[128,2048]{1,0:T(8,128)(2,1)}, u32[]{:S(2)}) copy-start(bf16[128,2048]{1,0:T(8,128)(2,1)} %param.15) | copy-start | bytes 1572868
  0.6 14.7 %collective-permute-start.2 = (bf16[256,512]{1,0:T(8,128)(2,1)}, bf16[256,512]{1,0:T(8,128)(2,1)S(1)}, u32[]{:S(2)}, u32[]{:S(2)}) collective-permute-start(bf16[256,512]{1,0:T(8,128)(2,1)} %rest_0_.3), channel_id=1, source_target_pairs={{0,4},{4,8},{8,12},{12,16},{16,20},{20,24},{24,28},{28,0},{1,5},{5... | collective-permute-start | bytes 786440 | tf_op jit(solution)/shard_map/ppermute | solution.py:213
  4.8 12.5 %collective-permute-start.3 = (bf16[256,512]{1,0:T(8,128)(2,1)}, bf16[256,512]{1,0:T(8,128)(2,1)S(1)}, u32[]{:S(2)}, u32[]{:S(2)}) collective-permute-start(bf16[256,512]{1,0:T(8,128)(2,1)} %rest_1_.3), channel_id=1, source_target_pairs={{0,4},{4,8},{8,12},{12,16},{16,20},{20,24},{24,28},{28,0},{1,5},{5... | collective-permute-start | bytes 786440 | tf_op jit(solution)/shard_map/ppermute | solution.py:213
  8.0 23.4 %collective-permute-start = (bf16[256,512]{1,0:T(8,128)(2,1)}, bf16[256,512]{1,0:T(8,128)(2,1)S(1)}, u32[]{:S(2)}, u32[]{:S(2)}) collective-permute-start(bf16[256,512]{1,0:T(8,128)(2,1)} %rest_0_.3), channel_id=1, source_target_pairs={{0,1},{1,0},{2,3},{3,2},{4,5},{5,4},{6,7},{7,6},{8,9},{9,8},{10,11... | collective-permute-start | bytes 786440 | tf_op jit(solution)/shard_map/ppermute | solution.py:208
  13.4 21.5 %collective-permute-start.1 = (bf16[256,512]{1,0:T(8,128)(2,1)}, bf16[256,512]{1,0:T(8,128)(2,1)S(1)}, u32[]{:S(2)}, u32[]{:S(2)}) collective-permute-start(bf16[256,512]{1,0:T(8,128)(2,1)} %rest_1_.3), channel_id=1, source_target_pairs={{0,1},{1,0},{2,3},{3,2},{4,5},{5,4},{6,7},{7,6},{8,9},{9,8},{10,11... | collective-permute-start | bytes 786440 | tf_op jit(solution)/shard_map/ppermute | solution.py:208
  15.4 21.5 %collective-permute-start.6 = (bf16[256,512]{1,0:T(8,128)(2,1)S(1)}, bf16[256,512]{1,0:T(8,128)(2,1)S(1)}, u32[]{:S(2)}, u32[]{:S(2)}) collective-permute-start(bf16[256,512]{1,0:T(8,128)(2,1)S(1)} %collective-permute-done.2.rest_4_), channel_id=1, source_target_pairs={{0,4},{4,8},{8,12},{12,16},{16,20},{20,24},{24,28},{28,0},{1,5},{5... | collective-permute-start | bytes 786440 | tf_op jit(solution)/shard_map/ppermute | solution.py:213
  17.3 22.0 %collective-permute-start.7 = (bf16[256,512]{1,0:T(8,128)(2,1)S(1)}, bf16[256,512]{1,0:T(8,128)(2,1)S(1)}, u32[]{:S(2)}, u32[]{:S(2)}) collective-permute-start(bf16[256,512]{1,0:T(8,128)(2,1)S(1)} %collective-permute-done.3.rest_5_), channel_id=1, source_target_pairs={{0,4},{4,8},{8,12},{12,16},{16,20},{20,24},{24,28},{28,0},{1,5},{5... | collective-permute-start | bytes 786440 | tf_op jit(solution)/shard_map/ppermute | solution.py:213
  20.8 20.6 %collective-permute-start.10 = (bf16[256,512]{1,0:T(8,128)(2,1)}, bf16[256,512]{1,0:T(8,128)(2,1)S(1)}, u32[]{:S(2)}, u32[]{:S(2)}) collective-permute-start(bf16[256,512]{1,0:T(8,128)(2,1)} %q_ref.1), channel_id=1, source_target_pairs={{0,2},{2,0},{1,3},{3,1},{4,6},{6,4},{5,7},{7,5},{8,10},{10,8},{9,1... | collective-permute-start | bytes 786440 | tf_op jit(solution)/shard_map/ppermute | solution.py:208
  31.4 9.9 %collective-permute-start.4 = (bf16[256,512]{1,0:T(8,128)(2,1)S(1)}, bf16[256,512]{1,0:T(8,128)(2,1)S(1)}, u32[]{:S(2)}, u32[]{:S(2)}) collective-permute-start(bf16[256,512]{1,0:T(8,128)(2,1)S(1)} %collective-permute-done.2.rest_4_), channel_id=1, source_target_pairs={{0,1},{1,0},{2,3},{3,2},{4,5},{5,4},{6,7},{7,6},{8,9},{9,8},{10,11... | collective-permute-start | bytes 786440 | tf_op jit(solution)/shard_map/ppermute | solution.py:208
  34.9 6.4 %collective-permute-start.5 = (bf16[256,512]{1,0:T(8,128)(2,1)S(1)}, bf16[256,512]{1,0:T(8,128)(2,1)S(1)}, u32[]{:S(2)}, u32[]{:S(2)}) collective-permute-start(bf16[256,512]{1,0:T(8,128)(2,1)S(1)} %collective-permute-done.3.rest_5_), channel_id=1, source_target_pairs={{0,1},{1,0},{2,3},{3,2},{4,5},{5,4},{6,7},{7,6},{8,9},{9,8},{10,11... | collective-permute-start | bytes 786440 | tf_op jit(solution)/shard_map/ppermute | solution.py:208
  36.9 4.5 %collective-permute-start.8 = (bf16[256,512]{1,0:T(8,128)(2,1)S(1)}, bf16[256,512]{1,0:T(8,128)(2,1)S(1)}, u32[]{:S(2)}, u32[]{:S(2)}) collective-permute-start(bf16[256,512]{1,0:T(8,128)(2,1)S(1)} %collective-permute-done.6.rest_8_), channel_id=1, source_target_pairs={{0,1},{1,0},{2,3},{3,2},{4,5},{5,4},{6,7},{7,6},{8,9},{9,8},{10,11... | collective-permute-start | bytes 786440 | tf_op jit(solution)/shard_map/ppermute | solution.py:208
  39.3 3.4 %collective-permute-start.9 = (bf16[256,512]{1,0:T(8,128)(2,1)S(1)}, bf16[256,512]{1,0:T(8,128)(2,1)S(1)}, u32[]{:S(2)}, u32[]{:S(2)}) collective-permute-start(bf16[256,512]{1,0:T(8,128)(2,1)S(1)} %collective-permute-done.7.rest_9_), channel_id=1, source_target_pairs={{0,1},{1,0},{2,3},{3,2},{4,5},{5,4},{6,7},{7,6},{8,9},{9,8},{10,11... | collective-permute-start | bytes 786440 | tf_op jit(solution)/shard_map/ppermute | solution.py:208
  45.3 3.3 %copy-start.5 = (bf16[256,512]{1,0:T(8,128)(2,1)S(1)}, bf16[256,512]{1,0:T(8,128)(2,1)}, u32[]{:S(2)}) copy-start(bf16[256,512]{1,0:T(8,128)(2,1)} %rest_1_.3) | copy-start | bytes 786436
  45.3 3.3 %copy-start.6 = (bf16[256,512]{1,0:T(8,128)(2,1)S(1)}, bf16[256,512]{1,0:T(8,128)(2,1)}, u32[]{:S(2)}) copy-start(bf16[256,512]{1,0:T(8,128)(2,1)} %q_ref.1) | copy-start | bytes 786436
  46.4 11.4 %copy-start.1 = (bf16[512,2048]{1,0:T(8,128)(2,1)S(1)}, bf16[512,2048]{1,0:T(8,128)(2,1)}, u32[]{:S(2)}) copy-start(bf16[512,2048]{1,0:T(8,128)(2,1)} %w_ref.1) | copy-start | bytes 6291460
  46.5 11.3 %collective-permute-start.11 = (bf16[528,256]{1,0:T(8,128)(2,1)S(1)}, bf16[528,256]{1,0:T(8,128)(2,1)S(1)}, u32[]{:S(2)}, u32[]{:S(2)}) collective-permute-start(bf16[528,256]{1,0:T(8,128)(2,1)S(1)} %attend_across.1), channel_id=1, source_target_pairs={{0,2},{2,0},{1,3},{3,1},{4,6},{6,4},{5,7},{7,5},{8,10},{10,8},{9,1... | collective-permute-start | bytes 811016 | tf_op jit(solution)/shard_map/ppermute | solution.py:208
  58.8 31.1 %copy-start.10 = (f32[256]{0:T(256)S(1)}, f32[256]{0:T(256)}, u32[]{:S(2)}) copy-start(f32[256]{0:T(256)} %param.19) | copy-start | bytes 3076
  73.9 22.8 %copy-start.9 = (bf16[2048,128]{1,0:T(8,128)(2,1)S(1)}, bf16[2048,128]{1,0:T(8,128)(2,1)}, u32[]{:S(2)}) copy-start(bf16[2048,128]{1,0:T(8,128)(2,1)} %param.16) | copy-start | bytes 1572868
  74.8 20.7 %all-to-all-start.1 = ((bf16[4,16,2048]{2,1,0:T(8,128)(2,1)}), bf16[4,16,2048]{2,1,0:T(8,128)(2,1)S(1)}, u32[]{:S(2)}, u32[]{:S(2)}) async-start(bf16[4,16,2048]{2,1,0:T(8,128)(2,1)} %bitcast.6), calls=%async_computation.1 | async-start | bytes 524288 | tf_op jit(solution)/shard_map/all_to_all | solution.py:217
  98.6 9.0 %copy-start.8 = (bf16[256,512]{1,0:T(8,128)(2,1)S(1)}, bf16[256,512]{1,0:T(8,128)(2,1)}, u32[]{:S(2)}) copy-start(bf16[256,512]{1,0:T(8,128)(2,1)} %get-tuple-element.6) | copy-start | bytes 786436
  100.0 20.2 %all-to-all-start.2 = ((bf16[16,16,512]{2,1,0:T(8,128)(2,1)}), bf16[16,16,512]{2,1,0:T(8,128)(2,1)S(1)}, u32[]{:S(2)}, u32[]{:S(2)}) async-start(bf16[16,16,512]{2,1,0:T(8,128)(2,1)} %all_to_all.33), calls=%async_computation.2 | async-start | bytes 524288 | tf_op jit(solution)/shard_map/all_to_all | solution.py:217
  107.6 23.3 %collective-permute-start.12 = (bf16[256,512]{1,0:T(8,128)(2,1)S(1)}, bf16[256,512]{1,0:T(8,128)(2,1)S(1)}, u32[]{:S(2)}, u32[]{:S(2)}) collective-permute-start(bf16[256,512]{1,0:T(8,128)(2,1)S(1)} %copy-done.8), channel_id=1, source_target_pairs={{0,2},{2,0},{1,3},{3,1},{4,6},{6,4},{5,7},{7,5},{8,10},{10,8},{9,1... | collective-permute-start | bytes 786440 | tf_op jit(solution)/shard_map/ppermute | solution.py:208
  121.2 18.0 %all-to-all-start.3 = ((bf16[4,256,512]{2,1,0:T(8,128)(2,1)}), bf16[4,256,512]{2,1,0:T(8,128)(2,1)S(1)}, u32[]{:S(2)}, u32[]{:S(2)}) async-start(bf16[4,256,512]{2,1,0:T(8,128)(2,1)} %broadcast_in_dim.10), calls=%async_computation.3 | async-start | bytes 2097152 | tf_op jit(solution)/shard_map/all_to_all | solution.py:217
  131.0 4.1 %collective-permute-start.13 = (bf16[2,256,512]{2,1,0:T(8,128)(2,1)S(1)}, bf16[2,256,512]{2,1,0:T(8,128)(2,1)S(1)}, u32[]{:S(2)}, u32[]{:S(2)}) collective-permute-start(bf16[2,256,512]{2,1,0:T(8,128)(2,1)S(1)} %pad_maximum_fusion.mine_ref), channel_id=1, source_target_pairs={{0,1},{1,0},{2,3},{3,2},{4,5},{5,4},{6,7},{7,6},{8,9},{9,8},{10,11... | collective-permute-start | bytes 1572872 | tf_op jit(solution)/shard_map/ppermute | solution.py:208
  (4 other events, 5.9 us)

commit v4 on v3

--- a/solution.py
+++ b/solution.py
@@ -175,33 +175,117 @@
     )(values, levels, other, w_first)
 
 
-def head_rows(hidden_sum, noise_draws, w_noise, w_out, target, loss_weights):
-    count, samples, depth = noise_draws.shape
-    lift = jnp.dot(
-        noise_draws.reshape(count * samples, depth), w_noise, preferred_element_type=jnp.float32
-    )
-    pre = hidden_sum[:, None, :] + lift.reshape(count, samples, -1)
-    act = jax.nn.silu(pre).astype(jnp.bfloat16)
-    latent = jnp.dot(act.reshape(count * samples, -1), w_out, preferred_element_type=jnp.float32)
-    latent = latent.reshape(count, samples, -1)
-    width = latent.shape[2]
-    apart = latent[:, :, None, :] - latent[:, None, :, :]
-    pair = jnp.sqrt(jnp.mean(apart * apart, axis=3) + EPS)
-    others = 1.0 - jnp.eye(samples, dtype=jnp.float32)
-    miss = latent - target.astype(jnp.float32)[:, None, :]
-    far = jnp.sqrt(jnp.mean(miss * miss, axis=2) + EPS)
+def head_kernel(parts_ref, lift_ref, w_ref, target_ref, weight_ref, losses_ref, units_ref, pre_ref, grad_ref, n_y):
+    n_zl, share, width = parts_ref.shape
+    count, latents = w_ref.shape[0], w_ref.shape[1]
+    samples = lift_ref.shape[0] // share
+    step = 512
+    latent = jnp.zeros((share * samples, latents), jnp.float32)
+    for at in range(0, width, step):
+        cols = slice(at, at + step)
+        hidden = parts_ref[0, :, cols].astype(jnp.float32)
+        for z in range(1, n_zl):
+            hidden = hidden + parts_ref[z, :, cols].astype(jnp.float32)
+        lift = lift_ref[:, cols].reshape(share, samples, step)
+        pre = (hidden[:, None, :] + lift).reshape(share * samples, step)
+        pre_ref[:, cols] = pre
+        act = (pre * jax.nn.sigmoid(pre)).astype(jnp.bfloat16)
+        latent = latent + jnp.dot(act, w_ref[cols, :], preferred_element_type=jnp.float32)
+    latent = latent.reshape(share, samples, latents)
     spread = samples * (samples - 1.0)
-    losses = 2.0 / samples * jnp.sum(far, axis=1) - jnp.sum(pair * others, axis=(1, 2)) / spread
-    toward = 2.0 / samples * miss / (width * far[:, :, None])
-    repel = 2.0 / spread * jnp.sum((others[None] / (width * pair))[:, :, :, None] * apart, axis=2)
-    latent_grad = (loss_weights[:, None, None] * (toward - repel)).astype(jnp.bfloat16)
-    act_grad = jnp.dot(
-        latent_grad.reshape(count * samples, width), w_out.T, preferred_element_type=jnp.float32
-    )
-    act_grad = act_grad.reshape(count, samples, -1)
-    sigma = jax.nn.sigmoid(pre)
-    pre_grad = act_grad * sigma * (1.0 + pre * (1.0 - sigma))
-    return (losses, jnp.sum(pre_grad, axis=1).astype(jnp.bfloat16))
+    pairs = jnp.zeros((share, samples, 1), jnp.float32)
+    repel = jnp.zeros_like(latent)
+    for by in range(1, samples):
+        apart = latent - pltpu.roll(latent, by, 1)
+        pair = jnp.sqrt(jnp.mean(apart * apart, axis=2, keepdims=True) + EPS)
+        pairs = pairs + pair
+        repel = repel + apart * (1.0 / (latents * pair))
+    miss = latent - target_ref[...].astype(jnp.float32)[:, None, :]
+    far = jnp.sqrt(jnp.mean(miss * miss, axis=2, keepdims=True) + EPS)
+    losses = jnp.sum(2.0 / samples * far - pairs / spread, axis=1)
+    losses_ref[...] = jnp.broadcast_to(losses, losses_ref.shape)
+    toward = 2.0 / samples * miss / (latents * far)
+    grad = weight_ref[...][:, None, :] * (toward - 2.0 / spread * repel)
+    grad = grad.reshape(share * samples, latents).astype(jnp.bfloat16)
+    for at in range(0, width, step):
+        cols = slice(at, at + step)
+        act_grad = lax.dot_general(
+            grad, w_ref[cols, :], (((1,), (1,)), ((), ())), preferred_element_type=jnp.float32
+        )
+        pre = pre_ref[:, cols]
+        sigma = jax.nn.sigmoid(pre)
+        pre_grad = act_grad * sigma * (1.0 + pre * (1.0 - sigma))
+        grad_ref[:, cols] = jnp.sum(pre_grad.reshape(share, samples, step), axis=1)
+    low = lax.broadcasted_iota(jnp.int32, (share, HD), 1) < HD // 2
+    for z_hi in range(2):
+        for y in range(0, n_y, 2):
+            first = grad_ref[:, pl.ds((2 * y + z_hi) * HD, HD)]
+            second = grad_ref[:, pl.ds((2 * y + 2 + z_hi) * HD, HD)]
+            for core in range(2):
+                if core == 0:
+                    both = jnp.where(low, first, pltpu.roll(second, HD // 2, 1))
+                else:
+                    both = jnp.where(low, pltpu.roll(first, HD // 2, 1), second)
+                both = both.astype(jnp.bfloat16)
+                for z in range(n_zl):
+                    row = ((z_hi * n_zl + z) * 2 + core) * share
+                    units_ref[row : row + share, y * HD // 2 : y * HD // 2 + HD] = both
+
+
+def head(parts, lift, w_out, target, weights, n_y):
+    n_zl, share, width = parts.shape
+    vmem = pl.BlockSpec(memory_space=pltpu.VMEM)
+    return pl.pallas_call(
+        functools.partial(head_kernel, n_y=n_y),
+        out_shape=(
+            jax.ShapeDtypeStruct((share, HD), jnp.float32),
+            jax.ShapeDtypeStruct((4 * n_zl * share, width // 4), jnp.bfloat16),
+        ),
+        in_specs=[vmem] * 5,
+        out_specs=(vmem, vmem),
+        scratch_shapes=[
+            pltpu.VMEM((lift.shape[0], width), jnp.float32),
+            pltpu.VMEM((share, width), jnp.float32),
+        ],
+        compiler_params=pltpu.CompilerParams(vmem_limit_bytes=16 * 1024 * 1024),
+        name="head",
+    )(parts, lift, w_out, target, weights)
+
+
+def fold_kernel(parts_ref, out_ref):
+    total = parts_ref[0].astype(jnp.float32)
+    for i in range(1, parts_ref.shape[0]):
+        total = total + parts_ref[i].astype(jnp.float32)
+    out_ref[...] = total.astype(jnp.bfloat16)
+
+
+def fold(parts):
+    vmem = pl.BlockSpec(memory_space=pltpu.VMEM)
+    return pl.pallas_call(
+        fold_kernel,
+        out_shape=jax.ShapeDtypeStruct(parts.shape[1:], jnp.bfloat16),
+        in_specs=[vmem],
+        out_specs=vmem,
+        compiler_params=pltpu.CompilerParams(vmem_limit_bytes=16 * 1024 * 1024),
+        name="fold",
+    )(parts)
+
+
+def repeat_kernel(one_ref, out_ref):
+    for i in range(out_ref.shape[0]):
+        out_ref[i] = one_ref[...]
+
+
+def repeat(one, times):
+    vmem = pl.BlockSpec(memory_space=pltpu.VMEM)
+    return pl.pallas_call(
+        repeat_kernel,
+        out_shape=jax.ShapeDtypeStruct((times,) + one.shape, one.dtype),
+        in_specs=[vmem],
+        out_specs=vmem,
+        compiler_params=pltpu.CompilerParams(vmem_limit_bytes=16 * 1024 * 1024),
+        name="repeat",
+    )(one)
 
 
 def swap(array, axis):
@@ -296,27 +380,23 @@
 
     over_z = swap(attended, "z_hi")
     partial = exchange(partial, "x").reshape(n_x, n_zl * share, width)
-    partial = jnp.sum(partial.astype(jnp.float32), axis=0).astype(jnp.bfloat16)
-    partial = exchange(partial, "z_lo").reshape(n_zl, share, width)
-    hidden_sum = jnp.sum(partial.astype(jnp.float32), axis=0)
+    partial = exchange(fold(partial), "z_lo").reshape(n_zl, share, width)
 
     here = lax.axis_index(("z_lo", "x")) * share
-    losses_here, grad_here = head_rows(
-        hidden_sum,
-        lax.dynamic_slice_in_dim(noise_draws, here, share, 0),
-        w_noise,
-        w_out,
-        lax.dynamic_slice_in_dim(target, here, share, 0),
-        lax.dynamic_slice_in_dim(loss_weights, here, share, 0),
+    noise = lax.dynamic_slice_in_dim(noise_draws, here, share, 0).reshape(-1, noise_draws.shape[2])
+    lift = jnp.dot(noise, w_noise, preferred_element_type=jnp.float32)
+    weights = lax.dynamic_slice_in_dim(loss_weights, here, share, 0)
+    weights = jnp.broadcast_to(weights[:, None], (share, HD))
+    part = width // (n_y * n_zh * n_c)
+    losses_here, units = head(
+        partial, lift, w_out, lax.dynamic_slice_in_dim(target, here, share, 0), weights, n_y
     )
-    part = width // (n_y * n_zh * n_c)
-    units = grad_here.reshape(share, n_y, n_zh, n_c, part).transpose(2, 3, 0, 1, 4)
-    units = jnp.broadcast_to(units[:, None], (n_zh, n_zl, n_c, share, n_y, part))
-    units = units.reshape(n_zh * n_zl * n_c * share, n_y * part)
+    losses_here = losses_here[:, 0]
     units = exchange(units, ("z_hi", "z_lo", "core"))
-    units = jnp.broadcast_to(units[None], (n_x,) + units.shape).reshape(-1, n_y * part)
+    units = repeat(units, n_x).reshape(-1, n_y * part)
     mine = jnp.stack((attended, over_z))
     other = swap(mine, "core")
+    units, other = lax.optimization_barrier((units, other))
     units = exchange(units, "x")
     place = jnp.stack([lax.axis_index(name) for name in ("z_hi", "core")]).astype(jnp.int32)
     carried = contract(place, units, mine, other, n_x, n_zl)

time: 171 us -> 167 us (0.977)
  starting transfers between devices: 78.7 us -> 71.9 us
  Pallas kernels: 7.41 us -> 11.6 us
  other arithmetic: 3.95 us -> 0.99 us
  waiting for transfers between devices: 27.5 us -> 30 us
  blocking collectives: 44.1 us -> 45.9 us
    all_to_all x3, waiting for transfers between devices: 14 us -> 23.5 us  [exchange(): return lax.all_to_all(array, axis, 0, 0, tiled=True)]
    ppermute x10, waiting for transfers between devices: 13.4 us -> 6.49 us  [swap(): return lax.ppermute(array, axis, [(0, 1), (1, 0)])]
    ppermute x10, starting transfers between devices: 39.7 us -> 36 us  [swap(): return lax.ppermute(array, axis, [(0, 1), (1, 0)])]
    pallas_call x0 -> x3, Pallas kernels: none -> 3.28 us  [the longest x1 1.35 us: head(): pl.pallas_call(functools.partial(head_kernel, n_y=n_y), out_shape=(jax.Sh...]
    all_to_all x3, starting transfers between devices: 26.2 us -> 23.1 us  [exchange(): return lax.all_to_all(array, axis, 0, 0, tiled=True)]
    all_to_all x2, blocking collectives: 44.1 us -> 45.9 us  [exchange(): return lax.all_to_all(array, axis, 0, 0, tiled=True)]
    reduce_sum x6 -> x0, other arithmetic: 1.72 us -> none  [the longest x1 0.91 us: shards(): partial = jnp.sum(partial.astype(jnp.float32), axis=0).astype(jnp.bfloat16)]
  transfers between devices with their start and end apart: 17 -> 17, of which waited for: 7 -> 4; matrix products, arithmetic and copies ran while one was open for 2% -> 2% of each run, Pallas kernels for 2% -> 4%
where the time goes in v4:
time: 167 us; the launch traced here: 166 us
  starting transfers between devices  71.9 us (43%)
  blocking collectives  45.9 us (27%)
  waiting for transfers between devices  30 us (18%)
  Pallas kernels  11.6 us (7%)
  local copies, waits for them, and re-layouts  4.06 us (2%)
    all_to_all x2, blocking collectives, exchange(): return lax.all_to_all(array, axis, 0, 0, tiled=True)  45.9 us
    ppermute x10, starting transfers between devices, swap(): return lax.ppermute(array, axis, [(0, 1), (1, 0)])  36 us
    all_to_all x3, waiting for transfers between devices, exchange(): return lax.all_to_all(array, axis, 0, 0, tiled=True)  23.5 us
    all_to_all x3, starting transfers between devices, exchange(): return lax.all_to_all(array, axis, 0, 0, tiled=True)  23.1 us
    ppermute x4, starting transfers between devices, shift(): lax.ppermute(array, axis, [(i, (i + 1) % length) for i in range(length)])  12.7 us
    ppermute x10, waiting for transfers between devices, swap(): return lax.ppermute(array, axis, [(0, 1), (1, 0)])  6.49 us
    pallas_call x2, Pallas kernels, attend(): pl.pallas_call(functools.partial(attend_kernel, final=final), out_shape=o...  5.16 us
  transfers between devices with their start and end apart: 17, of which 4 were waited for; matrix products, arithmetic and copies ran while one was open for 2% of the time, Pallas kernels for 4%

profile of v4, /device:TPU:1, one launch (start us, length us, event | category | flops | bytes accessed | tf_op | source)
XLA Modules:
  0.0 166.3 jit_solution(17016216828478015642)
XLA Ops:
  0.6 4.2 %collective-permute-start.2 = (bf16[256,512]{1,0:T(8,128)(2,1)}, bf16[256,512]{1,0:T(8,128)(2,1)S(1)}, u32[]{:S(2)}, u32[]{:S(2)}) collective-permute-start(bf16[256,512]{1,0:T(8,128)(2,1)} %rest_0_.3), channel_id=1, source_target_pairs={{0,4},{4,8},{8,12},{12,16},{16,20},{20,24},{24,28},{28,0},{1,5},{5... | collective-permute-start | bytes 786440 | tf_op jit(solution)/shard_map/ppermute | solution.py:297
  4.8 3.2 %collective-permute-start.3 = (bf16[256,512]{1,0:T(8,128)(2,1)}, bf16[256,512]{1,0:T(8,128)(2,1)S(1)}, u32[]{:S(2)}, u32[]{:S(2)}) collective-permute-start(bf16[256,512]{1,0:T(8,128)(2,1)} %rest_1_.3), channel_id=1, source_target_pairs={{0,4},{4,8},{8,12},{12,16},{16,20},{20,24},{24,28},{28,0},{1,5},{5... | collective-permute-start | bytes 786440 | tf_op jit(solution)/shard_map/ppermute | solution.py:297
  8.0 5.4 %collective-permute-start = (bf16[256,512]{1,0:T(8,128)(2,1)}, bf16[256,512]{1,0:T(8,128)(2,1)S(1)}, u32[]{:S(2)}, u32[]{:S(2)}) collective-permute-start(bf16[256,512]{1,0:T(8,128)(2,1)} %rest_0_.3), channel_id=1, source_target_pairs={{0,1},{1,0},{2,3},{3,2},{4,5},{5,4},{6,7},{7,6},{8,9},{9,8},{10,11... | collective-permute-start | bytes 786440 | tf_op jit(solution)/shard_map/ppermute | solution.py:292
  13.4 1.9 %collective-permute-start.1 = (bf16[256,512]{1,0:T(8,128)(2,1)}, bf16[256,512]{1,0:T(8,128)(2,1)S(1)}, u32[]{:S(2)}, u32[]{:S(2)}) collective-permute-start(bf16[256,512]{1,0:T(8,128)(2,1)} %rest_1_.3), channel_id=1, source_target_pairs={{0,1},{1,0},{2,3},{3,2},{4,5},{5,4},{6,7},{7,6},{8,9},{9,8},{10,11... | collective-permute-start | bytes 786440 | tf_op jit(solution)/shard_map/ppermute | solution.py:292
  15.4 1.9 %collective-permute-start.6 = (bf16[256,512]{1,0:T(8,128)(2,1)S(1)}, bf16[256,512]{1,0:T(8,128)(2,1)S(1)}, u32[]{:S(2)}, u32[]{:S(2)}) collective-permute-start(bf16[256,512]{1,0:T(8,128)(2,1)S(1)} %collective-permute-done.2.rest_4_), channel_id=1, source_target_pairs={{0,4},{4,8},{8,12},{12,16},{16,20},{20,24},{24,28},{28,0},{1,5},{5... | collective-permute-start | bytes 786440 | tf_op jit(solution)/shard_map/ppermute | solution.py:297
  17.3 3.5 %collective-permute-start.7 = (bf16[256,512]{1,0:T(8,128)(2,1)S(1)}, bf16[256,512]{1,0:T(8,128)(2,1)S(1)}, u32[]{:S(2)}, u32[]{:S(2)}) collective-permute-start(bf16[256,512]{1,0:T(8,128)(2,1)S(1)} %collective-permute-done.3.rest_5_), channel_id=1, source_target_pairs={{0,4},{4,8},{8,12},{12,16},{16,20},{20,24},{24,28},{28,0},{1,5},{5... | collective-permute-start | bytes 786440 | tf_op jit(solution)/shard_map/ppermute | solution.py:297
  20.8 10.6 %collective-permute-start.10 = (bf16[256,512]{1,0:T(8,128)(2,1)}, bf16[256,512]{1,0:T(8,128)(2,1)S(1)}, u32[]{:S(2)}, u32[]{:S(2)}) collective-permute-start(bf16[256,512]{1,0:T(8,128)(2,1)} %q_ref.1), channel_id=1, source_target_pairs={{0,2},{2,0},{1,3},{3,1},{4,6},{6,4},{5,7},{7,5},{8,10},{10,8},{9,1... | collective-permute-start | bytes 786440 | tf_op jit(solution)/shard_map/ppermute | solution.py:292
  31.4 3.5 %collective-permute-start.4 = (bf16[256,512]{1,0:T(8,128)(2,1)S(1)}, bf16[256,512]{1,0:T(8,128)(2,1)S(1)}, u32[]{:S(2)}, u32[]{:S(2)}) collective-permute-start(bf16[256,512]{1,0:T(8,128)(2,1)S(1)} %collective-permute-done.2.rest_4_), channel_id=1, source_target_pairs={{0,1},{1,0},{2,3},{3,2},{4,5},{5,4},{6,7},{7,6},{8,9},{9,8},{10,11... | collective-permute-start | bytes 786440 | tf_op jit(solution)/shard_map/ppermute | solution.py:292
  34.9 1.9 %collective-permute-start.5 = (bf16[256,512]{1,0:T(8,128)(2,1)S(1)}, bf16[256,512]{1,0:T(8,128)(2,1)S(1)}, u32[]{:S(2)}, u32[]{:S(2)}) collective-permute-start(bf16[256,512]{1,0:T(8,128)(2,1)S(1)} %collective-permute-done.3.rest_5_), channel_id=1, source_target_pairs={{0,1},{1,0},{2,3},{3,2},{4,5},{5,4},{6,7},{7,6},{8,9},{9,8},{10,11... | collective-permute-start | bytes 786440 | tf_op jit(solution)/shard_map/ppermute | solution.py:292
  36.9 2.4 %collective-permute-start.8 = (bf16[256,512]{1,0:T(8,128)(2,1)S(1)}, bf16[256,512]{1,0:T(8,128)(2,1)S(1)}, u32[]{:S(2)}, u32[]{:S(2)}) collective-permute-start(bf16[256,512]{1,0:T(8,128)(2,1)S(1)} %collective-permute-done.6.rest_8_), channel_id=1, source_target_pairs={{0,1},{1,0},{2,3},{3,2},{4,5},{5,4},{6,7},{7,6},{8,9},{9,8},{10,11... | collective-permute-start | bytes 786440 | tf_op jit(solution)/shard_map/ppermute | solution.py:292
  39.3 1.9 %collective-permute-start.9 = (bf16[256,512]{1,0:T(8,128)(2,1)S(1)}, bf16[256,512]{1,0:T(8,128)(2,1)S(1)}, u32[]{:S(2)}, u32[]{:S(2)}) collective-permute-start(bf16[256,512]{1,0:T(8,128)(2,1)S(1)} %collective-permute-done.7.rest_9_), channel_id=1, source_target_pairs={{0,1},{1,0},{2,3},{3,2},{4,5},{5,4},{6,7},{7,6},{8,9},{9,8},{10,11... | collective-permute-start | bytes 786440 | tf_op jit(solution)/shard_map/ppermute | solution.py:292
  46.5 2.1 %collective-permute-start.11 = (bf16[528,256]{1,0:T(8,128)(2,1)S(1)}, bf16[528,256]{1,0:T(8,128)(2,1)S(1)}, u32[]{:S(2)}, u32[]{:S(2)}) collective-permute-start(bf16[528,256]{1,0:T(8,128)(2,1)S(1)} %attend_across.1), channel_id=1, source_target_pairs={{0,2},{2,0},{1,3},{3,1},{4,6},{6,4},{5,7},{7,5},{8,10},{10,8},{9,1... | collective-permute-start | bytes 811016 | tf_op jit(solution)/shard_map/ppermute | solution.py:292
  48.6 4.0 %attend_own.1 = (f32[512,256]{1,0:T(8,128)S(1)}, f32[8,256]{1,0:T(8,128)S(1)}) custom-call(s32[64]{0:T(128)S(1)} %copy-done.8, s32[3]{0:T(128)S(1)} %add_add_fusion.where, bf16[256,512]{1,0:T(8,128)(2,1)S(1)} %copy-done.7, bf16[256,512]{1,0:T(8,128)(2,1)S(1)} %copy-done.3, bf16[256,512]{1,0:T(8,128)(2,1)S(1)} %copy-done.5, ...), custom_call_target="tpu_custom_call" | custom-call | flops 671088640 | bytes 3145728 | tf_op jit(solution)/shard_map/attend_own/pallas_call | solution.py:119
  52.7 5.1 %collective-permute-done.11.other_ref = bf16[528,256]{1,0:T(8,128)(2,1)S(1)} collective-permute-done((bf16[528,256]{1,0:T(8,128)(2,1)S(1)}, bf16[528,256]{1,0:T(8,128)(2,1)S(1)}, u32[]{:S(2)}, u32[]{:S(2)}) %collective-permute-start.11) | collective-permute-done | bytes 270368 | tf_op jit(solution)/shard_map/ppermute | solution.py:292
  57.8 1.8 %join.1 = (bf16[256,512]{1,0:T(8,128)(2,1)}, bf16[256,2048]{1,0:T(8,128)(2,1)}) custom-call(f32[512,256]{1,0:T(8,128)S(1)} %get-tuple-element.13.values_ref, f32[8,256]{1,0:T(8,128)S(1)} %get-tuple-element.14.levels_ref, bf16[528,256]{1,0:T(8,128)(2,1)S(1)} %collective-permute-done.11.other_ref, bf16[512,2048]{1,0:T(8,128)(2,1)S(1)} %copy-done.1), custom_call_target="tpu_custom_call" | custom-call | tf_op jit(solution)/shard_map/join/pallas_call | solution.py:164
  59.7 4.1 %all-to-all-start = ((bf16[4,64,2048]{2,1,0:T(8,128)(2,1)}), bf16[4,64,2048]{2,1,0:T(8,128)(2,1)S(1)}, u32[]{:S(2)}, u32[]{:S(2)}) async-start(bf16[4,64,2048]{2,1,0:T(8,128)(2,1)} %bitcast.5), calls=%async_computation | async-start | bytes 2097152 | tf_op jit(solution)/shard_map/all_to_all | solution.py:301
  63.8 2.3 %collective-permute-start.12 = (bf16[256,512]{1,0:T(8,128)(2,1)S(1)}, bf16[256,512]{1,0:T(8,128)(2,1)S(1)}, u32[]{:S(2)}, u32[]{:S(2)}) collective-permute-start(bf16[256,512]{1,0:T(8,128)(2,1)S(1)} %copy-done.9), channel_id=1, source_target_pairs={{0,2},{2,0},{1,3},{3,1},{4,6},{6,4},{5,7},{7,5},{8,10},{10,8},{9,1... | collective-permute-start | bytes 786440 | tf_op jit(solution)/shard_map/ppermute | solution.py:292
  66.1 8.6 %all-to-all-done.parts_ref = bf16[4,64,2048]{2,1,0:T(8,128)(2,1)S(1)} async-done(((bf16[4,64,2048]{2,1,0:T(8,128)(2,1)}), bf16[4,64,2048]{2,1,0:T(8,128)(2,1)S(1)}, u32[]{:S(2)}, u32[]{:S(2)}) %all-to-all-start) | async-done | bytes 1048608 | tf_op jit(solution)/shard_map/all_to_all | solution.py:301
  75.5 15.5 %all-to-all-start.1 = ((bf16[4,16,2048]{2,1,0:T(8,128)(2,1)}), bf16[4,16,2048]{2,1,0:T(8,128)(2,1)S(1)}, u32[]{:S(2)}, u32[]{:S(2)}) async-start(bf16[4,16,2048]{2,1,0:T(8,128)(2,1)} %bitcast.6), calls=%async_computation.1 | async-start | bytes 524288 | tf_op jit(solution)/shard_map/all_to_all | solution.py:301
  92.1 3.9 %collective-permute-start.13 = (bf16[2,256,512]{2,1,0:T(8,128)(2,1)S(1)}, bf16[2,256,512]{2,1,0:T(8,128)(2,1)S(1)}, u32[]{:S(2)}, u32[]{:S(2)}) collective-permute-start(bf16[2,256,512]{2,1,0:T(8,128)(2,1)S(1)} %pad_maximum_fusion.mine_ref), channel_id=1, source_target_pairs={{0,1},{1,0},{2,3},{3,2},{4,5},{5,4},{6,7},{7,6},{8,9},{9,8},{10,11... | collective-permute-start | bytes 1572872 | tf_op jit(solution)/shard_map/ppermute | solution.py:292
  98.3 18.7 %all_to_all.49 = bf16[16,16,512]{2,1,0:T(8,128)(2,1)S(1)} all-to-all(bf16[16,16,512]{2,1,0:T(8,128)(2,1)S(1)} %bitcast.23), channel_id=1, replica_groups=mesh['z_lo'=4,'x'=4,'y'=8,'z_hi'=2,'core'=2] {'z_hi','z_lo','core'}, dimensions={0} | all-to-all | bytes 524288 | tf_op jit(solution)/shard_map/all_to_all | solution.py:301
  118.1 3.5 %all-to-all-start.3 = ((bf16[4,256,512]{2,1,0:T(8,128)(2,1)}), bf16[4,256,512]{2,1,0:T(8,128)(2,1)S(1)}, u32[]{:S(2)}, u32[]{:S(2)}) async-start(bf16[4,256,512]{2,1,0:T(8,128)(2,1)} %bitcast.13), calls=%async_computation.3 | async-start | bytes 2097152 | tf_op jit(solution)/shard_map/all_to_all | solution.py:301
  122.3 14.9 %all-to-all-done.3 = bf16[4,256,512]{2,1,0:T(8,128)(2,1)S(1)} async-done(((bf16[4,256,512]{2,1,0:T(8,128)(2,1)}), bf16[4,256,512]{2,1,0:T(8,128)(2,1)S(1)}, u32[]{:S(2)}, u32[]{:S(2)}) %all-to-all-start.3) | async-done | bytes 1048608 | tf_op jit(solution)/shard_map/all_to_all | solution.py:301
  138.5 27.1 %all_to_all.50 = bf16[8,64,512]{2,1,0:T(8,128)(2,1)S(1)} all-to-all(bf16[8,64,512]{2,1,0:T(8,128)(2,1)S(1)} %bitcast.21), channel_id=1, replica_groups=mesh['z_lo'=4,'x'=4,'y'=8,'z_hi'=2,'core'=2] {'y'}, dimensions={0} | all-to-all | bytes 1048576 | tf_op jit(solution)/shard_map/all_to_all | solution.py:301
  (51 shorter events, 13.2 us)
Async XLA Ops:
  0.6 90.4 %copy-start = (bf16[128,2048]{1,0:T(8,128)(2,1)S(1)}, bf16[128,2048]{1,0:T(8,128)(2,1)}, u32[]{:S(2)}) copy-start(bf16[128,2048]{1,0:T(8,128)(2,1)} %param.15) | copy-start | bytes 1572868
  0.6 14.7 %collective-permute-start.2 = (bf16[256,512]{1,0:T(8,128)(2,1)}, bf16[256,512]{1,0:T(8,128)(2,1)S(1)}, u32[]{:S(2)}, u32[]{:S(2)}) collective-permute-start(bf16[256,512]{1,0:T(8,128)(2,1)} %rest_0_.3), channel_id=1, source_target_pairs={{0,4},{4,8},{8,12},{12,16},{16,20},{20,24},{24,28},{28,0},{1,5},{5... | collective-permute-start | bytes 786440 | tf_op jit(solution)/shard_map/ppermute | solution.py:297
  4.8 12.5 %collective-permute-start.3 = (bf16[256,512]{1,0:T(8,128)(2,1)}, bf16[256,512]{1,0:T(8,128)(2,1)S(1)}, u32[]{:S(2)}, u32[]{:S(2)}) collective-permute-start(bf16[256,512]{1,0:T(8,128)(2,1)} %rest_1_.3), channel_id=1, source_target_pairs={{0,4},{4,8},{8,12},{12,16},{16,20},{20,24},{24,28},{28,0},{1,5},{5... | collective-permute-start | bytes 786440 | tf_op jit(solution)/shard_map/ppermute | solution.py:297
  8.0 23.4 %collective-permute-start = (bf16[256,512]{1,0:T(8,128)(2,1)}, bf16[256,512]{1,0:T(8,128)(2,1)S(1)}, u32[]{:S(2)}, u32[]{:S(2)}) collective-permute-start(bf16[256,512]{1,0:T(8,128)(2,1)} %rest_0_.3), channel_id=1, source_target_pairs={{0,1},{1,0},{2,3},{3,2},{4,5},{5,4},{6,7},{7,6},{8,9},{9,8},{10,11... | collective-permute-start | bytes 786440 | tf_op jit(solution)/shard_map/ppermute | solution.py:292
  13.4 21.5 %collective-permute-start.1 = (bf16[256,512]{1,0:T(8,128)(2,1)}, bf16[256,512]{1,0:T(8,128)(2,1)S(1)}, u32[]{:S(2)}, u32[]{:S(2)}) collective-permute-start(bf16[256,512]{1,0:T(8,128)(2,1)} %rest_1_.3), channel_id=1, source_target_pairs={{0,1},{1,0},{2,3},{3,2},{4,5},{5,4},{6,7},{7,6},{8,9},{9,8},{10,11... | collective-permute-start | bytes 786440 | tf_op jit(solution)/shard_map/ppermute | solution.py:292
  15.4 21.5 %collective-permute-start.6 = (bf16[256,512]{1,0:T(8,128)(2,1)S(1)}, bf16[256,512]{1,0:T(8,128)(2,1)S(1)}, u32[]{:S(2)}, u32[]{:S(2)}) collective-permute-start(bf16[256,512]{1,0:T(8,128)(2,1)S(1)} %collective-permute-done.2.rest_4_), channel_id=1, source_target_pairs={{0,4},{4,8},{8,12},{12,16},{16,20},{20,24},{24,28},{28,0},{1,5},{5... | collective-permute-start | bytes 786440 | tf_op jit(solution)/shard_map/ppermute | solution.py:297
  17.3 22.0 %collective-permute-start.7 = (bf16[256,512]{1,0:T(8,128)(2,1)S(1)}, bf16[256,512]{1,0:T(8,128)(2,1)S(1)}, u32[]{:S(2)}, u32[]{:S(2)}) collective-permute-start(bf16[256,512]{1,0:T(8,128)(2,1)S(1)} %collective-permute-done.3.rest_5_), channel_id=1, source_target_pairs={{0,4},{4,8},{8,12},{12,16},{16,20},{20,24},{24,28},{28,0},{1,5},{5... | collective-permute-start | bytes 786440 | tf_op jit(solution)/shard_map/ppermute | solution.py:297
  20.8 20.6 %collective-permute-start.10 = (bf16[256,512]{1,0:T(8,128)(2,1)}, bf16[256,512]{1,0:T(8,128)(2,1)S(1)}, u32[]{:S(2)}, u32[]{:S(2)}) collective-permute-start(bf16[256,512]{1,0:T(8,128)(2,1)} %q_ref.1), channel_id=1, source_target_pairs={{0,2},{2,0},{1,3},{3,1},{4,6},{6,4},{5,7},{7,5},{8,10},{10,8},{9,1... | collective-permute-start | bytes 786440 | tf_op jit(solution)/shard_map/ppermute | solution.py:292
  31.4 9.9 %collective-permute-start.4 = (bf16[256,512]{1,0:T(8,128)(2,1)S(1)}, bf16[256,512]{1,0:T(8,128)(2,1)S(1)}, u32[]{:S(2)}, u32[]{:S(2)}) collective-permute-start(bf16[256,512]{1,0:T(8,128)(2,1)S(1)} %collective-permute-done.2.rest_4_), channel_id=1, source_target_pairs={{0,1},{1,0},{2,3},{3,2},{4,5},{5,4},{6,7},{7,6},{8,9},{9,8},{10,11... | collective-permute-start | bytes 786440 | tf_op jit(solution)/shard_map/ppermute | solution.py:292
  34.9 6.4 %collective-permute-start.5 = (bf16[256,512]{1,0:T(8,128)(2,1)S(1)}, bf16[256,512]{1,0:T(8,128)(2,1)S(1)}, u32[]{:S(2)}, u32[]{:S(2)}) collective-permute-start(bf16[256,512]{1,0:T(8,128)(2,1)S(1)} %collective-permute-done.3.rest_5_), channel_id=1, source_target_pairs={{0,1},{1,0},{2,3},{3,2},{4,5},{5,4},{6,7},{7,6},{8,9},{9,8},{10,11... | collective-permute-start | bytes 786440 | tf_op jit(solution)/shard_map/ppermute | solution.py:292
  36.9 4.5 %collective-permute-start.8 = (bf16[256,512]{1,0:T(8,128)(2,1)S(1)}, bf16[256,512]{1,0:T(8,128)(2,1)S(1)}, u32[]{:S(2)}, u32[]{:S(2)}) collective-permute-start(bf16[256,512]{1,0:T(8,128)(2,1)S(1)} %collective-permute-done.6.rest_8_), channel_id=1, source_target_pairs={{0,1},{1,0},{2,3},{3,2},{4,5},{5,4},{6,7},{7,6},{8,9},{9,8},{10,11... | collective-permute-start | bytes 786440 | tf_op jit(solution)/shard_map/ppermute | solution.py:292
  39.3 3.4 %collective-permute-start.9 = (bf16[256,512]{1,0:T(8,128)(2,1)S(1)}, bf16[256,512]{1,0:T(8,128)(2,1)S(1)}, u32[]{:S(2)}, u32[]{:S(2)}) collective-permute-start(bf16[256,512]{1,0:T(8,128)(2,1)S(1)} %collective-permute-done.7.rest_9_), channel_id=1, source_target_pairs={{0,1},{1,0},{2,3},{3,2},{4,5},{5,4},{6,7},{7,6},{8,9},{9,8},{10,11... | collective-permute-start | bytes 786440 | tf_op jit(solution)/shard_map/ppermute | solution.py:292
  45.3 3.3 %copy-start.5 = (bf16[256,512]{1,0:T(8,128)(2,1)S(1)}, bf16[256,512]{1,0:T(8,128)(2,1)}, u32[]{:S(2)}) copy-start(bf16[256,512]{1,0:T(8,128)(2,1)} %rest_1_.3) | copy-start | bytes 786436
  45.3 3.3 %copy-start.7 = (bf16[256,512]{1,0:T(8,128)(2,1)S(1)}, bf16[256,512]{1,0:T(8,128)(2,1)}, u32[]{:S(2)}) copy-start(bf16[256,512]{1,0:T(8,128)(2,1)} %q_ref.1) | copy-start | bytes 786436
  46.4 11.4 %copy-start.1 = (bf16[512,2048]{1,0:T(8,128)(2,1)S(1)}, bf16[512,2048]{1,0:T(8,128)(2,1)}, u32[]{:S(2)}) copy-start(bf16[512,2048]{1,0:T(8,128)(2,1)} %w_ref.2) | copy-start | bytes 6291460
  46.5 11.3 %collective-permute-start.11 = (bf16[528,256]{1,0:T(8,128)(2,1)S(1)}, bf16[528,256]{1,0:T(8,128)(2,1)S(1)}, u32[]{:S(2)}, u32[]{:S(2)}) collective-permute-start(bf16[528,256]{1,0:T(8,128)(2,1)S(1)} %attend_across.1), channel_id=1, source_target_pairs={{0,2},{2,0},{1,3},{3,1},{4,6},{6,4},{5,7},{7,5},{8,10},{10,8},{9,1... | collective-permute-start | bytes 811016 | tf_op jit(solution)/shard_map/ppermute | solution.py:292
  59.6 4.1 %copy-start.9 = (bf16[256,512]{1,0:T(8,128)(2,1)S(1)}, bf16[256,512]{1,0:T(8,128)(2,1)}, u32[]{:S(2)}) copy-start(bf16[256,512]{1,0:T(8,128)(2,1)} %get-tuple-element.10) | copy-start | bytes 786436
  59.7 15.0 %all-to-all-start = ((bf16[4,64,2048]{2,1,0:T(8,128)(2,1)}), bf16[4,64,2048]{2,1,0:T(8,128)(2,1)S(1)}, u32[]{:S(2)}, u32[]{:S(2)}) async-start(bf16[4,64,2048]{2,1,0:T(8,128)(2,1)} %bitcast.5), calls=%async_computation | async-start | bytes 2097152 | tf_op jit(solution)/shard_map/all_to_all | solution.py:301
  63.8 33.0 %copy-start.10 = (f32[256]{0:T(256)S(1)}, f32[256]{0:T(256)}, u32[]{:S(2)}) copy-start(f32[256]{0:T(256)} %param.19) | copy-start | bytes 3076
  63.8 33.1 %copy-start.6 = (bf16[2048,128]{1,0:T(8,128)(2,1)S(1)}, bf16[2048,128]{1,0:T(8,128)(2,1)}, u32[]{:S(2)}) copy-start(bf16[2048,128]{1,0:T(8,128)(2,1)} %w_ref.3) | copy-start | bytes 1572868
  63.8 28.3 %collective-permute-start.12 = (bf16[256,512]{1,0:T(8,128)(2,1)S(1)}, bf16[256,512]{1,0:T(8,128)(2,1)S(1)}, u32[]{:S(2)}, u32[]{:S(2)}) collective-permute-start(bf16[256,512]{1,0:T(8,128)(2,1)S(1)} %copy-done.9), channel_id=1, source_target_pairs={{0,2},{2,0},{1,3},{3,1},{4,6},{6,4},{5,7},{7,5},{8,10},{10,8},{9,1... | collective-permute-start | bytes 786440 | tf_op jit(solution)/shard_map/ppermute | solution.py:292
  75.5 21.3 %all-to-all-start.1 = ((bf16[4,16,2048]{2,1,0:T(8,128)(2,1)}), bf16[4,16,2048]{2,1,0:T(8,128)(2,1)S(1)}, u32[]{:S(2)}, u32[]{:S(2)}) async-start(bf16[4,16,2048]{2,1,0:T(8,128)(2,1)} %bitcast.6), calls=%async_computation.1 | async-start | bytes 524288 | tf_op jit(solution)/shard_map/all_to_all | solution.py:301
  92.1 26.0 %collective-permute-start.13 = (bf16[2,256,512]{2,1,0:T(8,128)(2,1)S(1)}, bf16[2,256,512]{2,1,0:T(8,128)(2,1)S(1)}, u32[]{:S(2)}, u32[]{:S(2)}) collective-permute-start(bf16[2,256,512]{2,1,0:T(8,128)(2,1)S(1)} %pad_maximum_fusion.mine_ref), channel_id=1, source_target_pairs={{0,1},{1,0},{2,3},{3,2},{4,5},{5,4},{6,7},{7,6},{8,9},{9,8},{10,11... | collective-permute-start | bytes 1572872 | tf_op jit(solution)/shard_map/ppermute | solution.py:292
  118.1 19.1 %all-to-all-start.3 = ((bf16[4,256,512]{2,1,0:T(8,128)(2,1)}), bf16[4,256,512]{2,1,0:T(8,128)(2,1)S(1)}, u32[]{:S(2)}, u32[]{:S(2)}) async-start(bf16[4,256,512]{2,1,0:T(8,128)(2,1)} %bitcast.13), calls=%async_computation.3 | async-start | bytes 2097152 | tf_op jit(solution)/shard_map/all_to_all | solution.py:301
  (4 other events, 5.9 us)

commit v5 on v4

--- a/solution.py
+++ b/solution.py
@@ -27,58 +27,67 @@
     query = query_at + lax.broadcasted_iota(jnp.int32, (1, rows), 1)
 
     def pass_end(i, carry):
-        end, start, lowest = carry
+        end, start, lowest, highest = carry
         end = end + lengths[i]
-        return (end, jnp.where(query >= end, end, start), jnp.where(query_at >= end, end, lowest))
+        return (
+            end,
+            jnp.where(query >= end, end, start),
+            jnp.where(query_at >= end, end, lowest),
+            jnp.where(query_at + rows - 1 >= end, end, highest),
+        )
 
     zero = jnp.int32(0)
-    _, start, lowest = lax.fori_loop(
-        0, lengths.shape[0], pass_end, (zero, jnp.zeros_like(query), zero)
+    _, start, lowest, highest = lax.fori_loop(
+        0, lengths.shape[0], pass_end, (zero, jnp.zeros_like(query), zero, zero)
     )
     start_ref[...] = jnp.broadcast_to(start, start_ref.shape)
     top_ref[...] = jnp.full_like(top_ref, FLOOR)
     total_ref[...] = jnp.zeros_like(total_ref)
     acc_ref[...] = jnp.zeros_like(acc_ref)
 
+    def add_tile(k_ref, v_ref, kept):
+        for head in range(heads):
+            cols = slice(head * HD, (head + 1) * HD)
+            scores = lax.dot_general(
+                k_ref[:, cols],
+                q_ref[:, cols],
+                (((1,), (1,)), ((), ())),
+                preferred_element_type=jnp.float32,
+            )
+            scores = scores * scale
+            if kept is not None:
+                scores = jnp.where(kept, scores, MASKED)
+            old = top_ref[head, 0:1, :]
+            top = jnp.maximum(old, jnp.max(scores, axis=0, keepdims=True))
+            raised = jnp.exp2(scores - top).astype(jnp.bfloat16)
+            decay = jnp.exp2(old - top)
+            sums = jnp.dot(jnp.ones((16, rows), jnp.bfloat16), raised, preferred_element_type=jnp.float32)
+            total = total_ref[head, 0:1, :] * decay + sums[0:1, :]
+            product = lax.dot_general(
+                v_ref[:, cols],
+                raised,
+                (((0,), (0,)), ((), ())),
+                preferred_element_type=jnp.float32,
+            )
+            acc_ref[head] = acc_ref[head] * decay + product
+            top_ref[head, 0:1, :] = top
+            total_ref[head, 0:1, :] = total
+
     for i in range(6):
         k_ref, v_ref = kv_refs[2 * i], kv_refs[2 * i + 1]
         key_at = (where[1 + i % 2] - 4 * (i // 2)) * rows
         live = (key_at <= query_at) & (key_at + rows > lowest)
-
-        @pl.when(live)
+        whole = (key_at < query_at) & (key_at >= highest)
+
+        @pl.when(whole)
+        def _(k_ref=k_ref, v_ref=v_ref):
+            add_tile(k_ref, v_ref, None)
+
+        @pl.when(live & jnp.logical_not(whole))
         def _(k_ref=k_ref, v_ref=v_ref, key_at=key_at):
             key = key_at + lax.broadcasted_iota(jnp.int32, (rows, rows), 0)
             at = query_at + lax.broadcasted_iota(jnp.int32, (rows, rows), 1)
-            kept = (key >= start_ref[0:1, :]) & (key <= at)
-
-            def two_heads(pair, carry):
-                for head in (2 * pair, 2 * pair + 1):
-                    cols = pl.ds(pl.multiple_of(head * HD, HD), HD)
-                    scores = lax.dot_general(
-                        k_ref[:, cols],
-                        q_ref[:, cols],
-                        (((1,), (1,)), ((), ())),
-                        preferred_element_type=jnp.float32,
-                    )
-                    scores = jnp.where(kept, scores * scale, MASKED)
-                    old = top_ref[head, 0:1, :]
-                    top = jnp.maximum(old, jnp.max(scores, axis=0, keepdims=True))
-                    raised = jnp.exp2(scores - top)
-                    decay = jnp.exp2(old - top)
-                    total = total_ref[head, 0:1, :] * decay
-                    total = total + jnp.sum(raised, axis=0, keepdims=True)
-                    product = lax.dot_general(
-                        v_ref[:, cols],
-                        raised.astype(jnp.bfloat16),
-                        (((0,), (0,)), ((), ())),
-                        preferred_element_type=jnp.float32,
-                    )
-                    acc_ref[head] = acc_ref[head] * decay + product
-                    top_ref[head] = jnp.broadcast_to(top, (8, rows))
-                    total_ref[head] = jnp.broadcast_to(total, (8, rows))
-                return carry
-
-            lax.fori_loop(0, heads // 2, two_heads, 0)
+            add_tile(k_ref, v_ref, (key >= start_ref[0:1, :]) & (key <= at))
 
     parts = []
     for head in range(heads):

time: 167 us -> 164 us (0.982)
  blocking collectives: 45.9 us -> 41.8 us
  waiting for transfers between devices: 30 us -> 32.7 us
  starting transfers between devices: 71.9 us -> 70.2 us
    all_to_all x2, blocking collectives: 45.9 us -> 41.8 us  [exchange(): return lax.all_to_all(array, axis, 0, 0, tiled=True)]
    ppermute x10, waiting for transfers between devices: 6.49 us -> 9.22 us  [swap(): return lax.ppermute(array, axis, [(0, 1), (1, 0)])]
where the time goes in v5:
time: 164 us; the launch traced here: 163 us
  starting transfers between devices  70.2 us (43%)
  blocking collectives  41.8 us (25%)
  waiting for transfers between devices  32.7 us (20%)
  Pallas kernels  11.7 us (7%)
  local copies, waits for them, and re-layouts  4.06 us (2%)
    all_to_all x2, blocking collectives, exchange(): return lax.all_to_all(array, axis, 0, 0, tiled=True)  41.8 us
    ppermute x10, starting transfers between devices, swap(): return lax.ppermute(array, axis, [(0, 1), (1, 0)])  35.6 us
    all_to_all x3, waiting for transfers between devices, exchange(): return lax.all_to_all(array, axis, 0, 0, tiled=True)  23.5 us
    all_to_all x3, starting transfers between devices, exchange(): return lax.all_to_all(array, axis, 0, 0, tiled=True)  21.8 us
    ppermute x4, starting transfers between devices, shift(): lax.ppermute(array, axis, [(i, (i + 1) % length) for i in range(length)])  12.7 us
    ppermute x10, waiting for transfers between devices, swap(): return lax.ppermute(array, axis, [(0, 1), (1, 0)])  9.22 us
    pallas_call x2, Pallas kernels, attend(): pl.pallas_call(functools.partial(attend_kernel, final=final), out_shape=o...  5.32 us
  transfers between devices with their start and end apart: 17, of which 4 were waited for; matrix products, arithmetic and copies ran while one was open for 2% of the time, Pallas kernels for 4%

profile of v5, /device:TPU:1, one launch (start us, length us, event | category | flops | bytes accessed | tf_op | source)
XLA Modules:
  0.0 163.4 jit_solution(11821152710268238533)
XLA Ops:
  0.6 4.2 %collective-permute-start.2 = (bf16[256,512]{1,0:T(8,128)(2,1)}, bf16[256,512]{1,0:T(8,128)(2,1)S(1)}, u32[]{:S(2)}, u32[]{:S(2)}) collective-permute-start(bf16[256,512]{1,0:T(8,128)(2,1)} %rest_0_.3), channel_id=1, source_target_pairs={{0,4},{4,8},{8,12},{12,16},{16,20},{20,24},{24,28},{28,0},{1,5},{5... | collective-permute-start | bytes 786440 | tf_op jit(solution)/shard_map/ppermute | solution.py:306
  4.8 3.2 %collective-permute-start.3 = (bf16[256,512]{1,0:T(8,128)(2,1)}, bf16[256,512]{1,0:T(8,128)(2,1)S(1)}, u32[]{:S(2)}, u32[]{:S(2)}) collective-permute-start(bf16[256,512]{1,0:T(8,128)(2,1)} %rest_1_.3), channel_id=1, source_target_pairs={{0,4},{4,8},{8,12},{12,16},{16,20},{20,24},{24,28},{28,0},{1,5},{5... | collective-permute-start | bytes 786440 | tf_op jit(solution)/shard_map/ppermute | solution.py:306
  8.0 5.4 %collective-permute-start = (bf16[256,512]{1,0:T(8,128)(2,1)}, bf16[256,512]{1,0:T(8,128)(2,1)S(1)}, u32[]{:S(2)}, u32[]{:S(2)}) collective-permute-start(bf16[256,512]{1,0:T(8,128)(2,1)} %rest_0_.3), channel_id=1, source_target_pairs={{0,1},{1,0},{2,3},{3,2},{4,5},{5,4},{6,7},{7,6},{8,9},{9,8},{10,11... | collective-permute-start | bytes 786440 | tf_op jit(solution)/shard_map/ppermute | solution.py:301
  13.4 1.9 %collective-permute-start.1 = (bf16[256,512]{1,0:T(8,128)(2,1)}, bf16[256,512]{1,0:T(8,128)(2,1)S(1)}, u32[]{:S(2)}, u32[]{:S(2)}) collective-permute-start(bf16[256,512]{1,0:T(8,128)(2,1)} %rest_1_.3), channel_id=1, source_target_pairs={{0,1},{1,0},{2,3},{3,2},{4,5},{5,4},{6,7},{7,6},{8,9},{9,8},{10,11... | collective-permute-start | bytes 786440 | tf_op jit(solution)/shard_map/ppermute | solution.py:301
  15.4 1.9 %collective-permute-start.6 = (bf16[256,512]{1,0:T(8,128)(2,1)S(1)}, bf16[256,512]{1,0:T(8,128)(2,1)S(1)}, u32[]{:S(2)}, u32[]{:S(2)}) collective-permute-start(bf16[256,512]{1,0:T(8,128)(2,1)S(1)} %collective-permute-done.2.rest_4_), channel_id=1, source_target_pairs={{0,4},{4,8},{8,12},{12,16},{16,20},{20,24},{24,28},{28,0},{1,5},{5... | collective-permute-start | bytes 786440 | tf_op jit(solution)/shard_map/ppermute | solution.py:306
  17.3 3.5 %collective-permute-start.7 = (bf16[256,512]{1,0:T(8,128)(2,1)S(1)}, bf16[256,512]{1,0:T(8,128)(2,1)S(1)}, u32[]{:S(2)}, u32[]{:S(2)}) collective-permute-start(bf16[256,512]{1,0:T(8,128)(2,1)S(1)} %collective-permute-done.3.rest_5_), channel_id=1, source_target_pairs={{0,4},{4,8},{8,12},{12,16},{16,20},{20,24},{24,28},{28,0},{1,5},{5... | collective-permute-start | bytes 786440 | tf_op jit(solution)/shard_map/ppermute | solution.py:306
  20.8 10.6 %collective-permute-start.10 = (bf16[256,512]{1,0:T(8,128)(2,1)}, bf16[256,512]{1,0:T(8,128)(2,1)S(1)}, u32[]{:S(2)}, u32[]{:S(2)}) collective-permute-start(bf16[256,512]{1,0:T(8,128)(2,1)} %q_ref.1), channel_id=1, source_target_pairs={{0,2},{2,0},{1,3},{3,1},{4,6},{6,4},{5,7},{7,5},{8,10},{10,8},{9,1... | collective-permute-start | bytes 786440 | tf_op jit(solution)/shard_map/ppermute | solution.py:301
  31.4 3.5 %collective-permute-start.4 = (bf16[256,512]{1,0:T(8,128)(2,1)S(1)}, bf16[256,512]{1,0:T(8,128)(2,1)S(1)}, u32[]{:S(2)}, u32[]{:S(2)}) collective-permute-start(bf16[256,512]{1,0:T(8,128)(2,1)S(1)} %collective-permute-done.2.rest_4_), channel_id=1, source_target_pairs={{0,1},{1,0},{2,3},{3,2},{4,5},{5,4},{6,7},{7,6},{8,9},{9,8},{10,11... | collective-permute-start | bytes 786440 | tf_op jit(solution)/shard_map/ppermute | solution.py:301
  34.9 1.9 %collective-permute-start.5 = (bf16[256,512]{1,0:T(8,128)(2,1)S(1)}, bf16[256,512]{1,0:T(8,128)(2,1)S(1)}, u32[]{:S(2)}, u32[]{:S(2)}) collective-permute-start(bf16[256,512]{1,0:T(8,128)(2,1)S(1)} %collective-permute-done.3.rest_5_), channel_id=1, source_target_pairs={{0,1},{1,0},{2,3},{3,2},{4,5},{5,4},{6,7},{7,6},{8,9},{9,8},{10,11... | collective-permute-start | bytes 786440 | tf_op jit(solution)/shard_map/ppermute | solution.py:301
  36.9 2.4 %collective-permute-start.8 = (bf16[256,512]{1,0:T(8,128)(2,1)S(1)}, bf16[256,512]{1,0:T(8,128)(2,1)S(1)}, u32[]{:S(2)}, u32[]{:S(2)}) collective-permute-start(bf16[256,512]{1,0:T(8,128)(2,1)S(1)} %collective-permute-done.6.rest_8_), channel_id=1, source_target_pairs={{0,1},{1,0},{2,3},{3,2},{4,5},{5,4},{6,7},{7,6},{8,9},{9,8},{10,11... | collective-permute-start | bytes 786440 | tf_op jit(solution)/shard_map/ppermute | solution.py:301
  39.3 1.9 %collective-permute-start.9 = (bf16[256,512]{1,0:T(8,128)(2,1)S(1)}, bf16[256,512]{1,0:T(8,128)(2,1)S(1)}, u32[]{:S(2)}, u32[]{:S(2)}) collective-permute-start(bf16[256,512]{1,0:T(8,128)(2,1)S(1)} %collective-permute-done.7.rest_9_), channel_id=1, source_target_pairs={{0,1},{1,0},{2,3},{3,2},{4,5},{5,4},{6,7},{7,6},{8,9},{9,8},{10,11... | collective-permute-start | bytes 786440 | tf_op jit(solution)/shard_map/ppermute | solution.py:301
  45.3 2.6 %attend_across.1 = bf16[528,256]{1,0:T(8,128)(2,1)S(1)} custom-call(s32[64]{0:T(128)S(1)} %copy-done.8, s32[3]{0:T(128)S(1)} %add_add_fusion.1.where, bf16[256,512]{1,0:T(8,128)(2,1)S(1)} %collective-permute-done.10.q_ref, bf16[256,512]{1,0:T(8,128)(2,1)S(1)} %copy-done.2, bf16[256,512]{1,0:T(8,128)(2,1)S(1)} %copy-done.4, ...), custom_call_target="tpu_custom_call" | custom-call | flops 671088640 | bytes 3145728 | tf_op jit(solution)/shard_map/attend_across/pallas_call | solution.py:128
  47.9 2.1 %collective-permute-start.11 = (bf16[528,256]{1,0:T(8,128)(2,1)S(1)}, bf16[528,256]{1,0:T(8,128)(2,1)S(1)}, u32[]{:S(2)}, u32[]{:S(2)}) collective-permute-start(bf16[528,256]{1,0:T(8,128)(2,1)S(1)} %attend_across.1), channel_id=1, source_target_pairs={{0,2},{2,0},{1,3},{3,1},{4,6},{6,4},{5,7},{7,5},{8,10},{10,8},{9,1... | collective-permute-start | bytes 811016 | tf_op jit(solution)/shard_map/ppermute | solution.py:301
  50.0 2.7 %attend_own.1 = (f32[512,256]{1,0:T(8,128)S(1)}, f32[8,256]{1,0:T(8,128)S(1)}) custom-call(s32[64]{0:T(128)S(1)} %copy-done.8, s32[3]{0:T(128)S(1)} %add_add_fusion.where, bf16[256,512]{1,0:T(8,128)(2,1)S(1)} %copy-done.7, bf16[256,512]{1,0:T(8,128)(2,1)S(1)} %copy-done.3, bf16[256,512]{1,0:T(8,128)(2,1)S(1)} %copy-done.5, ...), custom_call_target="tpu_custom_call" | custom-call | flops 671088640 | bytes 3145728 | tf_op jit(solution)/shard_map/attend_own/pallas_call | solution.py:128
  52.8 7.8 %collective-permute-done.11.other_ref = bf16[528,256]{1,0:T(8,128)(2,1)S(1)} collective-permute-done((bf16[528,256]{1,0:T(8,128)(2,1)S(1)}, bf16[528,256]{1,0:T(8,128)(2,1)S(1)}, u32[]{:S(2)}, u32[]{:S(2)}) %collective-permute-start.11) | collective-permute-done | bytes 270368 | tf_op jit(solution)/shard_map/ppermute | solution.py:301
  62.5 4.1 %all-to-all-start = ((bf16[4,64,2048]{2,1,0:T(8,128)(2,1)}), bf16[4,64,2048]{2,1,0:T(8,128)(2,1)S(1)}, u32[]{:S(2)}, u32[]{:S(2)}) async-start(bf16[4,64,2048]{2,1,0:T(8,128)(2,1)} %bitcast.5), calls=%async_computation | async-start | bytes 2097152 | tf_op jit(solution)/shard_map/all_to_all | solution.py:310
  66.6 2.1 %collective-permute-start.12 = (bf16[256,512]{1,0:T(8,128)(2,1)S(1)}, bf16[256,512]{1,0:T(8,128)(2,1)S(1)}, u32[]{:S(2)}, u32[]{:S(2)}) collective-permute-start(bf16[256,512]{1,0:T(8,128)(2,1)S(1)} %copy-done.9), channel_id=1, source_target_pairs={{0,2},{2,0},{1,3},{3,1},{4,6},{6,4},{5,7},{7,5},{8,10},{10,8},{9,1... | collective-permute-start | bytes 786440 | tf_op jit(solution)/shard_map/ppermute | solution.py:301
  68.7 8.9 %all-to-all-done.parts_ref = bf16[4,64,2048]{2,1,0:T(8,128)(2,1)S(1)} async-done(((bf16[4,64,2048]{2,1,0:T(8,128)(2,1)}), bf16[4,64,2048]{2,1,0:T(8,128)(2,1)S(1)}, u32[]{:S(2)}, u32[]{:S(2)}) %all-to-all-start) | async-done | bytes 1048608 | tf_op jit(solution)/shard_map/all_to_all | solution.py:310
  78.5 14.1 %all-to-all-start.1 = ((bf16[4,16,2048]{2,1,0:T(8,128)(2,1)}), bf16[4,16,2048]{2,1,0:T(8,128)(2,1)S(1)}, u32[]{:S(2)}, u32[]{:S(2)}) async-start(bf16[4,16,2048]{2,1,0:T(8,128)(2,1)} %bitcast.6), calls=%async_computation.1 | async-start | bytes 524288 | tf_op jit(solution)/shard_map/all_to_all | solution.py:310
  93.7 3.8 %collective-permute-start.13 = (bf16[2,256,512]{2,1,0:T(8,128)(2,1)S(1)}, bf16[2,256,512]{2,1,0:T(8,128)(2,1)S(1)}, u32[]{:S(2)}, u32[]{:S(2)}) collective-permute-start(bf16[2,256,512]{2,1,0:T(8,128)(2,1)S(1)} %pad_maximum_fusion.mine_ref), channel_id=1, source_target_pairs={{0,1},{1,0},{2,3},{3,2},{4,5},{5,4},{6,7},{7,6},{8,9},{9,8},{10,11... | collective-permute-start | bytes 1572872 | tf_op jit(solution)/shard_map/ppermute | solution.py:301
  99.8 18.6 %all_to_all.49 = bf16[16,16,512]{2,1,0:T(8,128)(2,1)S(1)} all-to-all(bf16[16,16,512]{2,1,0:T(8,128)(2,1)S(1)} %bitcast.23), channel_id=1, replica_groups=mesh['z_lo'=4,'x'=4,'y'=8,'z_hi'=2,'core'=2] {'z_hi','z_lo','core'}, dimensions={0} | all-to-all | bytes 524288 | tf_op jit(solution)/shard_map/all_to_all | solution.py:310
  119.4 3.5 %all-to-all-start.3 = ((bf16[4,256,512]{2,1,0:T(8,128)(2,1)}), bf16[4,256,512]{2,1,0:T(8,128)(2,1)S(1)}, u32[]{:S(2)}, u32[]{:S(2)}) async-start(bf16[4,256,512]{2,1,0:T(8,128)(2,1)} %bitcast.13), calls=%async_computation.3 | async-start | bytes 2097152 | tf_op jit(solution)/shard_map/all_to_all | solution.py:310
  123.7 14.6 %all-to-all-done.3 = bf16[4,256,512]{2,1,0:T(8,128)(2,1)S(1)} async-done(((bf16[4,256,512]{2,1,0:T(8,128)(2,1)}), bf16[4,256,512]{2,1,0:T(8,128)(2,1)S(1)}, u32[]{:S(2)}, u32[]{:S(2)}) %all-to-all-start.3) | async-done | bytes 1048608 | tf_op jit(solution)/shard_map/all_to_all | solution.py:310
  139.5 23.2 %all_to_all.50 = bf16[8,64,512]{2,1,0:T(8,128)(2,1)S(1)} all-to-all(bf16[8,64,512]{2,1,0:T(8,128)(2,1)S(1)} %bitcast.21), channel_id=1, replica_groups=mesh['z_lo'=4,'x'=4,'y'=8,'z_hi'=2,'core'=2] {'y'}, dimensions={0} | all-to-all | bytes 1048576 | tf_op jit(solution)/shard_map/all_to_all | solution.py:310
  (51 shorter events, 13.9 us)
Async XLA Ops:
  0.6 92.0 %copy-start = (bf16[128,2048]{1,0:T(8,128)(2,1)S(1)}, bf16[128,2048]{1,0:T(8,128)(2,1)}, u32[]{:S(2)}) copy-start(bf16[128,2048]{1,0:T(8,128)(2,1)} %param.15) | copy-start | bytes 1572868
  0.6 14.7 %collective-permute-start.2 = (bf16[256,512]{1,0:T(8,128)(2,1)}, bf16[256,512]{1,0:T(8,128)(2,1)S(1)}, u32[]{:S(2)}, u32[]{:S(2)}) collective-permute-start(bf16[256,512]{1,0:T(8,128)(2,1)} %rest_0_.3), channel_id=1, source_target_pairs={{0,4},{4,8},{8,12},{12,16},{16,20},{20,24},{24,28},{28,0},{1,5},{5... | collective-permute-start | bytes 786440 | tf_op jit(solution)/shard_map/ppermute | solution.py:306
  4.8 12.5 %collective-permute-start.3 = (bf16[256,512]{1,0:T(8,128)(2,1)}, bf16[256,512]{1,0:T(8,128)(2,1)S(1)}, u32[]{:S(2)}, u32[]{:S(2)}) collective-permute-start(bf16[256,512]{1,0:T(8,128)(2,1)} %rest_1_.3), channel_id=1, source_target_pairs={{0,4},{4,8},{8,12},{12,16},{16,20},{20,24},{24,28},{28,0},{1,5},{5... | collective-permute-start | bytes 786440 | tf_op jit(solution)/shard_map/ppermute | solution.py:306
  8.0 23.4 %collective-permute-start = (bf16[256,512]{1,0:T(8,128)(2,1)}, bf16[256,512]{1,0:T(8,128)(2,1)S(1)}, u32[]{:S(2)}, u32[]{:S(2)}) collective-permute-start(bf16[256,512]{1,0:T(8,128)(2,1)} %rest_0_.3), channel_id=1, source_target_pairs={{0,1},{1,0},{2,3},{3,2},{4,5},{5,4},{6,7},{7,6},{8,9},{9,8},{10,11... | collective-permute-start | bytes 786440 | tf_op jit(solution)/shard_map/ppermute | solution.py:301
  13.4 21.5 %collective-permute-start.1 = (bf16[256,512]{1,0:T(8,128)(2,1)}, bf16[256,512]{1,0:T(8,128)(2,1)S(1)}, u32[]{:S(2)}, u32[]{:S(2)}) collective-permute-start(bf16[256,512]{1,0:T(8,128)(2,1)} %rest_1_.3), channel_id=1, source_target_pairs={{0,1},{1,0},{2,3},{3,2},{4,5},{5,4},{6,7},{7,6},{8,9},{9,8},{10,11... | collective-permute-start | bytes 786440 | tf_op jit(solution)/shard_map/ppermute | solution.py:301
  15.4 21.5 %collective-permute-start.6 = (bf16[256,512]{1,0:T(8,128)(2,1)S(1)}, bf16[256,512]{1,0:T(8,128)(2,1)S(1)}, u32[]{:S(2)}, u32[]{:S(2)}) collective-permute-start(bf16[256,512]{1,0:T(8,128)(2,1)S(1)} %collective-permute-done.2.rest_4_), channel_id=1, source_target_pairs={{0,4},{4,8},{8,12},{12,16},{16,20},{20,24},{24,28},{28,0},{1,5},{5... | collective-permute-start | bytes 786440 | tf_op jit(solution)/shard_map/ppermute | solution.py:306
  17.3 22.0 %collective-permute-start.7 = (bf16[256,512]{1,0:T(8,128)(2,1)S(1)}, bf16[256,512]{1,0:T(8,128)(2,1)S(1)}, u32[]{:S(2)}, u32[]{:S(2)}) collective-permute-start(bf16[256,512]{1,0:T(8,128)(2,1)S(1)} %collective-permute-done.3.rest_5_), channel_id=1, source_target_pairs={{0,4},{4,8},{8,12},{12,16},{16,20},{20,24},{24,28},{28,0},{1,5},{5... | collective-permute-start | bytes 786440 | tf_op jit(solution)/shard_map/ppermute | solution.py:306
  20.8 20.6 %collective-permute-start.10 = (bf16[256,512]{1,0:T(8,128)(2,1)}, bf16[256,512]{1,0:T(8,128)(2,1)S(1)}, u32[]{:S(2)}, u32[]{:S(2)}) collective-permute-start(bf16[256,512]{1,0:T(8,128)(2,1)} %q_ref.1), channel_id=1, source_target_pairs={{0,2},{2,0},{1,3},{3,1},{4,6},{6,4},{5,7},{7,5},{8,10},{10,8},{9,1... | collective-permute-start | bytes 786440 | tf_op jit(solution)/shard_map/ppermute | solution.py:301
  31.4 9.9 %collective-permute-start.4 = (bf16[256,512]{1,0:T(8,128)(2,1)S(1)}, bf16[256,512]{1,0:T(8,128)(2,1)S(1)}, u32[]{:S(2)}, u32[]{:S(2)}) collective-permute-start(bf16[256,512]{1,0:T(8,128)(2,1)S(1)} %collective-permute-done.2.rest_4_), channel_id=1, source_target_pairs={{0,1},{1,0},{2,3},{3,2},{4,5},{5,4},{6,7},{7,6},{8,9},{9,8},{10,11... | collective-permute-start | bytes 786440 | tf_op jit(solution)/shard_map/ppermute | solution.py:301
  34.9 6.4 %collective-permute-start.5 = (bf16[256,512]{1,0:T(8,128)(2,1)S(1)}, bf16[256,512]{1,0:T(8,128)(2,1)S(1)}, u32[]{:S(2)}, u32[]{:S(2)}) collective-permute-start(bf16[256,512]{1,0:T(8,128)(2,1)S(1)} %collective-permute-done.3.rest_5_), channel_id=1, source_target_pairs={{0,1},{1,0},{2,3},{3,2},{4,5},{5,4},{6,7},{7,6},{8,9},{9,8},{10,11... | collective-permute-start | bytes 786440 | tf_op jit(solution)/shard_map/ppermute | solution.py:301
  36.9 4.5 %collective-permute-start.8 = (bf16[256,512]{1,0:T(8,128)(2,1)S(1)}, bf16[256,512]{1,0:T(8,128)(2,1)S(1)}, u32[]{:S(2)}, u32[]{:S(2)}) collective-permute-start(bf16[256,512]{1,0:T(8,128)(2,1)S(1)} %collective-permute-done.6.rest_8_), channel_id=1, source_target_pairs={{0,1},{1,0},{2,3},{3,2},{4,5},{5,4},{6,7},{7,6},{8,9},{9,8},{10,11... | collective-permute-start | bytes 786440 | tf_op jit(solution)/shard_map/ppermute | solution.py:301
  39.3 3.4 %collective-permute-start.9 = (bf16[256,512]{1,0:T(8,128)(2,1)S(1)}, bf16[256,512]{1,0:T(8,128)(2,1)S(1)}, u32[]{:S(2)}, u32[]{:S(2)}) collective-permute-start(bf16[256,512]{1,0:T(8,128)(2,1)S(1)} %collective-permute-done.7.rest_9_), channel_id=1, source_target_pairs={{0,1},{1,0},{2,3},{3,2},{4,5},{5,4},{6,7},{7,6},{8,9},{9,8},{10,11... | collective-permute-start | bytes 786440 | tf_op jit(solution)/shard_map/ppermute | solution.py:301
  45.3 4.7 %copy-start.3 = (bf16[256,512]{1,0:T(8,128)(2,1)S(1)}, bf16[256,512]{1,0:T(8,128)(2,1)}, u32[]{:S(2)}) copy-start(bf16[256,512]{1,0:T(8,128)(2,1)} %rest_0_.3) | copy-start | bytes 786436
  45.3 4.7 %copy-start.5 = (bf16[256,512]{1,0:T(8,128)(2,1)S(1)}, bf16[256,512]{1,0:T(8,128)(2,1)}, u32[]{:S(2)}) copy-start(bf16[256,512]{1,0:T(8,128)(2,1)} %rest_1_.3) | copy-start | bytes 786436
  45.3 4.7 %copy-start.7 = (bf16[256,512]{1,0:T(8,128)(2,1)S(1)}, bf16[256,512]{1,0:T(8,128)(2,1)}, u32[]{:S(2)}) copy-start(bf16[256,512]{1,0:T(8,128)(2,1)} %q_ref.1) | copy-start | bytes 786436
  47.9 12.8 %copy-start.1 = (bf16[512,2048]{1,0:T(8,128)(2,1)S(1)}, bf16[512,2048]{1,0:T(8,128)(2,1)}, u32[]{:S(2)}) copy-start(bf16[512,2048]{1,0:T(8,128)(2,1)} %w_ref.2) | copy-start | bytes 6291460
  47.9 12.8 %collective-permute-start.11 = (bf16[528,256]{1,0:T(8,128)(2,1)S(1)}, bf16[528,256]{1,0:T(8,128)(2,1)S(1)}, u32[]{:S(2)}, u32[]{:S(2)}) collective-permute-start(bf16[528,256]{1,0:T(8,128)(2,1)S(1)} %attend_across.1), channel_id=1, source_target_pairs={{0,2},{2,0},{1,3},{3,1},{4,6},{6,4},{5,7},{7,5},{8,10},{10,8},{9,1... | collective-permute-start | bytes 811016 | tf_op jit(solution)/shard_map/ppermute | solution.py:301
  62.5 15.2 %all-to-all-start = ((bf16[4,64,2048]{2,1,0:T(8,128)(2,1)}), bf16[4,64,2048]{2,1,0:T(8,128)(2,1)S(1)}, u32[]{:S(2)}, u32[]{:S(2)}) async-start(bf16[4,64,2048]{2,1,0:T(8,128)(2,1)} %bitcast.5), calls=%async_computation | async-start | bytes 2097152 | tf_op jit(solution)/shard_map/all_to_all | solution.py:310
  66.6 31.6 %copy-start.10 = (f32[256]{0:T(256)S(1)}, f32[256]{0:T(256)}, u32[]{:S(2)}) copy-start(f32[256]{0:T(256)} %param.19) | copy-start | bytes 3076
  66.6 31.8 %copy-start.6 = (bf16[2048,128]{1,0:T(8,128)(2,1)S(1)}, bf16[2048,128]{1,0:T(8,128)(2,1)}, u32[]{:S(2)}) copy-start(bf16[2048,128]{1,0:T(8,128)(2,1)} %w_ref.3) | copy-start | bytes 1572868
  66.6 27.0 %collective-permute-start.12 = (bf16[256,512]{1,0:T(8,128)(2,1)S(1)}, bf16[256,512]{1,0:T(8,128)(2,1)S(1)}, u32[]{:S(2)}, u32[]{:S(2)}) collective-permute-start(bf16[256,512]{1,0:T(8,128)(2,1)S(1)} %copy-done.9), channel_id=1, source_target_pairs={{0,2},{2,0},{1,3},{3,1},{4,6},{6,4},{5,7},{7,5},{8,10},{10,8},{9,1... | collective-permute-start | bytes 786440 | tf_op jit(solution)/shard_map/ppermute | solution.py:301
  78.5 19.9 %all-to-all-start.1 = ((bf16[4,16,2048]{2,1,0:T(8,128)(2,1)}), bf16[4,16,2048]{2,1,0:T(8,128)(2,1)S(1)}, u32[]{:S(2)}, u32[]{:S(2)}) async-start(bf16[4,16,2048]{2,1,0:T(8,128)(2,1)} %bitcast.6), calls=%async_computation.1 | async-start | bytes 524288 | tf_op jit(solution)/shard_map/all_to_all | solution.py:310
  93.7 25.7 %collective-permute-start.13 = (bf16[2,256,512]{2,1,0:T(8,128)(2,1)S(1)}, bf16[2,256,512]{2,1,0:T(8,128)(2,1)S(1)}, u32[]{:S(2)}, u32[]{:S(2)}) collective-permute-start(bf16[2,256,512]{2,1,0:T(8,128)(2,1)S(1)} %pad_maximum_fusion.mine_ref), channel_id=1, source_target_pairs={{0,1},{1,0},{2,3},{3,2},{4,5},{5,4},{6,7},{7,6},{8,9},{9,8},{10,11... | collective-permute-start | bytes 1572872 | tf_op jit(solution)/shard_map/ppermute | solution.py:301
  119.4 18.8 %all-to-all-start.3 = ((bf16[4,256,512]{2,1,0:T(8,128)(2,1)}), bf16[4,256,512]{2,1,0:T(8,128)(2,1)S(1)}, u32[]{:S(2)}, u32[]{:S(2)}) async-start(bf16[4,256,512]{2,1,0:T(8,128)(2,1)} %bitcast.13), calls=%async_computation.3 | async-start | bytes 2097152 | tf_op jit(solution)/shard_map/all_to_all | solution.py:310
  (4 other events, 6.7 us)

commit v6 on v5

--- a/solution.py
+++ b/solution.py
@@ -38,7 +38,7 @@
 
     zero = jnp.int32(0)
     _, start, lowest, highest = lax.fori_loop(
-        0, lengths.shape[0], pass_end, (zero, jnp.zeros_like(query), zero, zero)
+        0, lengths.shape[0], pass_end, (zero, jnp.zeros_like(query), zero, zero), unroll=16
     )
     start_ref[...] = jnp.broadcast_to(start, start_ref.shape)
     top_ref[...] = jnp.full_like(top_ref, FLOOR)

time: 164 us -> 164 us (level)
  blocking collectives: 41.8 us -> 43.7 us
    all_to_all x2, blocking collectives: 41.8 us -> 43.7 us  [exchange(): return lax.all_to_all(array, axis, 0, 0, tiled=True)]
  transfers between devices with their start and end apart: 17 -> 17, of which waited for: 4 -> 4; matrix products, arithmetic and copies ran while one was open for 2% -> 2% of each run, Pallas kernels for 4% -> 3%
where the time goes in v6:
time: 164 us
  starting transfers between devices  70.1 us (43%)
  blocking collectives  43.7 us (27%)
  waiting for transfers between devices  33.1 us (20%)
  Pallas kernels  10.5 us (6%)
  local copies, waits for them, and re-layouts  4.06 us (2%)
    all_to_all x2, blocking collectives, exchange(): return lax.all_to_all(array, axis, 0, 0, tiled=True)  43.7 us
    ppermute x10, starting transfers between devices, swap(): return lax.ppermute(array, axis, [(0, 1), (1, 0)])  35.6 us
    all_to_all x3, waiting for transfers between devices, exchange(): return lax.all_to_all(array, axis, 0, 0, tiled=True)  23.5 us
    all_to_all x3, starting transfers between devices, exchange(): return lax.all_to_all(array, axis, 0, 0, tiled=True)  21.7 us
    ppermute x4, starting transfers between devices, shift(): lax.ppermute(array, axis, [(i, (i + 1) % length) for i in range(length)])  12.7 us
    ppermute x10, waiting for transfers between devices, swap(): return lax.ppermute(array, axis, [(0, 1), (1, 0)])  9.55 us
    pallas_call x2, Pallas kernels, attend(): pl.pallas_call(functools.partial(attend_kernel, final=final), out_shape=o...  4.05 us
  transfers between devices with their start and end apart: 17, of which 4 were waited for; matrix products, arithmetic and copies ran while one was open for 2% of the time, Pallas kernels for 3%

profile of v6, /device:TPU:1, one launch (start us, length us, event | category | flops | bytes accessed | tf_op | source)
XLA Modules:
  0.0 164.4 jit_solution(16031728934337196220)
XLA Ops:
  0.6 4.2 %collective-permute-start.2 = (bf16[256,512]{1,0:T(8,128)(2,1)}, bf16[256,512]{1,0:T(8,128)(2,1)S(1)}, u32[]{:S(2)}, u32[]{:S(2)}) collective-permute-start(bf16[256,512]{1,0:T(8,128)(2,1)} %rest_0_.3), channel_id=1, source_target_pairs={{0,4},{4,8},{8,12},{12,16},{16,20},{20,24},{24,28},{28,0},{1,5},{5... | collective-permute-start | bytes 786440 | tf_op jit(solution)/shard_map/ppermute | solution.py:306
  4.8 3.2 %collective-permute-start.3 = (bf16[256,512]{1,0:T(8,128)(2,1)}, bf16[256,512]{1,0:T(8,128)(2,1)S(1)}, u32[]{:S(2)}, u32[]{:S(2)}) collective-permute-start(bf16[256,512]{1,0:T(8,128)(2,1)} %rest_1_.3), channel_id=1, source_target_pairs={{0,4},{4,8},{8,12},{12,16},{16,20},{20,24},{24,28},{28,0},{1,5},{5... | collective-permute-start | bytes 786440 | tf_op jit(solution)/shard_map/ppermute | solution.py:306
  8.0 5.4 %collective-permute-start = (bf16[256,512]{1,0:T(8,128)(2,1)}, bf16[256,512]{1,0:T(8,128)(2,1)S(1)}, u32[]{:S(2)}, u32[]{:S(2)}) collective-permute-start(bf16[256,512]{1,0:T(8,128)(2,1)} %rest_0_.3), channel_id=1, source_target_pairs={{0,1},{1,0},{2,3},{3,2},{4,5},{5,4},{6,7},{7,6},{8,9},{9,8},{10,11... | collective-permute-start | bytes 786440 | tf_op jit(solution)/shard_map/ppermute | solution.py:301
  13.4 1.9 %collective-permute-start.1 = (bf16[256,512]{1,0:T(8,128)(2,1)}, bf16[256,512]{1,0:T(8,128)(2,1)S(1)}, u32[]{:S(2)}, u32[]{:S(2)}) collective-permute-start(bf16[256,512]{1,0:T(8,128)(2,1)} %rest_1_.3), channel_id=1, source_target_pairs={{0,1},{1,0},{2,3},{3,2},{4,5},{5,4},{6,7},{7,6},{8,9},{9,8},{10,11... | collective-permute-start | bytes 786440 | tf_op jit(solution)/shard_map/ppermute | solution.py:301
  15.4 1.9 %collective-permute-start.6 = (bf16[256,512]{1,0:T(8,128)(2,1)S(1)}, bf16[256,512]{1,0:T(8,128)(2,1)S(1)}, u32[]{:S(2)}, u32[]{:S(2)}) collective-permute-start(bf16[256,512]{1,0:T(8,128)(2,1)S(1)} %collective-permute-done.2.rest_4_), channel_id=1, source_target_pairs={{0,4},{4,8},{8,12},{12,16},{16,20},{20,24},{24,28},{28,0},{1,5},{5... | collective-permute-start | bytes 786440 | tf_op jit(solution)/shard_map/ppermute | solution.py:306
  17.3 3.5 %collective-permute-start.7 = (bf16[256,512]{1,0:T(8,128)(2,1)S(1)}, bf16[256,512]{1,0:T(8,128)(2,1)S(1)}, u32[]{:S(2)}, u32[]{:S(2)}) collective-permute-start(bf16[256,512]{1,0:T(8,128)(2,1)S(1)} %collective-permute-done.3.rest_5_), channel_id=1, source_target_pairs={{0,4},{4,8},{8,12},{12,16},{16,20},{20,24},{24,28},{28,0},{1,5},{5... | collective-permute-start | bytes 786440 | tf_op jit(solution)/shard_map/ppermute | solution.py:306
  20.8 10.6 %collective-permute-start.10 = (bf16[256,512]{1,0:T(8,128)(2,1)}, bf16[256,512]{1,0:T(8,128)(2,1)S(1)}, u32[]{:S(2)}, u32[]{:S(2)}) collective-permute-start(bf16[256,512]{1,0:T(8,128)(2,1)} %q_ref.1), channel_id=1, source_target_pairs={{0,2},{2,0},{1,3},{3,1},{4,6},{6,4},{5,7},{7,5},{8,10},{10,8},{9,1... | collective-permute-start | bytes 786440 | tf_op jit(solution)/shard_map/ppermute | solution.py:301
  31.4 3.5 %collective-permute-start.4 = (bf16[256,512]{1,0:T(8,128)(2,1)S(1)}, bf16[256,512]{1,0:T(8,128)(2,1)S(1)}, u32[]{:S(2)}, u32[]{:S(2)}) collective-permute-start(bf16[256,512]{1,0:T(8,128)(2,1)S(1)} %collective-permute-done.2.rest_4_), channel_id=1, source_target_pairs={{0,1},{1,0},{2,3},{3,2},{4,5},{5,4},{6,7},{7,6},{8,9},{9,8},{10,11... | collective-permute-start | bytes 786440 | tf_op jit(solution)/shard_map/ppermute | solution.py:301
  34.9 1.9 %collective-permute-start.5 = (bf16[256,512]{1,0:T(8,128)(2,1)S(1)}, bf16[256,512]{1,0:T(8,128)(2,1)S(1)}, u32[]{:S(2)}, u32[]{:S(2)}) collective-permute-start(bf16[256,512]{1,0:T(8,128)(2,1)S(1)} %collective-permute-done.3.rest_5_), channel_id=1, source_target_pairs={{0,1},{1,0},{2,3},{3,2},{4,5},{5,4},{6,7},{7,6},{8,9},{9,8},{10,11... | collective-permute-start | bytes 786440 | tf_op jit(solution)/shard_map/ppermute | solution.py:301
  36.9 2.4 %collective-permute-start.8 = (bf16[256,512]{1,0:T(8,128)(2,1)S(1)}, bf16[256,512]{1,0:T(8,128)(2,1)S(1)}, u32[]{:S(2)}, u32[]{:S(2)}) collective-permute-start(bf16[256,512]{1,0:T(8,128)(2,1)S(1)} %collective-permute-done.6.rest_8_), channel_id=1, source_target_pairs={{0,1},{1,0},{2,3},{3,2},{4,5},{5,4},{6,7},{7,6},{8,9},{9,8},{10,11... | collective-permute-start | bytes 786440 | tf_op jit(solution)/shard_map/ppermute | solution.py:301
  39.3 1.9 %collective-permute-start.9 = (bf16[256,512]{1,0:T(8,128)(2,1)S(1)}, bf16[256,512]{1,0:T(8,128)(2,1)S(1)}, u32[]{:S(2)}, u32[]{:S(2)}) collective-permute-start(bf16[256,512]{1,0:T(8,128)(2,1)S(1)} %collective-permute-done.7.rest_9_), channel_id=1, source_target_pairs={{0,1},{1,0},{2,3},{3,2},{4,5},{5,4},{6,7},{7,6},{8,9},{9,8},{10,11... | collective-permute-start | bytes 786440 | tf_op jit(solution)/shard_map/ppermute | solution.py:301
  46.9 2.1 %collective-permute-start.11 = (bf16[528,256]{1,0:T(8,128)(2,1)S(1)}, bf16[528,256]{1,0:T(8,128)(2,1)S(1)}, u32[]{:S(2)}, u32[]{:S(2)}) collective-permute-start(bf16[528,256]{1,0:T(8,128)(2,1)S(1)} %attend_across.1), channel_id=1, source_target_pairs={{0,2},{2,0},{1,3},{3,1},{4,6},{6,4},{5,7},{7,5},{8,10},{10,8},{9,1... | collective-permute-start | bytes 811016 | tf_op jit(solution)/shard_map/ppermute | solution.py:301
  49.1 2.4 %attend_own.1 = (f32[512,256]{1,0:T(8,128)S(1)}, f32[8,256]{1,0:T(8,128)S(1)}) custom-call(s32[64]{0:T(128)S(1)} %copy-done.8, s32[3]{0:T(128)S(1)} %add_add_fusion.where, bf16[256,512]{1,0:T(8,128)(2,1)S(1)} %copy-done.7, bf16[256,512]{1,0:T(8,128)(2,1)S(1)} %copy-done.3, bf16[256,512]{1,0:T(8,128)(2,1)S(1)} %copy-done.5, ...), custom_call_target="tpu_custom_call" | custom-call | flops 671088640 | bytes 3145728 | tf_op jit(solution)/shard_map/attend_own/pallas_call | solution.py:128
  51.5 8.2 %collective-permute-done.11.other_ref = bf16[528,256]{1,0:T(8,128)(2,1)S(1)} collective-permute-done((bf16[528,256]{1,0:T(8,128)(2,1)S(1)}, bf16[528,256]{1,0:T(8,128)(2,1)S(1)}, u32[]{:S(2)}, u32[]{:S(2)}) %collective-permute-start.11) | collective-permute-done | bytes 270368 | tf_op jit(solution)/shard_map/ppermute | solution.py:301
  59.7 1.8 %join.1 = (bf16[256,512]{1,0:T(8,128)(2,1)}, bf16[256,2048]{1,0:T(8,128)(2,1)}) custom-call(f32[512,256]{1,0:T(8,128)S(1)} %get-tuple-element.13.values_ref, f32[8,256]{1,0:T(8,128)S(1)} %get-tuple-element.14.levels_ref, bf16[528,256]{1,0:T(8,128)(2,1)S(1)} %collective-permute-done.11.other_ref, bf16[512,2048]{1,0:T(8,128)(2,1)S(1)} %copy-done.1), custom_call_target="tpu_custom_call" | custom-call | tf_op jit(solution)/shard_map/join/pallas_call | solution.py:173
  61.5 4.1 %all-to-all-start = ((bf16[4,64,2048]{2,1,0:T(8,128)(2,1)}), bf16[4,64,2048]{2,1,0:T(8,128)(2,1)S(1)}, u32[]{:S(2)}, u32[]{:S(2)}) async-start(bf16[4,64,2048]{2,1,0:T(8,128)(2,1)} %bitcast.5), calls=%async_computation | async-start | bytes 2097152 | tf_op jit(solution)/shard_map/all_to_all | solution.py:310
  65.7 2.1 %collective-permute-start.12 = (bf16[256,512]{1,0:T(8,128)(2,1)S(1)}, bf16[256,512]{1,0:T(8,128)(2,1)S(1)}, u32[]{:S(2)}, u32[]{:S(2)}) collective-permute-start(bf16[256,512]{1,0:T(8,128)(2,1)S(1)} %copy-done.9), channel_id=1, source_target_pairs={{0,2},{2,0},{1,3},{3,1},{4,6},{6,4},{5,7},{7,5},{8,10},{10,8},{9,1... | collective-permute-start | bytes 786440 | tf_op jit(solution)/shard_map/ppermute | solution.py:301
  67.8 9.0 %all-to-all-done.parts_ref = bf16[4,64,2048]{2,1,0:T(8,128)(2,1)S(1)} async-done(((bf16[4,64,2048]{2,1,0:T(8,128)(2,1)}), bf16[4,64,2048]{2,1,0:T(8,128)(2,1)S(1)}, u32[]{:S(2)}, u32[]{:S(2)}) %all-to-all-start) | async-done | bytes 1048608 | tf_op jit(solution)/shard_map/all_to_all | solution.py:310
  77.6 14.1 %all-to-all-start.1 = ((bf16[4,16,2048]{2,1,0:T(8,128)(2,1)}), bf16[4,16,2048]{2,1,0:T(8,128)(2,1)S(1)}, u32[]{:S(2)}, u32[]{:S(2)}) async-start(bf16[4,16,2048]{2,1,0:T(8,128)(2,1)} %bitcast.6), calls=%async_computation.1 | async-start | bytes 524288 | tf_op jit(solution)/shard_map/all_to_all | solution.py:310
  92.8 3.8 %collective-permute-start.13 = (bf16[2,256,512]{2,1,0:T(8,128)(2,1)S(1)}, bf16[2,256,512]{2,1,0:T(8,128)(2,1)S(1)}, u32[]{:S(2)}, u32[]{:S(2)}) collective-permute-start(bf16[2,256,512]{2,1,0:T(8,128)(2,1)S(1)} %pad_maximum_fusion.mine_ref), channel_id=1, source_target_pairs={{0,1},{1,0},{2,3},{3,2},{4,5},{5,4},{6,7},{7,6},{8,9},{9,8},{10,11... | collective-permute-start | bytes 1572872 | tf_op jit(solution)/shard_map/ppermute | solution.py:301
  98.8 18.6 %all_to_all.49 = bf16[16,16,512]{2,1,0:T(8,128)(2,1)S(1)} all-to-all(bf16[16,16,512]{2,1,0:T(8,128)(2,1)S(1)} %bitcast.23), channel_id=1, replica_groups=mesh['z_lo'=4,'x'=4,'y'=8,'z_hi'=2,'core'=2] {'z_hi','z_lo','core'}, dimensions={0} | all-to-all | bytes 524288 | tf_op jit(solution)/shard_map/all_to_all | solution.py:310
  118.5 3.5 %all-to-all-start.3 = ((bf16[4,256,512]{2,1,0:T(8,128)(2,1)}), bf16[4,256,512]{2,1,0:T(8,128)(2,1)S(1)}, u32[]{:S(2)}, u32[]{:S(2)}) async-start(bf16[4,256,512]{2,1,0:T(8,128)(2,1)} %bitcast.13), calls=%async_computation.3 | async-start | bytes 2097152 | tf_op jit(solution)/shard_map/all_to_all | solution.py:310
  122.7 14.6 %all-to-all-done.3 = bf16[4,256,512]{2,1,0:T(8,128)(2,1)S(1)} async-done(((bf16[4,256,512]{2,1,0:T(8,128)(2,1)}), bf16[4,256,512]{2,1,0:T(8,128)(2,1)S(1)}, u32[]{:S(2)}, u32[]{:S(2)}) %all-to-all-start.3) | async-done | bytes 1048608 | tf_op jit(solution)/shard_map/all_to_all | solution.py:310
  138.6 25.1 %all_to_all.50 = bf16[8,64,512]{2,1,0:T(8,128)(2,1)S(1)} all-to-all(bf16[8,64,512]{2,1,0:T(8,128)(2,1)S(1)} %bitcast.21), channel_id=1, replica_groups=mesh['z_lo'=4,'x'=4,'y'=8,'z_hi'=2,'core'=2] {'y'}, dimensions={0} | all-to-all | bytes 1048576 | tf_op jit(solution)/shard_map/all_to_all | solution.py:310
  (51 shorter events, 13.6 us)
Async XLA Ops:
  0.6 91.0 %copy-start = (bf16[128,2048]{1,0:T(8,128)(2,1)S(1)}, bf16[128,2048]{1,0:T(8,128)(2,1)}, u32[]{:S(2)}) copy-start(bf16[128,2048]{1,0:T(8,128)(2,1)} %param.15) | copy-start | bytes 1572868
  0.6 14.7 %collective-permute-start.2 = (bf16[256,512]{1,0:T(8,128)(2,1)}, bf16[256,512]{1,0:T(8,128)(2,1)S(1)}, u32[]{:S(2)}, u32[]{:S(2)}) collective-permute-start(bf16[256,512]{1,0:T(8,128)(2,1)} %rest_0_.3), channel_id=1, source_target_pairs={{0,4},{4,8},{8,12},{12,16},{16,20},{20,24},{24,28},{28,0},{1,5},{5... | collective-permute-start | bytes 786440 | tf_op jit(solution)/shard_map/ppermute | solution.py:306
  4.8 12.5 %collective-permute-start.3 = (bf16[256,512]{1,0:T(8,128)(2,1)}, bf16[256,512]{1,0:T(8,128)(2,1)S(1)}, u32[]{:S(2)}, u32[]{:S(2)}) collective-permute-start(bf16[256,512]{1,0:T(8,128)(2,1)} %rest_1_.3), channel_id=1, source_target_pairs={{0,4},{4,8},{8,12},{12,16},{16,20},{20,24},{24,28},{28,0},{1,5},{5... | collective-permute-start | bytes 786440 | tf_op jit(solution)/shard_map/ppermute | solution.py:306
  8.0 23.4 %collective-permute-start = (bf16[256,512]{1,0:T(8,128)(2,1)}, bf16[256,512]{1,0:T(8,128)(2,1)S(1)}, u32[]{:S(2)}, u32[]{:S(2)}) collective-permute-start(bf16[256,512]{1,0:T(8,128)(2,1)} %rest_0_.3), channel_id=1, source_target_pairs={{0,1},{1,0},{2,3},{3,2},{4,5},{5,4},{6,7},{7,6},{8,9},{9,8},{10,11... | collective-permute-start | bytes 786440 | tf_op jit(solution)/shard_map/ppermute | solution.py:301
  13.4 21.5 %collective-permute-start.1 = (bf16[256,512]{1,0:T(8,128)(2,1)}, bf16[256,512]{1,0:T(8,128)(2,1)S(1)}, u32[]{:S(2)}, u32[]{:S(2)}) collective-permute-start(bf16[256,512]{1,0:T(8,128)(2,1)} %rest_1_.3), channel_id=1, source_target_pairs={{0,1},{1,0},{2,3},{3,2},{4,5},{5,4},{6,7},{7,6},{8,9},{9,8},{10,11... | collective-permute-start | bytes 786440 | tf_op jit(solution)/shard_map/ppermute | solution.py:301
  15.4 21.5 %collective-permute-start.6 = (bf16[256,512]{1,0:T(8,128)(2,1)S(1)}, bf16[256,512]{1,0:T(8,128)(2,1)S(1)}, u32[]{:S(2)}, u32[]{:S(2)}) collective-permute-start(bf16[256,512]{1,0:T(8,128)(2,1)S(1)} %collective-permute-done.2.rest_4_), channel_id=1, source_target_pairs={{0,4},{4,8},{8,12},{12,16},{16,20},{20,24},{24,28},{28,0},{1,5},{5... | collective-permute-start | bytes 786440 | tf_op jit(solution)/shard_map/ppermute | solution.py:306
  17.3 22.0 %collective-permute-start.7 = (bf16[256,512]{1,0:T(8,128)(2,1)S(1)}, bf16[256,512]{1,0:T(8,128)(2,1)S(1)}, u32[]{:S(2)}, u32[]{:S(2)}) collective-permute-start(bf16[256,512]{1,0:T(8,128)(2,1)S(1)} %collective-permute-done.3.rest_5_), channel_id=1, source_target_pairs={{0,4},{4,8},{8,12},{12,16},{16,20},{20,24},{24,28},{28,0},{1,5},{5... | collective-permute-start | bytes 786440 | tf_op jit(solution)/shard_map/ppermute | solution.py:306
  20.8 20.6 %collective-permute-start.10 = (bf16[256,512]{1,0:T(8,128)(2,1)}, bf16[256,512]{1,0:T(8,128)(2,1)S(1)}, u32[]{:S(2)}, u32[]{:S(2)}) collective-permute-start(bf16[256,512]{1,0:T(8,128)(2,1)} %q_ref.1), channel_id=1, source_target_pairs={{0,2},{2,0},{1,3},{3,1},{4,6},{6,4},{5,7},{7,5},{8,10},{10,8},{9,1... | collective-permute-start | bytes 786440 | tf_op jit(solution)/shard_map/ppermute | solution.py:301
  31.4 9.9 %collective-permute-start.4 = (bf16[256,512]{1,0:T(8,128)(2,1)S(1)}, bf16[256,512]{1,0:T(8,128)(2,1)S(1)}, u32[]{:S(2)}, u32[]{:S(2)}) collective-permute-start(bf16[256,512]{1,0:T(8,128)(2,1)S(1)} %collective-permute-done.2.rest_4_), channel_id=1, source_target_pairs={{0,1},{1,0},{2,3},{3,2},{4,5},{5,4},{6,7},{7,6},{8,9},{9,8},{10,11... | collective-permute-start | bytes 786440 | tf_op jit(solution)/shard_map/ppermute | solution.py:301
  34.9 6.4 %collective-permute-start.5 = (bf16[256,512]{1,0:T(8,128)(2,1)S(1)}, bf16[256,512]{1,0:T(8,128)(2,1)S(1)}, u32[]{:S(2)}, u32[]{:S(2)}) collective-permute-start(bf16[256,512]{1,0:T(8,128)(2,1)S(1)} %collective-permute-done.3.rest_5_), channel_id=1, source_target_pairs={{0,1},{1,0},{2,3},{3,2},{4,5},{5,4},{6,7},{7,6},{8,9},{9,8},{10,11... | collective-permute-start | bytes 786440 | tf_op jit(solution)/shard_map/ppermute | solution.py:301
  36.9 4.5 %collective-permute-start.8 = (bf16[256,512]{1,0:T(8,128)(2,1)S(1)}, bf16[256,512]{1,0:T(8,128)(2,1)S(1)}, u32[]{:S(2)}, u32[]{:S(2)}) collective-permute-start(bf16[256,512]{1,0:T(8,128)(2,1)S(1)} %collective-permute-done.6.rest_8_), channel_id=1, source_target_pairs={{0,1},{1,0},{2,3},{3,2},{4,5},{5,4},{6,7},{7,6},{8,9},{9,8},{10,11... | collective-permute-start | bytes 786440 | tf_op jit(solution)/shard_map/ppermute | solution.py:301
  39.3 3.4 %collective-permute-start.9 = (bf16[256,512]{1,0:T(8,128)(2,1)S(1)}, bf16[256,512]{1,0:T(8,128)(2,1)S(1)}, u32[]{:S(2)}, u32[]{:S(2)}) collective-permute-start(bf16[256,512]{1,0:T(8,128)(2,1)S(1)} %collective-permute-done.7.rest_9_), channel_id=1, source_target_pairs={{0,1},{1,0},{2,3},{3,2},{4,5},{5,4},{6,7},{7,6},{8,9},{9,8},{10,11... | collective-permute-start | bytes 786440 | tf_op jit(solution)/shard_map/ppermute | solution.py:301
  45.3 3.8 %copy-start.5 = (bf16[256,512]{1,0:T(8,128)(2,1)S(1)}, bf16[256,512]{1,0:T(8,128)(2,1)}, u32[]{:S(2)}) copy-start(bf16[256,512]{1,0:T(8,128)(2,1)} %rest_1_.3) | copy-start | bytes 786436
  45.3 3.8 %copy-start.7 = (bf16[256,512]{1,0:T(8,128)(2,1)S(1)}, bf16[256,512]{1,0:T(8,128)(2,1)}, u32[]{:S(2)}) copy-start(bf16[256,512]{1,0:T(8,128)(2,1)} %q_ref.1) | copy-start | bytes 786436
  46.9 12.8 %copy-start.1 = (bf16[512,2048]{1,0:T(8,128)(2,1)S(1)}, bf16[512,2048]{1,0:T(8,128)(2,1)}, u32[]{:S(2)}) copy-start(bf16[512,2048]{1,0:T(8,128)(2,1)} %w_ref.2) | copy-start | bytes 6291460
  46.9 12.8 %collective-permute-start.11 = (bf16[528,256]{1,0:T(8,128)(2,1)S(1)}, bf16[528,256]{1,0:T(8,128)(2,1)S(1)}, u32[]{:S(2)}, u32[]{:S(2)}) collective-permute-start(bf16[528,256]{1,0:T(8,128)(2,1)S(1)} %attend_across.1), channel_id=1, source_target_pairs={{0,2},{2,0},{1,3},{3,1},{4,6},{6,4},{5,7},{7,5},{8,10},{10,8},{9,1... | collective-permute-start | bytes 811016 | tf_op jit(solution)/shard_map/ppermute | solution.py:301
  61.5 4.1 %copy-start.9 = (bf16[256,512]{1,0:T(8,128)(2,1)S(1)}, bf16[256,512]{1,0:T(8,128)(2,1)}, u32[]{:S(2)}) copy-start(bf16[256,512]{1,0:T(8,128)(2,1)} %get-tuple-element.10) | copy-start | bytes 786436
  61.5 15.2 %all-to-all-start = ((bf16[4,64,2048]{2,1,0:T(8,128)(2,1)}), bf16[4,64,2048]{2,1,0:T(8,128)(2,1)S(1)}, u32[]{:S(2)}, u32[]{:S(2)}) async-start(bf16[4,64,2048]{2,1,0:T(8,128)(2,1)} %bitcast.5), calls=%async_computation | async-start | bytes 2097152 | tf_op jit(solution)/shard_map/all_to_all | solution.py:310
  65.7 31.6 %copy-start.10 = (f32[256]{0:T(256)S(1)}, f32[256]{0:T(256)}, u32[]{:S(2)}) copy-start(f32[256]{0:T(256)} %param.19) | copy-start | bytes 3076
  65.7 31.8 %copy-start.6 = (bf16[2048,128]{1,0:T(8,128)(2,1)S(1)}, bf16[2048,128]{1,0:T(8,128)(2,1)}, u32[]{:S(2)}) copy-start(bf16[2048,128]{1,0:T(8,128)(2,1)} %w_ref.3) | copy-start | bytes 1572868
  65.7 27.0 %collective-permute-start.12 = (bf16[256,512]{1,0:T(8,128)(2,1)S(1)}, bf16[256,512]{1,0:T(8,128)(2,1)S(1)}, u32[]{:S(2)}, u32[]{:S(2)}) collective-permute-start(bf16[256,512]{1,0:T(8,128)(2,1)S(1)} %copy-done.9), channel_id=1, source_target_pairs={{0,2},{2,0},{1,3},{3,1},{4,6},{6,4},{5,7},{7,5},{8,10},{10,8},{9,1... | collective-permute-start | bytes 786440 | tf_op jit(solution)/shard_map/ppermute | solution.py:301
  77.6 19.8 %all-to-all-start.1 = ((bf16[4,16,2048]{2,1,0:T(8,128)(2,1)}), bf16[4,16,2048]{2,1,0:T(8,128)(2,1)S(1)}, u32[]{:S(2)}, u32[]{:S(2)}) async-start(bf16[4,16,2048]{2,1,0:T(8,128)(2,1)} %bitcast.6), calls=%async_computation.1 | async-start | bytes 524288 | tf_op jit(solution)/shard_map/all_to_all | solution.py:310
  92.8 25.7 %collective-permute-start.13 = (bf16[2,256,512]{2,1,0:T(8,128)(2,1)S(1)}, bf16[2,256,512]{2,1,0:T(8,128)(2,1)S(1)}, u32[]{:S(2)}, u32[]{:S(2)}) collective-permute-start(bf16[2,256,512]{2,1,0:T(8,128)(2,1)S(1)} %pad_maximum_fusion.mine_ref), channel_id=1, source_target_pairs={{0,1},{1,0},{2,3},{3,2},{4,5},{5,4},{6,7},{7,6},{8,9},{9,8},{10,11... | collective-permute-start | bytes 1572872 | tf_op jit(solution)/shard_map/ppermute | solution.py:301
  118.5 18.8 %all-to-all-start.3 = ((bf16[4,256,512]{2,1,0:T(8,128)(2,1)}), bf16[4,256,512]{2,1,0:T(8,128)(2,1)S(1)}, u32[]{:S(2)}, u32[]{:S(2)}) async-start(bf16[4,256,512]{2,1,0:T(8,128)(2,1)} %bitcast.13), calls=%async_computation.3 | async-start | bytes 2097152 | tf_op jit(solution)/shard_map/all_to_all | solution.py:310
  (4 other events, 6.3 us)
